TPU v7x, 32 devices: a whole 2x2x4 slice. The times are simulated.
32 devices in a mesh: blk: 4 (over x, core), grp: 8 (over z, y).
Axes of the slice: x: 2, y: 2, z: 4, core: 2. Of those that a mesh axis runs over, the one named last changes fastest.
Arguments:
- normals: bfloat16 [2048, 131072], P('blk', 'grp'), may hold values from -6 to 6
- mean_square: float32 [2048], P('blk'), may hold values from 0.5 to 2
- freedom_degrees: int32 [2048], P('blk'), may hold values from 3 to 30
- gamma_slab: bfloat16 [1024, 131072], P('blk', 'grp'), may hold values from -0.015625 to 0.015625
- deltas: bfloat16 [131072], P('grp'), may hold values from -0.5 to 0.5
- desk_map: int32 [131072], P('grp'), may hold values from 0 to 127
Outputs:
- desk_pnl: float32 [2048, 128], P(('blk', 'grp'))
All inputs are finite; a program needn't handle non-finite values.
Results may differ from a plain program's by a relative error of at most 0.0038.
Values may be sent and summed in bfloat16 or wider, within the bound.
No kernel may reach another device: no remote copies, remote signals or barrier semaphores. Data moves between devices by JAX's collectives and lax.ppermute only.
A program may use at most 128 MiB of HBM per device.

v0:
```python
import jax
import jax.numpy as jnp
from jax import lax
from jax.sharding import PartitionSpec as P

DESKS = 128
STRIDE = 128


def local(normals, mean_square, freedom_degrees, gamma_slab, deltas, desk_map):
    degrees = freedom_degrees.astype(jnp.float32)
    scaling = jnp.sqrt((degrees - 2.0) / degrees / mean_square)
    shocks = (normals.astype(jnp.float32) * scaling[:, None]).astype(jnp.bfloat16)
    levels = jnp.arange(DESKS, dtype=jnp.int32)
    weights = jnp.where(
        desk_map[:, None] == levels[None, :], deltas[:, None], jnp.zeros((), deltas.dtype)
    )
    linear = jnp.dot(shocks, weights, preferred_element_type=jnp.float32)
    window_shocks = shocks[:, ::STRIDE]
    window_desks = desk_map[::STRIDE]
    partial_value = lax.dot_general(
        shocks,
        lax.all_gather(gamma_slab, "blk", axis=0, tiled=True),
        (((1,), (1,)), ((), ())),
        preferred_element_type=jnp.float32,
    )
    summed = lax.psum_scatter(partial_value, "grp", scatter_dimension=1, tiled=True)
    quadratic = window_shocks.astype(jnp.float32) * summed
    window_hot = (window_desks[:, None] == levels[None, :]).astype(jnp.float32)
    desk_terms = linear + 0.5 * jnp.dot(
        quadratic, window_hot, precision=lax.Precision.HIGHEST, preferred_element_type=jnp.float32
    )
    return lax.psum_scatter(desk_terms, "grp", scatter_dimension=0, tiled=True)


def solution(mesh):
    in_specs = (P("blk", "grp"), P("blk"), P("blk"), P("blk", "grp"), P("grp"), P("grp"))
    out_specs = P(("blk", "grp"), None)
    return jax.shard_map(local, mesh=mesh, in_specs=in_specs, out_specs=out_specs, check_vma=False)
```

profile of v0, /device:TPU:0, one launch (start us, length us, event | category | flops | bytes accessed | tf_op | source)
XLA Modules:
  0.0 378.0 jit_solution(2832350443240793699)
XLA Ops:
  6.5 0.0 all-gather.2.cloned.1.call-start
  6.5 0.7 all-gather.2.cloned.1.call-update
  7.3 0.0 reduce-scatter.3.cloned.1.call-start
  7.3 0.7 fusion.10
  8.0 15.7 %multiply_convert_fusion = bf16[512,16384]{1,0:T(8,128)(2,1)} fusion(bf16[512,16384]{1,0:T(8,128)(2,1)} %param.6, f32[512]{0:T(512)S(1)} %fusion.10), kind=kLoop, calls=%fused_computation | loop fusion | flops 25165824 | bytes 33556480 | tf_op jit(solution)/shard_map/convert_element_type | solution.py:13
  23.7 0.0 copy-start
  23.7 0.0 copy-start.1
  23.7 189.4 %all-gather.2.cloned.1.call-done = bf16[1024,16384]{1,0:T(8,128)(2,1)} async-done(((bf16[256,16384]{1,0:T(8,128)(2,1)}), bf16[1024,16384]{1,0:T(8,128)(2,1)}) %all-gather.2.cloned.1.call-update) | async-done | bytes 33554448 | tf_op jit(solution)/shard_map/all_gather | solution.py:23
  213.2 25.6 %fusion.12 = f32[512,1024]{1,0:T(8,128)} fusion(bf16[512,16384]{1,0:T(8,128)(2,1)} %multiply_convert_fusion, bf16[1024,16384]{1,0:T(8,128)(2,1)} %all-gather.2.cloned.1.call-done), kind=kOutput, calls=%fused_computation.16 | convolution fusion | flops 17179869184 | bytes 52428800 | tf_op jit(solution)/shard_map/dot_general | solution.py:21
  238.8 0.0 reduce-scatter.3.cloned.1.call-update
  238.8 0.0 reduce-scatter.5.cloned.1.call-start
  238.9 9.2 %slice.6 = bf16[512,128]{1,0:T(8,128)(2,1)S(1)} slice(bf16[512,16384]{1,0:T(8,128)(2,1)} %multiply_convert_fusion), slice={[0:512:1], [0:16384:128]} | slice | bytes 262144 | tf_op jit(solution)/shard_map/slice | solution.py:19
  248.1 0.0 copy-done
  248.1 0.2 slice.7
  248.3 0.0 copy-done.1
  248.3 11.2 %fusion.1 = f32[512,128]{1,0:T(8,128)S(1)} fusion(bf16[512,16384]{1,0:T(8,128)(2,1)} %multiply_convert_fusion, s32[16384]{0:T(1024)S(1)} %copy-done, bf16[16384]{0:T(1024)(128)(2,1)S(1)} %copy-done.1), kind=kOutput, calls=%fused_computation.3 | convolution fusion | flops 2151677952 | bytes 17137664 | tf_op jit(solution)/shard_map/dot_general | solution.py:18
  259.6 47.7 %reduce-scatter.3.cloned.1.call-done = f32[512,128]{1,0:T(8,128)} async-done(((f32[512,1024]{1,0:T(8,128)}), f32[512,128]{1,0:T(8,128)}) %reduce-scatter.3.cloned.1.call-update) | async-done | bytes 262160 | tf_op jit(solution)/shard_map/reduce_scatter | solution.py:27
  307.3 2.0 fusion.6
  309.3 0.0 reduce-scatter.5.cloned.1.call-update
  309.3 62.1 %reduce-scatter.5.cloned.1.call-done = f32[64,128]{1,0:T(8,128)} async-done(((f32[512,128]{1,0:T(8,128)}), f32[64,128]{1,0:T(8,128)}) %reduce-scatter.5.cloned.1.call-update) | async-done | bytes 32784 | tf_op jit(solution)/shard_map/reduce_scatter | solution.py:33
Async XLA Ops:
  6.5 206.6 %all-gather.2.cloned.1.call-start = ((), (), s32[]{:S(2)}) async-start(), calls=%async_computation.2 | async-start | bytes 41943040 | tf_op jit(solution)/shard_map/all_gather | solution.py:23
  7.3 300.0 %reduce-scatter.3.cloned.1.call-start = ((), (), s32[]{:S(2)}) async-start(), calls=%async_computation.3 | async-start | bytes 2359296 | tf_op jit(solution)/shard_map/reduce_scatter | solution.py:27
  23.7 224.4 %copy-start = (s32[16384]{0:T(1024)S(1)}, s32[16384]{0:T(1024)}, u32[]{:S(2)}) copy-start(s32[16384]{0:T(1024)} %param.11) | copy-start | bytes 196612
  23.7 224.6 %copy-start.1 = (bf16[16384]{0:T(1024)(128)(2,1)S(1)}, bf16[16384]{0:T(1024)(128)(2,1)}, u32[]{:S(2)}) copy-start(bf16[16384]{0:T(1024)(128)(2,1)} %param.10) | copy-start | bytes 98308
  238.8 132.6 %reduce-scatter.5.cloned.1.call-start = ((), (), s32[]{:S(2)}) async-start(), calls=%async_computation.4 | async-start | bytes 294912 | tf_op jit(solution)/shard_map/reduce_scatter | solution.py:33
Sparse Core Ops, SparseCore 0:
  8.9 204.2 all-gather.1
  239.0 68.2 reduce-scatter.2
  310.6 60.7 reduce-scatter.4
where the time goes:
time: 378 us
  waiting for transfers between devices  300 us (79%)
  matrix products  38.8 us (10%)
  other arithmetic  16.4 us (4%)
  between operations  13.1 us (3%)
  local copies, waits for them, and re-layouts  9.42 us (2%)
    all_gather x1, waiting for transfers between devices, local(): lax.all_gather(gamma_slab, 'blk', axis=0, tiled=True)  189 us
    reduce_scatter x1, waiting for transfers between devices, local(): return lax.psum_scatter(desk_terms, 'grp', scatter_dimension=0, tiled=True)  62.1 us
    reduce_scatter x1, waiting for transfers between devices, local(): lax.psum_scatter(partial_value, 'grp', scatter_dimension=1, tiled=True)  47.7 us
    dot_general x1, matrix products, local(): lax.dot_general(shocks, lax.all_gather(gamma_slab, 'blk', axis=0, tiled=T...  25.6 us
    convert_element_type x1, other arithmetic, local(): (normals.astype(jnp.float32) * scaling[:, None]).astype(jnp.bfloat16)  15.7 us
    dot_general x1, matrix products, local(): linear = jnp.dot(shocks, weights, preferred_element_type=jnp.float32)  11.2 us
    slice x1, local copies, waits for them, and re-layouts, local(): window_shocks = shocks[:, ::STRIDE]  9.2 us
  transfers between devices with their start and end apart: 3, of which 3 were waited for; matrix products, arithmetic and copies ran while one was open for 10% of the time, Pallas kernels for 0%

commit v1 on v0

v1 whole, which is shorter than its diff:
```python
import functools

import jax
import jax.numpy as jnp
from jax import lax
from jax.experimental import pallas as pl
from jax.experimental.pallas import tpu as pltpu
from jax.sharding import PartitionSpec as P

DESKS = 128
STRIDE = 128
CORES = 2
PARTS = (1, 15, 10, 4, 1, 1)
EARLY = 3
VMEM_BYTES = 40 * 2**20

F32 = jnp.float32
BF16 = jnp.bfloat16


def dot_t(left, right):
    return lax.dot_general(left, right, (((1,), (1,)), ((), ())), preferred_element_type=F32)


def call(kernel, **options):
    return pl.pallas_call(
        kernel, compiler_params=pltpu.CompilerParams(vmem_limit_bytes=VMEM_BYTES), **options
    )


def whole(shape):
    return pl.BlockSpec(shape, lambda *_: (0,) * len(shape))


def shock_kernel(blocks, grp_ref, normals_ref, scaling_ref, desks_ref, deltas_ref, shocks_ref, sums_ref):
    step = pl.program_id(0)
    height = normals_ref.shape[0] // blocks
    width = normals_ref.shape[1]
    for index in range(blocks):
        source = pl.ds(pl.multiple_of((index ^ grp_ref[0]) * height, height), height)
        scaled = normals_ref[source, :].astype(F32) * scaling_ref[source, :]
        shocks_ref[index * height : (index + 1) * height, :] = scaled.astype(BF16)
    level = lax.broadcasted_iota(jnp.int32, (DESKS, width), 0)
    factor = lax.broadcasted_iota(jnp.int32, (STRIDE, width), 1) + step * width
    entry = lax.broadcasted_iota(jnp.int32, (STRIDE, width), 0)
    weights = jnp.where(level == desks_ref[...], deltas_ref[...], 0.0).astype(BF16)
    chosen = jnp.where(factor == entry * STRIDE, 1.0, 0.0).astype(BF16)
    sums = dot_t(shocks_ref[...], jnp.concatenate([weights, chosen], 0))

    @pl.when(step == 0)
    def _():
        sums_ref[...] = sums

    @pl.when(step > 0)
    def _():
        sums_ref[...] += sums


def make_shocks(normals, scaling, grp, blocks, desks, deltas):
    rows, cols = normals.shape
    width = min(cols, 2048)
    tile = pl.BlockSpec((rows, width), lambda j, _: (0, j))
    vector = pl.BlockSpec((1, width), lambda j, _: (0, j))
    return call(
        functools.partial(shock_kernel, blocks),
        grid_spec=pltpu.PrefetchScalarGridSpec(
            num_scalar_prefetch=1,
            grid=(cols // width,),
            in_specs=[tile, whole((rows, 1)), vector, vector],
            out_specs=[tile, whole((rows, DESKS + STRIDE))],
        ),
        out_shape=[
            jax.ShapeDtypeStruct((rows, cols), BF16),
            jax.ShapeDtypeStruct((rows, DESKS + STRIDE), F32),
        ],
        name="shocks",
    )(grp[None], normals, scaling[:, None], desks[None, :], deltas.astype(F32)[None, :])


def moved_kernel(has_start, *refs):
    own_ref, sibling_ref, gamma_ref, *start_ref, out_ref = refs
    half = own_ref.shape[0]

    @pl.when(pl.program_id(0) == 0)
    def _():
        out_ref[...] = start_ref[0][...] if has_start else jnp.zeros_like(out_ref)

    gamma = gamma_ref[...]
    out_ref[:half] += dot_t(own_ref[...], gamma)
    out_ref[half:] += dot_t(sibling_ref[...], gamma)


def add_moved(own, sibling, gamma, first, start=None):
    rows, (count, cols) = own.shape[0], gamma.shape
    width = next(size for size in (1024, 512, 256, 128) if cols % size == 0 and first % size == 0)
    shocks = pl.BlockSpec((rows, width), lambda j: (0, j + first // width))
    return call(
        functools.partial(moved_kernel, start is not None),
        grid=(cols // width,),
        in_specs=[shocks, shocks, pl.BlockSpec((count, width), lambda j: (0, j))]
        + [whole((2 * rows, count))] * (start is not None),
        out_specs=whole((2 * rows, count)),
        out_shape=jax.ShapeDtypeStruct((2 * rows, count), F32),
        name="moved",
    )(own, sibling, gamma, *([] if start is None else [start]))


def by_desk(moved, window, hot):
    quadratic = 0.5 * window.astype(F32) * moved
    total = None
    for _ in range(3):
        piece = quadratic.astype(BF16)
        quadratic = quadratic - piece.astype(F32)
        product = jnp.dot(piece, hot, preferred_element_type=F32)
        total = product if total is None else total + product
    return total


def early_kernel(linear_ref, *refs):
    *groups, mine_ref, theirs_ref = refs
    half = mine_ref.shape[0]
    total = None
    for index in range(0, len(groups), 3):
        moved_ref, window_ref, hot_ref = groups[index : index + 3]
        terms = by_desk(moved_ref[...], window_ref[...], hot_ref[...])
        total = terms if total is None else total + terms
    mine_ref[...] = total[:half] + linear_ref[...]
    theirs_ref[...] = total[half:]


def early_terms(linear, *groups):
    shape = jax.ShapeDtypeStruct(linear.shape, F32)
    return call(early_kernel, out_shape=[shape, shape], name="early")(linear, *groups)


def late_kernel(own_ref, sibling_ref, gamma_ref, start_ref, window_ref, hot_ref, mine_ref, theirs_ref):
    gamma, hot, half = gamma_ref[...], hot_ref[...], own_ref.shape[0]
    moved = start_ref[half:] + dot_t(sibling_ref[...], gamma)
    theirs_ref[...] = by_desk(moved, window_ref[half:], hot).astype(BF16)
    moved = start_ref[:half] + dot_t(own_ref[...], gamma)
    mine_ref[...] = by_desk(moved, window_ref[:half], hot)


def late_terms(own, sibling, gamma, first, start, window, hot):
    rows, (count, cols) = own.shape[0], gamma.shape
    shocks = pl.BlockSpec((rows, cols), lambda _: (0, first // cols))
    return call(
        late_kernel,
        grid=(1,),
        in_specs=[shocks, shocks]
        + [whole(shape) for shape in (gamma.shape, start.shape, window.shape, hot.shape)],
        out_specs=[whole((rows, DESKS)), whole((rows, DESKS))],
        out_shape=[jax.ShapeDtypeStruct((rows, DESKS), F32), jax.ShapeDtypeStruct((rows, DESKS), BF16)],
        name="late",
    )(own, sibling, gamma, start, window, hot)


def local(n_blk, n_grp, normals, mean_square, freedom_degrees, gamma_slab, deltas, desk_map):
    together = lax.optimization_barrier
    blk, grp = lax.axis_index("blk"), lax.axis_index("grp")
    scenarios, columns = normals.shape
    rows = gamma_slab.shape[0]
    chips = n_blk // CORES
    block = scenarios // n_grp
    per_grp = columns // STRIDE
    sibling = [(i, i ^ 1) for i in range(n_blk)]

    def to_sibling(array):
        return lax.ppermute(array, "blk", sibling)

    def from_chips(array):
        parts = [
            lax.ppermute(array, "blk", [(i, (i + CORES * step) % n_blk) for i in range(n_blk)])
            for step in range(1, chips)
        ]
        return parts[0] if len(parts) == 1 else jnp.concatenate(parts, 0)

    def window_of(array, axis):
        own = lax.dynamic_slice_in_dim(array, blk * rows, rows, axis)
        others = [
            lax.dynamic_slice_in_dim(array, lax.rem(blk + n_blk - CORES * step, n_blk) * rows, rows, axis)
            for step in range(1, chips)
        ]
        return own, others[0] if len(others) == 1 else jnp.concatenate(others, axis)

    unit = columns // sum(PARTS)
    starts = [sum(PARTS[:i]) * unit for i in range(len(PARTS) + 1)]
    last = len(PARTS) - 1

    def chunk(index):
        return gamma_slab[:, starts[index] : starts[index + 1]]

    first = chunk(0)
    first, gamma_slab = together((first, gamma_slab))
    arrived = [from_chips(first)] + [from_chips(chunk(index)) for index in range(1, len(PARTS))]
    normals, arrived[0] = together((normals, arrived[0]))

    degrees = freedom_degrees.astype(F32)
    scaling = jnp.sqrt((degrees - 2.0) / degrees / mean_square)
    own, sums = make_shocks(normals, scaling, grp, n_grp, desk_map, deltas)
    other = to_sibling(own)
    linear = sums[:, :DESKS]

    order = jnp.arange(n_grp, dtype=jnp.int32) ^ grp
    plain = jnp.take(sums[:, DESKS : DESKS + per_grp].reshape(n_grp, block, per_grp), order, axis=0)
    window_desks = jnp.broadcast_to(desk_map[::STRIDE].astype(F32), (16, per_grp))
    packed = jnp.concatenate([plain.reshape(scenarios, per_grp), window_desks], 0).astype(BF16)
    packed = lax.all_to_all(jnp.broadcast_to(packed, (n_grp,) + packed.shape), "grp", 0, 0, tiled=True)
    desks = packed[:, scenarios].reshape(-1)
    hot = (desks[:, None] == jnp.arange(DESKS).astype(BF16)[None, :]).astype(BF16)
    own_hot, other_hot = window_of(hot, 0)
    window = packed[:, :scenarios].reshape(n_grp, n_grp, block, per_grp)
    window = jnp.take(window, order, axis=1).transpose(1, 2, 0, 3).reshape(scenarios, n_grp * per_grp)
    window = jnp.concatenate([window, to_sibling(window)], 0)
    own_window, other_window = window_of(window, 1)

    own_moved = add_moved(own, other, gamma_slab, 0)
    moved = None
    for index in range(EARLY):
        moved = add_moved(own, other, arrived[index], starts[index], moved)
    mine, theirs = early_terms(linear, own_moved, own_window, own_hot, moved, other_window, other_hot)
    mine = jnp.take((mine + to_sibling(theirs)).reshape(n_grp, block, DESKS), order, axis=0)
    early = lax.all_to_all(mine, "grp", 0, 0, tiled=True).sum(0)

    moved = None
    for index in range(EARLY, last):
        moved = add_moved(own, other, arrived[index], starts[index], moved)
    final, early = together((arrived[last], early))
    mine, theirs = late_terms(own, other, final, starts[last], moved, other_window, other_hot)
    late = mine + to_sibling(theirs).astype(F32)
    late = late.reshape(n_grp, block, DESKS)
    bit = 1
    while bit < n_grp:
        halves = late.reshape(late.shape[0] // 2, 2, block, DESKS)
        sent = lax.ppermute(halves[:, 1].astype(BF16), "grp", [(i, i ^ bit) for i in range(n_grp)])
        late = halves[:, 0] + sent.astype(F32)
        bit *= 2
    return early + late[0]


def solution(mesh):
    in_specs = (P("blk", "grp"), P("blk"), P("blk"), P("blk", "grp"), P("grp"), P("grp"))
    out_specs = P(("blk", "grp"), None)
    body = functools.partial(local, mesh.shape["blk"], mesh.shape["grp"])
    return jax.shard_map(body, mesh=mesh, in_specs=in_specs, out_specs=out_specs, check_vma=False)
```

time: 378 us -> 229 us (0.61)
  waiting for transfers between devices: 300 us -> 95.2 us
  Pallas kernels: 0 us -> 68.8 us
  matrix products: 38.8 us -> 0 us
  starting transfers between devices: 0.08 us -> 26.6 us
  local copies, waits for them, and re-layouts: 9.42 us -> 31.8 us
  between operations: 13.1 us -> 0.32 us
  other arithmetic: 16.4 us -> 4.72 us
    all_gather x1 -> x0, waiting for transfers between devices: 189 us -> none  [local(): lax.all_gather(gamma_slab, 'blk', axis=0, tiled=True)]
    reduce_scatter x2 -> x0, waiting for transfers between devices: 110 us -> none  [the longest x1 62.1 us: local(): return lax.psum_scatter(desk_terms, 'grp', scatter_dimension=0, tiled=True)]
    ppermute x0 -> x13, waiting for transfers between devices: none -> 72.4 us  [the longest x6 63.1 us: from_chips(): lax.ppermute(array, 'blk', [(i, (i + CORES * step) % n_blk) for i in rang...]
    pallas_call x0 -> x9, Pallas kernels: none -> 68.8 us  [the longest x6 48.3 us: add_moved(): call(functools.partial(moved_kernel, start is not None), grid=(cols // wi...]
    dot_general x3 -> x0, matrix products: 38.8 us -> none  [the longest x1 25.6 us: local(): lax.dot_general(shocks, lax.all_gather(gamma_slab, 'blk', axis=0, tiled=T...]
    all_to_all x0 -> x2, waiting for transfers between devices: none -> 22.8 us  [the longest x1 22.8 us: local(): lax.all_to_all(jnp.broadcast_to(packed, (n_grp,) + packed.shape), 'grp',...]
    convert_element_type x1 -> x2, other arithmetic: 15.7 us -> 0.21 us  [the longest x1 0.21 us: local(): (desks[:, None] == jnp.arange(DESKS).astype(BF16)[None, :]).astype(BF16)]
    ppermute x0 -> x13, starting transfers between devices: none -> 14.7 us  [the longest x6 7.9 us: from_chips(): lax.ppermute(array, 'blk', [(i, (i + CORES * step) % n_blk) for i in rang...]
  transfers between devices with their start and end apart: 3 -> 15, of which waited for: 3 -> 12; matrix products, arithmetic and copies ran while one was open for 10% -> 13% of each run, Pallas kernels for 0% -> 22%
where the time goes in v1:
time: 229 us; the launch traced here: 227 us
  waiting for transfers between devices  95.2 us (42%)
  Pallas kernels  68.8 us (30%)
  local copies, waits for them, and re-layouts  31.8 us (14%)
  starting transfers between devices  26.6 us (12%)
  other arithmetic  4.72 us (2%)
    ppermute x6, waiting for transfers between devices, from_chips(): lax.ppermute(array, 'blk', [(i, (i + CORES * step) % n_blk) for i in rang...  63.1 us
    pallas_call x6, Pallas kernels, add_moved(): call(functools.partial(moved_kernel, start is not None), grid=(cols // wi...  48.3 us
    all_to_all x1, waiting for transfers between devices, local(): lax.all_to_all(jnp.broadcast_to(packed, (n_grp,) + packed.shape), 'grp',...  22.8 us
    pallas_call x1, Pallas kernels, make_shocks(): call(functools.partial(shock_kernel, blocks), grid_spec=pltpu.PrefetchSca...  17 us
    slice x5, local copies, waits for them, and re-layouts, chunk(): return gamma_slab[:, starts[index]:starts[index + 1]]  12.3 us
    unnamed x13, local copies, waits for them, and re-layouts  7.9 us
    ppermute x6, starting transfers between devices, from_chips(): lax.ppermute(array, 'blk', [(i, (i + CORES * step) % n_blk) for i in rang...  7.9 us
    ppermute x3, starting transfers between devices, local(): lax.ppermute(halves[:, 1].astype(BF16), 'grp', [(i, i ^ bit) for i in ran...  6.62 us
  transfers between devices with their start and end apart: 15, of which 12 were waited for; matrix products, arithmetic and copies ran while one was open for 13% of the time, Pallas kernels for 22%

profile of v1, /device:TPU:0, one launch (start us, length us, event | category | flops | bytes accessed | tf_op | source)
XLA Modules:
  0.0 227.4 jit_solution(10876537356564470735)
XLA Ops:
  0.0 1.0 slice.54
  1.0 3.0 %collective-permute-start.1 = (bf16[256,512]{1,0:T(8,128)(2,1)S(1)}, bf16[256,512]{1,0:T(8,128)(2,1)S(1)}, u32[]{:S(2)}, u32[]{:S(2)}) collective-permute-start(bf16[256,512]{1,0:T(8,128)(2,1)S(1)} %slice.54), channel_id=1, source_target_pairs={{0,16},{8,24},{16,0},{24,8},{1,17},{9,25},{17,1},{25,9},{2,18},{10... | collective-permute-start | bytes 786440 | tf_op jit(solution)/shard_map/ppermute | solution.py:173
  4.0 0.7 fusion.9
  4.7 0.2 copy.14.scaling_ref
  4.8 0.8 broadcast_in_dim.52
  5.6 4.7 %collective-permute-done.1.refs_2_ = bf16[256,512]{1,0:T(8,128)(2,1)S(1)} collective-permute-done((bf16[256,512]{1,0:T(8,128)(2,1)S(1)}, bf16[256,512]{1,0:T(8,128)(2,1)S(1)}, u32[]{:S(2)}, u32[]{:S(2)}) %collective-permute-start.1) | collective-permute-done | bytes 262176 | tf_op jit(solution)/shard_map/ppermute | solution.py:173
  10.3 0.8 copy-done.3
  11.1 17.0 %shocks.1 = (bf16[512,16384]{1,0:T(8,128)(2,1)}, f32[512,256]{1,0:T(8,128)S(1)}) custom-call(s32[1]{0:T(128)} %bitcast.grp_ref, bf16[512,16384]{1,0:T(8,128)(2,1)} %normals_ref, f32[512,1]{1,0:T(8,128)S(1)} %copy.14.scaling_ref, s32[1,16384]{1,0:T(1,128)S(1)} %bitcast.57, f32[1,16384]{1,0:T(1,128)S(1)} %bitcast.56), custom_call_target="tpu_custom_call" | custom-call | tf_op jit(solution)/shard_map/shocks/pallas_call | solution.py:64
  28.1 4.5 %slice.62 = bf16[256,7680]{1,0:T(8,128)(2,1)} slice(bf16[256,16384]{1,0:T(8,128)(2,1)} %refs_2_), slice={[0:256], [512:8192]} | slice | bytes 7864320 | tf_op jit(solution)/shard_map/slice | solution.py:191
  32.7 1.7 collective-permute-start.5
  34.4 1.0 slice.58
  35.5 0.6 gather_fusion.1
  36.1 0.1 select_convert_fusion
  36.2 1.1 broadcast_in_dim.47
  37.4 5.8 %all-to-all-start = ((bf16[8,528,128]{2,1,0:T(8,128)(2,1)}), bf16[8,528,128]{2,1,0:T(8,128)(2,1)}, u32[]{:S(2)}, u32[]{:S(2)}) async-start(bf16[8,528,128]{2,1,0:T(8,128)(2,1)} %broadcast_in_dim.47), calls=%async_computation | async-start | bytes 2162688 | tf_op jit(solution)/shard_map/all_to_all | solution.py:208
  43.2 3.4 %slice.61 = bf16[256,5120]{1,0:T(8,128)(2,1)} slice(bf16[256,16384]{1,0:T(8,128)(2,1)} %refs_2_), slice={[0:256], [8192:13312]} | slice | bytes 5242880 | tf_op jit(solution)/shard_map/slice | solution.py:191
  46.6 0.5 collective-permute-start.4
  47.2 22.8 %all-to-all-done = bf16[8,528,128]{2,1,0:T(8,128)(2,1)} async-done(((bf16[8,528,128]{2,1,0:T(8,128)(2,1)}), bf16[8,528,128]{2,1,0:T(8,128)(2,1)}, u32[]{:S(2)}, u32[]{:S(2)}) %all-to-all-start) | async-done | bytes 1081376 | tf_op jit(solution)/shard_map/all_to_all | solution.py:208
  70.0 2.3 %slice.77 = bf16[8,512,128]{2,1,0:T(8,128)(2,1)} slice(bf16[8,528,128]{2,1,0:T(8,128)(2,1)} %all-to-all-done), slice={[0:8], [0:512], [0:128]} | slice | bytes 2097152 | tf_op jit(solution)/shard_map/slice | solution.py:212
  72.3 2.9 %gather_fusion = bf16[8,8,64,128]{3,2,1,0:T(8,128)(2,1)} fusion(bf16[8,8,64,128]{3,2,1,0:T(8,128)(2,1)} %bitcast.60, s32[1024]{0:T(1024)S(1)} %pad_clamp_fusion), kind=kCustom, calls=%fused_computation.2 | custom fusion | bytes 2097184 | tf_op jit(solution)/shard_map/jit(_take)/gather | solution.py:213
  75.2 1.4 select_bitcast_fusion
  76.6 0.7 copy.15
  77.3 1.0 copy-done.4
  78.2 1.3 copy.35
  79.5 2.3 %slice.64 = bf16[256,2048]{1,0:T(8,128)(2,1)} slice(bf16[256,16384]{1,0:T(8,128)(2,1)} %refs_2_), slice={[0:256], [13312:15360]} | slice | bytes 2097152 | tf_op jit(solution)/shard_map/slice | solution.py:191
  81.8 0.5 collective-permute-start.8
  82.4 0.7 slice.78
  83.1 0.2 compare_convert_fusion
  83.3 1.5 constant_dynamic-update-slice_fusion.1
  84.8 1.3 constant_dynamic-update-slice_fusion
  86.1 0.1 constant_dynamic-slice_fusion.1
  86.3 0.0 collective-permute-done.2.refs_1_.sibling_ref
  86.3 0.0 copy-start
  86.3 3.4 %copy-done = bf16[256,16384]{1,0:T(8,128)(2,1)S(1)} copy-done((bf16[256,16384]{1,0:T(8,128)(2,1)S(1)}, bf16[256,16384]{1,0:T(8,128)(2,1)}, u32[]{:S(2)}) %copy-start) | copy-done | bytes 8388632
  89.7 20.2 %moved.6.refs_0_ = f32[1024,256]{1,0:T(8,128)S(1)} custom-call(bf16[512,16384]{1,0:T(8,128)(2,1)} %get-tuple-element.22.refs_0_.own_ref, bf16[512,16384]{1,0:T(8,128)(2,1)} %collective-permute-done.2.refs_1_.sibling_ref, bf16[256,16384]{1,0:T(8,128)(2,1)S(1)} %copy-done), custom_call_target="tpu_custom_call" | custom-call | tf_op jit(solution)/shard_map/moved/pallas_call | solution.py:97
  109.9 1.7 moved.7.refs_3_
  111.5 9.2 %collective-permute-done.5.refs_2_ = bf16[256,7680]{1,0:T(8,128)(2,1)} collective-permute-done((bf16[256,7680]{1,0:T(8,128)(2,1)}, bf16[256,7680]{1,0:T(8,128)(2,1)}, u32[]{:S(2)}, u32[]{:S(2)}) %collective-permute-start.5) | collective-permute-done | bytes 3932192 | tf_op jit(solution)/shard_map/ppermute | solution.py:173
  120.8 14.5 %moved.8.refs_3_ = f32[1024,256]{1,0:T(8,128)S(1)} custom-call(bf16[512,16384]{1,0:T(8,128)(2,1)} %get-tuple-element.22.refs_0_.own_ref, bf16[512,16384]{1,0:T(8,128)(2,1)} %collective-permute-done.2.refs_1_.sibling_ref, bf16[256,7680]{1,0:T(8,128)(2,1)} %collective-permute-done.5.refs_2_, f32[1024,256]{1,0:T(8,128)S(1)} %moved.7.refs_3_), custom_call_target="tpu_custom_call" | custom-call | tf_op jit(solution)/shard_map/moved/pallas_call | solution.py:97
  135.2 41.6 %collective-permute-done.4.refs_2_ = bf16[256,5120]{1,0:T(8,128)(2,1)S(1)} collective-permute-done((bf16[256,5120]{1,0:T(8,128)(2,1)}, bf16[256,5120]{1,0:T(8,128)(2,1)S(1)}, u32[]{:S(2)}, u32[]{:S(2)}) %collective-permute-start.4) | collective-permute-done | bytes 2621472 | tf_op jit(solution)/shard_map/ppermute | solution.py:173
  176.8 7.1 %moved.9.refs_3_ = f32[1024,256]{1,0:T(8,128)S(1)} custom-call(bf16[512,16384]{1,0:T(8,128)(2,1)} %get-tuple-element.22.refs_0_.own_ref, bf16[512,16384]{1,0:T(8,128)(2,1)} %collective-permute-done.2.refs_1_.sibling_ref, bf16[256,5120]{1,0:T(8,128)(2,1)S(1)} %collective-permute-done.4.refs_2_, f32[1024,256]{1,0:T(8,128)S(1)} %moved.8.refs_3_), custom_call_target="tpu_custom_call" | custom-call | tf_op jit(solution)/shard_map/moved/pallas_call | solution.py:97
  183.9 1.1 early.1
  185.0 0.1 collective-permute-start.6
  185.1 1.5 collective-permute-done.6
  186.7 0.6 gather_fusion.2
  187.2 0.8 broadcast_select_fusion
  188.0 6.1 %all-to-all-start.1 = ((f32[8,64,128]{2,1,0:T(8,128)}), f32[8,64,128]{2,1,0:T(8,128)S(1)}, u32[]{:S(2)}, u32[]{:S(2)}) async-start(f32[8,64,128]{2,1,0:T(8,128)} %broadcast_select_fusion), calls=%async_computation.1 | async-start | bytes 524288 | tf_op jit(solution)/shard_map/all_to_all | solution.py:223
  194.1 1.1 fusion.11
  195.2 1.6 collective-permute-start.7
  196.7 0.5 collective-permute-start
  197.3 2.1 collective-permute-done.8.refs_2_
  199.4 3.3 %moved.10.refs_3_ = f32[1024,256]{1,0:T(8,128)S(1)} custom-call(bf16[512,16384]{1,0:T(8,128)(2,1)} %get-tuple-element.22.refs_0_.own_ref, bf16[512,16384]{1,0:T(8,128)(2,1)} %collective-permute-done.2.refs_1_.sibling_ref, bf16[256,2048]{1,0:T(8,128)(2,1)} %collective-permute-done.8.refs_2_), custom_call_target="tpu_custom_call" | custom-call | tf_op jit(solution)/shard_map/moved/pallas_call | solution.py:97
  202.7 2.2 collective-permute-done.7.refs_2_
  204.9 1.7 moved.11.start_ref
  206.6 3.3 %collective-permute-done.gamma_ref = bf16[256,512]{1,0:T(8,128)(2,1)S(1)} collective-permute-done((bf16[256,512]{1,0:T(8,128)(2,1)S(1)}, bf16[256,512]{1,0:T(8,128)(2,1)S(1)}, u32[]{:S(2)}, u32[]{:S(2)}) %collective-permute-start) | collective-permute-done | bytes 262176 | tf_op jit(solution)/shard_map/ppermute | solution.py:173
  209.9 2.3 %late.1 = (f32[512,128]{1,0:T(8,128)S(1)}, bf16[512,128]{1,0:T(8,128)(2,1)S(1)}) custom-call(bf16[512,16384]{1,0:T(8,128)(2,1)} %get-tuple-element.22.refs_0_.own_ref, bf16[512,16384]{1,0:T(8,128)(2,1)} %collective-permute-done.2.refs_1_.sibling_ref, bf16[256,512]{1,0:T(8,128)(2,1)S(1)} %collective-permute-done.gamma_ref, f32[1024,256]{1,0:T(8,128)S(1)} %moved.11.start_ref, ...), custom_call_target="tpu_custom_call" | custom-call | tf_op jit(solution)/shard_map/late/pallas_call | solution.py:147
  212.3 0.1 collective-permute-start.9
  212.4 1.3 collective-permute-done.9
  213.7 1.8 collective-permute-start.10
  215.6 2.5 %collective-permute-done.10 = bf16[4,64,128]{2,1,0:T(8,128)(2,1)S(1)} collective-permute-done((bf16[4,64,128]{2,1,0:T(8,128)(2,1)S(1)}, bf16[4,64,128]{2,1,0:T(8,128)(2,1)S(1)}, u32[]{:S(2)}, u32[]{:S(2)}) %collective-permute-start.10) | collective-permute-done | bytes 65568 | tf_op jit(solution)/shard_map/ppermute | solution.py:235
  218.1 1.9 collective-permute-start.11
  220.0 2.1 collective-permute-done.11
  222.1 2.9 %collective-permute-start.12 = (bf16[1,64,128]{2,1,0:T(8,128)(2,1)S(1)}, bf16[1,64,128]{2,1,0:T(8,128)(2,1)S(1)}, u32[]{:S(2)}, u32[]{:S(2)}) collective-permute-start(bf16[1,64,128]{2,1,0:T(8,128)(2,1)S(1)} %fusion.8), channel_id=1, source_target_pairs={{0,4},{1,5},{2,6},{3,7},{4,0},{5,1},{6,2},{7,3},{8,12},{9,13},{10,... | collective-permute-start | bytes 49160 | tf_op jit(solution)/shard_map/ppermute | solution.py:235
  225.0 1.8 collective-permute-done.12
  226.8 0.6 fusion.7
  (31 shorter events, 0.3 us)
Async XLA Ops:
  1.0 9.3 %collective-permute-start.1 = (bf16[256,512]{1,0:T(8,128)(2,1)S(1)}, bf16[256,512]{1,0:T(8,128)(2,1)S(1)}, u32[]{:S(2)}, u32[]{:S(2)}) collective-permute-start(bf16[256,512]{1,0:T(8,128)(2,1)S(1)} %slice.54), channel_id=1, source_target_pairs={{0,16},{8,24},{16,0},{24,8},{1,17},{9,25},{17,1},{25,9},{2,18},{10... | collective-permute-start | bytes 786440 | tf_op jit(solution)/shard_map/ppermute | solution.py:173
  10.3 0.8 copy-start.3
  28.1 7.4 %copy-start.1 = (f32[512,256]{1,0:T(8,128)}, f32[512,256]{1,0:T(8,128)S(1)}, u32[]{:S(2)}) copy-start(f32[512,256]{1,0:T(8,128)S(1)} %get-tuple-element.21) | copy-start | bytes 1572868
  28.1 58.2 %collective-permute-start.2 = (bf16[512,16384]{1,0:T(8,128)(2,1)}, bf16[512,16384]{1,0:T(8,128)(2,1)}, u32[]{:S(2)}, u32[]{:S(2)}) collective-permute-start(bf16[512,16384]{1,0:T(8,128)(2,1)} %get-tuple-element.22.refs_0_.own_ref), channel_id=1, source_target_pairs={{0,8},{8,0},{16,24},{24,16},{1,9},{9,1},{17,25},{25,17},{2,10},{10... | collective-permute-start | bytes 50331656 | tf_op jit(solution)/shard_map/ppermute | solution.py:169
  32.7 88.1 %collective-permute-start.5 = (bf16[256,7680]{1,0:T(8,128)(2,1)}, bf16[256,7680]{1,0:T(8,128)(2,1)}, u32[]{:S(2)}, u32[]{:S(2)}) collective-permute-start(bf16[256,7680]{1,0:T(8,128)(2,1)} %slice.62), channel_id=1, source_target_pairs={{0,16},{8,24},{16,0},{24,8},{1,17},{9,25},{17,1},{25,9},{2,18},{10... | collective-permute-start | bytes 11796488 | tf_op jit(solution)/shard_map/ppermute | solution.py:173
  37.4 32.6 %all-to-all-start = ((bf16[8,528,128]{2,1,0:T(8,128)(2,1)}), bf16[8,528,128]{2,1,0:T(8,128)(2,1)}, u32[]{:S(2)}, u32[]{:S(2)}) async-start(bf16[8,528,128]{2,1,0:T(8,128)(2,1)} %broadcast_in_dim.47), calls=%async_computation | async-start | bytes 2162688 | tf_op jit(solution)/shard_map/all_to_all | solution.py:208
  46.6 130.2 %collective-permute-start.4 = (bf16[256,5120]{1,0:T(8,128)(2,1)}, bf16[256,5120]{1,0:T(8,128)(2,1)S(1)}, u32[]{:S(2)}, u32[]{:S(2)}) collective-permute-start(bf16[256,5120]{1,0:T(8,128)(2,1)} %slice.61), channel_id=1, source_target_pairs={{0,16},{8,24},{16,0},{24,8},{1,17},{9,25},{17,1},{25,9},{2,18},{10... | collective-permute-start | bytes 7864328 | tf_op jit(solution)/shard_map/ppermute | solution.py:173
  77.3 1.0 copy-start.4
  77.3 5.1 %copy-start.2 = (f32[512,256]{1,0:T(8,128)S(1)}, f32[512,256]{1,0:T(8,128)}, u32[]{:S(2)}) copy-start(f32[512,256]{1,0:T(8,128)} %copy-done.1) | copy-start | bytes 1572868
  79.5 5.3 %collective-permute-start.3 = (bf16[512,1024]{1,0:T(8,128)(2,1)}, bf16[512,1024]{1,0:T(8,128)(2,1)}, u32[]{:S(2)}, u32[]{:S(2)}) collective-permute-start(bf16[512,1024]{1,0:T(8,128)(2,1)} %bitcast.54), channel_id=1, source_target_pairs={{0,8},{8,0},{16,24},{24,16},{1,9},{9,1},{17,25},{25,17},{2,10},{10... | collective-permute-start | bytes 3145736 | tf_op jit(solution)/shard_map/ppermute | solution.py:169
  81.8 117.6 %collective-permute-start.8 = (bf16[256,2048]{1,0:T(8,128)(2,1)}, bf16[256,2048]{1,0:T(8,128)(2,1)}, u32[]{:S(2)}, u32[]{:S(2)}) collective-permute-start(bf16[256,2048]{1,0:T(8,128)(2,1)} %slice.64), channel_id=1, source_target_pairs={{0,16},{8,24},{16,0},{24,8},{1,17},{9,25},{17,1},{25,9},{2,18},{10... | collective-permute-start | bytes 3145736 | tf_op jit(solution)/shard_map/ppermute | solution.py:173
  86.3 3.4 %copy-start = (bf16[256,16384]{1,0:T(8,128)(2,1)S(1)}, bf16[256,16384]{1,0:T(8,128)(2,1)}, u32[]{:S(2)}) copy-start(bf16[256,16384]{1,0:T(8,128)(2,1)} %refs_2_) | copy-start | bytes 25165828
  185.0 1.6 collective-permute-start.6
  188.0 18.6 %all-to-all-start.1 = ((f32[8,64,128]{2,1,0:T(8,128)}), f32[8,64,128]{2,1,0:T(8,128)S(1)}, u32[]{:S(2)}, u32[]{:S(2)}) async-start(f32[8,64,128]{2,1,0:T(8,128)} %broadcast_select_fusion), calls=%async_computation.1 | async-start | bytes 524288 | tf_op jit(solution)/shard_map/all_to_all | solution.py:223
  195.2 9.7 %collective-permute-start.7 = (bf16[256,512]{1,0:T(8,128)(2,1)S(1)}, bf16[256,512]{1,0:T(8,128)(2,1)S(1)}, u32[]{:S(2)}, u32[]{:S(2)}) collective-permute-start(bf16[256,512]{1,0:T(8,128)(2,1)S(1)} %get-tuple-element.30), channel_id=1, source_target_pairs={{0,16},{8,24},{16,0},{24,8},{1,17},{9,25},{17,1},{25,9},{2,18},{10... | collective-permute-start | bytes 786440 | tf_op jit(solution)/shard_map/ppermute | solution.py:173
  196.7 13.2 %collective-permute-start = (bf16[256,512]{1,0:T(8,128)(2,1)S(1)}, bf16[256,512]{1,0:T(8,128)(2,1)S(1)}, u32[]{:S(2)}, u32[]{:S(2)}) collective-permute-start(bf16[256,512]{1,0:T(8,128)(2,1)S(1)} %get-tuple-element.31), channel_id=1, source_target_pairs={{0,16},{8,24},{16,0},{24,8},{1,17},{9,25},{17,1},{25,9},{2,18},{10... | collective-permute-start | bytes 786440 | tf_op jit(solution)/shard_map/ppermute | solution.py:173
  212.3 1.4 collective-permute-start.9
  213.7 4.3 %collective-permute-start.10 = (bf16[4,64,128]{2,1,0:T(8,128)(2,1)S(1)}, bf16[4,64,128]{2,1,0:T(8,128)(2,1)S(1)}, u32[]{:S(2)}, u32[]{:S(2)}) collective-permute-start(bf16[4,64,128]{2,1,0:T(8,128)(2,1)S(1)} %fusion.1), channel_id=1, source_target_pairs={{0,1},{1,0},{2,3},{3,2},{4,5},{5,4},{6,7},{7,6},{8,9},{9,8},{10,11... | collective-permute-start | bytes 196616 | tf_op jit(solution)/shard_map/ppermute | solution.py:235
  218.1 4.0 %collective-permute-start.11 = (bf16[2,64,128]{2,1,0:T(8,128)(2,1)S(1)}, bf16[2,64,128]{2,1,0:T(8,128)(2,1)S(1)}, u32[]{:S(2)}, u32[]{:S(2)}) collective-permute-start(bf16[2,64,128]{2,1,0:T(8,128)(2,1)S(1)} %fusion.4), channel_id=1, source_target_pairs={{0,2},{1,3},{2,0},{3,1},{4,6},{5,7},{6,4},{7,5},{8,10},{9,11},{10,... | collective-permute-start | bytes 98312 | tf_op jit(solution)/shard_map/ppermute | solution.py:235
  222.1 4.7 %collective-permute-start.12 = (bf16[1,64,128]{2,1,0:T(8,128)(2,1)S(1)}, bf16[1,64,128]{2,1,0:T(8,128)(2,1)S(1)}, u32[]{:S(2)}, u32[]{:S(2)}) collective-permute-start(bf16[1,64,128]{2,1,0:T(8,128)(2,1)S(1)} %fusion.8), channel_id=1, source_target_pairs={{0,4},{1,5},{2,6},{3,7},{4,0},{5,1},{6,2},{7,3},{8,12},{9,13},{10,... | collective-permute-start | bytes 49160 | tf_op jit(solution)/shard_map/ppermute | solution.py:235

commit v2 on v1

v2 whole, which is shorter than its diff:
```python
import functools

import jax
import jax.numpy as jnp
from jax import lax
from jax.experimental import pallas as pl
from jax.experimental.pallas import tpu as pltpu
from jax.sharding import PartitionSpec as P

DESKS = 128
STRIDE = 128
CORES = 2
PARTS = (5, 15, 9, 2, 1)
EARLY = 2
VMEM_BYTES = 40 * 2**20

F32 = jnp.float32
BF16 = jnp.bfloat16


def dot_t(left, right):
    return lax.dot_general(left, right, (((1,), (1,)), ((), ())), preferred_element_type=F32)


def call(kernel, **options):
    return pl.pallas_call(
        kernel, compiler_params=pltpu.CompilerParams(vmem_limit_bytes=VMEM_BYTES), **options
    )


def whole(shape):
    return pl.BlockSpec(shape, lambda *_: (0,) * len(shape))


def scaled(normals_ref, scaling_ref):
    return (normals_ref[...].astype(F32) * scaling_ref[...]).astype(BF16)


def own_kernel(own_ref, sibling_ref, own_scaling_ref, sibling_scaling_ref, gamma_ref, desks_ref, deltas_ref, moved_ref, sums_ref):
    step = pl.program_id(0)
    half, width = own_ref.shape

    @pl.when(step == 0)
    def _():
        moved_ref[...] = jnp.zeros_like(moved_ref)
        sums_ref[...] = jnp.zeros_like(sums_ref)

    level = lax.broadcasted_iota(jnp.int32, (DESKS, width), 0)
    factor = lax.broadcasted_iota(jnp.int32, (STRIDE, width), 1) + step * width
    entry = lax.broadcasted_iota(jnp.int32, (STRIDE, width), 0)
    weights = jnp.where(level == desks_ref[...], deltas_ref[...], 0.0).astype(BF16)
    chosen = jnp.where(factor == entry * STRIDE, 1.0, 0.0).astype(BF16)
    own, gamma = scaled(own_ref, own_scaling_ref), gamma_ref[...]
    sums_ref[...] += dot_t(own, jnp.concatenate([weights, chosen], 0))
    moved_ref[:half] += dot_t(own, gamma)
    moved_ref[half:] += dot_t(scaled(sibling_ref, sibling_scaling_ref), gamma)


def own_moved(own, sibling, own_scaling, sibling_scaling, gamma, desks, deltas):
    rows, (count, cols) = own.shape[0], gamma.shape
    width = min(cols, 1024)
    normals = pl.BlockSpec((rows, width), lambda j: (0, j))
    vector = pl.BlockSpec((1, width), lambda j: (0, j))
    return call(
        own_kernel,
        grid=(cols // width,),
        in_specs=[normals, normals, whole((rows, 1)), whole((rows, 1))]
        + [pl.BlockSpec((count, width), lambda j: (0, j)), vector, vector],
        out_specs=[whole((2 * rows, count)), whole((rows, DESKS + STRIDE))],
        out_shape=[
            jax.ShapeDtypeStruct((2 * rows, count), F32),
            jax.ShapeDtypeStruct((rows, DESKS + STRIDE), F32),
        ],
        name="own_rows",
    )(own, sibling, own_scaling, sibling_scaling, gamma, desks[None, :], deltas.astype(F32)[None, :])


def moved_kernel(has_start, *refs):
    own_ref, sibling_ref, own_scaling_ref, sibling_scaling_ref, gamma_ref, *start_ref, out_ref = refs
    half = own_ref.shape[0]

    @pl.when(pl.program_id(0) == 0)
    def _():
        out_ref[...] = start_ref[0][...] if has_start else jnp.zeros_like(out_ref)

    gamma = gamma_ref[...]
    out_ref[:half] += dot_t(scaled(own_ref, own_scaling_ref), gamma)
    out_ref[half:] += dot_t(scaled(sibling_ref, sibling_scaling_ref), gamma)


def add_moved(own, sibling, own_scaling, sibling_scaling, gamma, first, start=None):
    rows, (count, cols) = own.shape[0], gamma.shape
    width = next(size for size in (1024, 512, 256, 128) if cols % size == 0 and first % size == 0)
    normals = pl.BlockSpec((rows, width), lambda j: (0, j + first // width))
    return call(
        functools.partial(moved_kernel, start is not None),
        grid=(cols // width,),
        in_specs=[normals, normals, whole((rows, 1)), whole((rows, 1))]
        + [pl.BlockSpec((count, width), lambda j: (0, j))]
        + [whole((2 * rows, count))] * (start is not None),
        out_specs=whole((2 * rows, count)),
        out_shape=jax.ShapeDtypeStruct((2 * rows, count), F32),
        name="moved",
    )(own, sibling, own_scaling, sibling_scaling, gamma, *([] if start is None else [start]))


def by_desk(moved, window, hot):
    quadratic = 0.5 * window.astype(F32) * moved
    total = None
    for _ in range(3):
        piece = quadratic.astype(BF16)
        quadratic = quadratic - piece.astype(F32)
        product = jnp.dot(piece, hot, preferred_element_type=F32)
        total = product if total is None else total + product
    return total


def early_kernel(linear_ref, *refs):
    *groups, mine_ref, theirs_ref = refs
    half = mine_ref.shape[0]
    total = None
    for index in range(0, len(groups), 3):
        moved_ref, window_ref, hot_ref = groups[index : index + 3]
        terms = by_desk(moved_ref[...], window_ref[...], hot_ref[...])
        total = terms if total is None else total + terms
    mine_ref[...] = total[:half] + linear_ref[...]
    theirs_ref[...] = total[half:]


def early_terms(linear, *groups):
    shape = jax.ShapeDtypeStruct(linear.shape, F32)
    return call(early_kernel, out_shape=[shape, shape], name="early")(linear, *groups)


def late_kernel(
    blocks,
    grp_ref,
    own_ref,
    sibling_ref,
    own_scaling_ref,
    sibling_scaling_ref,
    gamma_ref,
    start_ref,
    window_ref,
    hot_ref,
    mine_ref,
    theirs_ref,
    terms_ref,
):
    gamma, hot, half = gamma_ref[...], hot_ref[...], own_ref.shape[0]
    moved = start_ref[half:] + dot_t(scaled(sibling_ref, sibling_scaling_ref), gamma)
    terms_ref[half:] = by_desk(moved, window_ref[half:], hot)
    moved = start_ref[:half] + dot_t(scaled(own_ref, own_scaling_ref), gamma)
    terms_ref[:half] = by_desk(moved, window_ref[:half], hot)
    height = half // blocks
    for index in range(blocks):
        source = pl.multiple_of((index ^ grp_ref[0]) * height, height)
        place = slice(index * height, (index + 1) * height)
        mine_ref[place, :] = terms_ref[pl.ds(source, height), :]
        theirs_ref[place, :] = terms_ref[pl.ds(half + source, height), :].astype(BF16)


def late_terms(grp, blocks, own, sibling, own_scaling, sibling_scaling, gamma, first, start, window, hot):
    rows, (count, cols) = own.shape[0], gamma.shape
    normals = pl.BlockSpec((rows, cols), lambda *_: (0, first // cols))
    return call(
        functools.partial(late_kernel, blocks),
        grid_spec=pltpu.PrefetchScalarGridSpec(
            num_scalar_prefetch=1,
            grid=(1,),
            in_specs=[normals, normals, whole((rows, 1)), whole((rows, 1))]
            + [whole(shape) for shape in (gamma.shape, start.shape, window.shape, hot.shape)],
            out_specs=[whole((rows, DESKS)), whole((rows, DESKS))],
            scratch_shapes=[pltpu.VMEM((2 * rows, DESKS), F32)],
        ),
        out_shape=[jax.ShapeDtypeStruct((rows, DESKS), F32), jax.ShapeDtypeStruct((rows, DESKS), BF16)],
        name="late",
    )(grp[None], own, sibling, own_scaling, sibling_scaling, gamma, start, window, hot)


def local(n_blk, n_grp, normals, mean_square, freedom_degrees, gamma_slab, deltas, desk_map):
    together = lax.optimization_barrier
    blk, grp = lax.axis_index("blk"), lax.axis_index("grp")
    scenarios, columns = normals.shape
    rows = gamma_slab.shape[0]
    chips = n_blk // CORES
    block = scenarios // n_grp
    per_grp = columns // STRIDE
    sibling = [(i, i ^ 1) for i in range(n_blk)]

    def to_sibling(array):
        return lax.ppermute(array, "blk", sibling)

    def from_chips(array):
        parts = [
            lax.ppermute(array, "blk", [(i, (i + CORES * step) % n_blk) for i in range(n_blk)])
            for step in range(1, chips)
        ]
        return parts[0] if len(parts) == 1 else jnp.concatenate(parts, 0)

    def window_of(array, axis):
        own = lax.dynamic_slice_in_dim(array, blk * rows, rows, axis)
        others = [
            lax.dynamic_slice_in_dim(array, lax.rem(blk + n_blk - CORES * step, n_blk) * rows, rows, axis)
            for step in range(1, chips)
        ]
        return own, others[0] if len(others) == 1 else jnp.concatenate(others, axis)

    unit = columns // sum(PARTS)
    starts = [sum(PARTS[:i]) * unit for i in range(len(PARTS) + 1)]
    last = len(PARTS) - 1

    def chunk(index):
        return gamma_slab[:, starts[index] : starts[index + 1]]

    other = to_sibling(normals)
    first = chunk(0)
    first, gamma_slab = together((first, gamma_slab))
    arrived = [from_chips(first)] + [from_chips(chunk(index)) for index in range(1, len(PARTS))]
    gamma_slab, arrived[0] = together((gamma_slab, arrived[0]))

    degrees = freedom_degrees.astype(F32)
    scaling = jnp.sqrt((degrees - 2.0) / degrees / mean_square)[:, None]
    sides = (normals, other, scaling, to_sibling(scaling))
    own_rows, sums = own_moved(*sides, gamma_slab, desk_map, deltas)
    linear = sums[:, :DESKS]

    window_desks = jnp.broadcast_to(desk_map[::STRIDE].astype(F32), (16, per_grp))
    packed = jnp.concatenate([sums[:, DESKS : DESKS + per_grp], window_desks], 0).astype(BF16)
    packed = lax.all_to_all(jnp.broadcast_to(packed, (n_grp,) + packed.shape), "grp", 0, 0, tiled=True)
    desks = packed[:, scenarios].reshape(-1)
    hot = (desks[:, None] == jnp.arange(DESKS).astype(BF16)[None, :]).astype(BF16)
    own_hot, other_hot = window_of(hot, 0)
    window = packed[:, :scenarios].transpose(1, 0, 2).reshape(scenarios, n_grp * per_grp)
    window = jnp.concatenate([window, to_sibling(window)], 0)
    own_window, other_window = window_of(window, 1)

    moved = None
    for index in range(EARLY):
        moved = add_moved(*sides, arrived[index], starts[index], moved)
    mine, theirs = early_terms(linear, own_rows, own_window, own_hot, moved, other_window, other_hot)
    mine = (mine + to_sibling(theirs)).reshape(n_grp, block, DESKS)
    early = lax.all_to_all(mine, "grp", 0, 0, tiled=True).sum(0)

    moved = None
    for index in range(EARLY, last):
        moved = add_moved(*sides, arrived[index], starts[index], moved)
    final, early = together((arrived[last], early))
    mine, theirs = late_terms(grp, n_grp, *sides, final, starts[last], moved, other_window, other_hot)
    late = mine + to_sibling(theirs).astype(F32)
    late = late.reshape(n_grp, block, DESKS)
    bit = 1
    while bit < n_grp:
        halves = late.reshape(late.shape[0] // 2, 2, block, DESKS)
        sent = lax.ppermute(halves[:, 1].astype(BF16), "grp", [(i, i ^ bit) for i in range(n_grp)])
        late = halves[:, 0] + sent.astype(F32)
        bit *= 2
    return early + late[0]


def solution(mesh):
    in_specs = (P("blk", "grp"), P("blk"), P("blk"), P("blk", "grp"), P("grp"), P("grp"))
    out_specs = P(("blk", "grp"), None)
    body = functools.partial(local, mesh.shape["blk"], mesh.shape["grp"])
    return jax.shard_map(body, mesh=mesh, in_specs=in_specs, out_specs=out_specs, check_vma=False)
```

time: 229 us -> 205 us (0.90)
  Pallas kernels: 68.8 us -> 57.8 us
  waiting for transfers between devices: 95.2 us -> 89.4 us
  local copies, waits for them, and re-layouts: 31.8 us -> 27 us
    pallas_call x6 -> x4, Pallas kernels: 48.3 us -> 31.7 us  [add_moved(): call(functools.partial(moved_kernel, start is not None), grid=(cols // wi...]
    pallas_call x2, Pallas kernels: 19.3 us -> 25 us  [the longest x1 22.5 us: own_moved(): call(own_kernel, grid=(cols // width,), in_specs=[normals, normals, whole...]
    gather x3 -> x0, local copies, waits for them, and re-layouts: 4.04 us -> none  [the longest x1 2.91 us: local(): jnp.take(window, order, axis=1).transpose(1, 2, 0, 3)]
    ppermute x6 -> x5, waiting for transfers between devices: 63.1 us -> 60.1 us  [from_chips(): lax.ppermute(array, 'blk', [(i, (i + CORES * step) % n_blk) for i in rang...]
    reshape x0 -> x1, local copies, waits for them, and re-layouts: none -> 2.37 us  [local(): packed[:, :scenarios].transpose(1, 0, 2).reshape(scenarios, n_grp * per_grp)]
    ppermute x6 -> x5, starting transfers between devices: 7.9 us -> 6.53 us  [from_chips(): lax.ppermute(array, 'blk', [(i, (i + CORES * step) % n_blk) for i in rang...]
    unnamed x13 -> x24, local copies, waits for them, and re-layouts: 7.9 us -> 8.33 us
  transfers between devices with their start and end apart: 15 -> 15, of which waited for: 12 -> 10; matrix products, arithmetic and copies ran while one was open for 13% -> 11% of each run, Pallas kernels for 22% -> 27%
where the time goes in v2:
time: 205 us; the launch traced here: 203 us
  waiting for transfers between devices  89.4 us (44%)
  Pallas kernels  57.8 us (28%)
  local copies, waits for them, and re-layouts  27 us (13%)
  starting transfers between devices  26.2 us (13%)
  other arithmetic  2.62 us (1%)
    ppermute x5, waiting for transfers between devices, from_chips(): lax.ppermute(array, 'blk', [(i, (i + CORES * step) % n_blk) for i in rang...  60.1 us
    pallas_call x4, Pallas kernels, add_moved(): call(functools.partial(moved_kernel, start is not None), grid=(cols // wi...  31.7 us
    pallas_call x1, Pallas kernels, own_moved(): call(own_kernel, grid=(cols // width,), in_specs=[normals, normals, whole...  22.5 us
    all_to_all x1, waiting for transfers between devices, local(): lax.all_to_all(jnp.broadcast_to(packed, (n_grp,) + packed.shape), 'grp',...  21.6 us
    slice x5, local copies, waits for them, and re-layouts, chunk(): return gamma_slab[:, starts[index]:starts[index + 1]]  12.5 us
    unnamed x24, local copies, waits for them, and re-layouts  8.33 us
    ppermute x3, starting transfers between devices, local(): lax.ppermute(halves[:, 1].astype(BF16), 'grp', [(i, i ^ bit) for i in ran...  6.63 us
    ppermute x5, starting transfers between devices, from_chips(): lax.ppermute(array, 'blk', [(i, (i + CORES * step) % n_blk) for i in rang...  6.53 us
  transfers between devices with their start and end apart: 15, of which 10 were waited for; matrix products, arithmetic and copies ran while one was open for 11% of the time, Pallas kernels for 27%

profile of v2, /device:TPU:0, one launch (start us, length us, event | category | flops | bytes accessed | tf_op | source)
XLA Modules:
  0.0 203.4 jit_solution(18080619268043892128)
XLA Ops:
  0.0 0.5 collective-permute-start.1
  0.5 1.4 slice.52
  1.9 0.0 copy-start.9
  1.9 0.0 copy-start.10
  1.9 0.0 copy-start.7
  1.9 0.0 copy-start.8
  1.9 2.6 %collective-permute-start.3 = (bf16[256,2560]{1,0:T(8,128)(2,1)S(1)}, bf16[256,2560]{1,0:T(8,128)(2,1)S(1)}, u32[]{:S(2)}, u32[]{:S(2)}) collective-permute-start(bf16[256,2560]{1,0:T(8,128)(2,1)S(1)} %slice.52), channel_id=1, source_target_pairs={{0,16},{8,24},{16,0},{24,8},{1,17},{9,25},{17,1},{25,9},{2,18},{10... | collective-permute-start | bytes 3932168 | tf_op jit(solution)/shard_map/ppermute | solution.py:196
  4.5 4.3 %slice.59 = bf16[256,7680]{1,0:T(8,128)(2,1)} slice(bf16[256,16384]{1,0:T(8,128)(2,1)} %gamma_ref), slice={[0:256], [2560:10240]} | slice | bytes 7864320 | tf_op jit(solution)/shard_map/slice | solution.py:214
  8.7 0.0 collective-permute-start.5
  8.7 0.0 copy-done.9
  8.8 0.2 copy.30.own_scaling_ref.refs_2_
  8.9 0.3 collective-permute-start.2
  9.2 0.2 slice.56
  9.5 24.6 %collective-permute-done.3.refs_4_ = bf16[256,2560]{1,0:T(8,128)(2,1)S(1)} collective-permute-done((bf16[256,2560]{1,0:T(8,128)(2,1)S(1)}, bf16[256,2560]{1,0:T(8,128)(2,1)S(1)}, u32[]{:S(2)}, u32[]{:S(2)}) %collective-permute-start.3) | collective-permute-done | bytes 1310752 | tf_op jit(solution)/shard_map/ppermute | solution.py:196
  34.1 0.0 collective-permute-done.2.sibling_scaling_ref.refs_3_
  34.1 0.0 collective-permute-done.1.sibling_ref.refs_1_
  34.1 0.0 copy-start
  34.1 3.8 %copy-done = bf16[256,16384]{1,0:T(8,128)(2,1)S(1)} copy-done((bf16[256,16384]{1,0:T(8,128)(2,1)S(1)}, bf16[256,16384]{1,0:T(8,128)(2,1)}, u32[]{:S(2)}) %copy-start) | copy-done | bytes 8388632
  38.0 22.5 %own_rows.1 = (f32[1024,256]{1,0:T(8,128)S(1)}, f32[512,256]{1,0:T(8,128)S(1)}) custom-call(bf16[512,16384]{1,0:T(8,128)(2,1)} %own_ref.3, bf16[512,16384]{1,0:T(8,128)(2,1)} %collective-permute-done.1.sibling_ref.refs_1_, f32[512,1]{1,0:T(8,128)S(1)} %copy.30.own_scaling_ref.refs_2_, f32[512,1]{1,0:T(8,128)S(1)} %collective-permute-done.2.sibling_scaling_ref.refs_3_, ...), custom_call_target="tpu_custom_call" | custom-call | tf_op jit(solution)/shard_map/own_rows/pallas_call | solution.py:64
  60.5 1.0 copy-done.3
  61.4 0.8 copy-done.5
  62.3 1.1 broadcast_in_dim.26
  63.4 6.3 %all-to-all-start = ((bf16[8,528,128]{2,1,0:T(8,128)(2,1)}), bf16[8,528,128]{2,1,0:T(8,128)(2,1)}, u32[]{:S(2)}, u32[]{:S(2)}) async-start(bf16[8,528,128]{2,1,0:T(8,128)(2,1)} %broadcast_in_dim.26), calls=%async_computation | async-start | bytes 2162688 | tf_op jit(solution)/shard_map/all_to_all | solution.py:230
  69.7 3.2 %slice.61 = bf16[256,4608]{1,0:T(8,128)(2,1)} slice(bf16[256,16384]{1,0:T(8,128)(2,1)} %gamma_ref), slice={[0:256], [10240:14848]} | slice | bytes 4718592 | tf_op jit(solution)/shard_map/slice | solution.py:214
  72.9 1.5 collective-permute-start.8
  74.4 21.6 %all-to-all-done = bf16[8,528,128]{2,1,0:T(8,128)(2,1)} async-done(((bf16[8,528,128]{2,1,0:T(8,128)(2,1)}), bf16[8,528,128]{2,1,0:T(8,128)(2,1)}, u32[]{:S(2)}, u32[]{:S(2)}) %all-to-all-start) | async-done | bytes 1081376 | tf_op jit(solution)/shard_map/all_to_all | solution.py:230
  96.0 2.4 %copy_bitcast_fusion = bf16[512,1024]{1,0:T(8,128)(2,1)} fusion(bf16[8,528,128]{2,1,0:T(8,128)(2,1)} %all-to-all-done), kind=kLoop, calls=%fused_computation | loop fusion | bytes 2097152 | tf_op jit(solution)/shard_map/reshape | solution.py:234
  98.4 0.0 collective-permute-start.4
  98.4 1.3 copy-done.2
  99.7 5.3 %moved.4.refs_5_ = f32[1024,256]{1,0:T(8,128)S(1)} custom-call(bf16[512,16384]{1,0:T(8,128)(2,1)} %own_ref.3, bf16[512,16384]{1,0:T(8,128)(2,1)} %collective-permute-done.1.sibling_ref.refs_1_, f32[512,1]{1,0:T(8,128)S(1)} %copy.30.own_scaling_ref.refs_2_, f32[512,1]{1,0:T(8,128)S(1)} %collective-permute-done.2.sibling_scaling_ref.refs_3_, ...), custom_call_target="tpu_custom_call" | custom-call | tf_op jit(solution)/shard_map/moved/pallas_call | solution.py:95
  105.1 13.4 %collective-permute-done.5.refs_4_ = bf16[256,7680]{1,0:T(8,128)(2,1)} collective-permute-done((bf16[256,7680]{1,0:T(8,128)(2,1)}, bf16[256,7680]{1,0:T(8,128)(2,1)}, u32[]{:S(2)}, u32[]{:S(2)}) %collective-permute-start.5) | collective-permute-done | bytes 3932192 | tf_op jit(solution)/shard_map/ppermute | solution.py:196
  118.5 15.0 %moved.5.refs_3_ = f32[1024,256]{1,0:T(8,128)S(1)} custom-call(bf16[512,16384]{1,0:T(8,128)(2,1)} %own_ref.3, bf16[512,16384]{1,0:T(8,128)(2,1)} %collective-permute-done.1.sibling_ref.refs_1_, f32[512,1]{1,0:T(8,128)S(1)} %copy.30.own_scaling_ref.refs_2_, f32[512,1]{1,0:T(8,128)S(1)} %collective-permute-done.2.sibling_scaling_ref.refs_3_, ...), custom_call_target="tpu_custom_call" | custom-call | tf_op jit(solution)/shard_map/moved/pallas_call | solution.py:95
  133.4 0.7 slice.70
  134.2 0.2 compare_convert_fusion
  134.4 1.4 constant_dynamic-update-slice_fusion.1
  135.8 0.0 collective-permute-done.4
  135.8 1.4 constant_dynamic-update-slice_fusion
  137.2 0.1 constant_dynamic-slice_fusion.1
  137.4 1.1 early.1
  138.5 0.1 collective-permute-start.6
  138.6 1.9 slice.60
  140.5 1.9 collective-permute-start.7
  142.4 0.0 collective-permute-done.6
  142.4 0.7 add.34
  143.1 5.8 %all-to-all-start.1 = ((f32[8,64,128]{2,1,0:T(8,128)}), f32[8,64,128]{2,1,0:T(8,128)}, u32[]{:S(2)}, u32[]{:S(2)}) async-start(f32[8,64,128]{2,1,0:T(8,128)} %bitcast.53), calls=%async_computation.1 | async-start | bytes 524288 | tf_op jit(solution)/shard_map/all_to_all | solution.py:243
  149.0 1.7 slice.53
  150.6 0.5 collective-permute-start
  151.2 17.7 %collective-permute-done.8.refs_4_ = bf16[256,4608]{1,0:T(8,128)(2,1)S(1)} collective-permute-done((bf16[256,4608]{1,0:T(8,128)(2,1)}, bf16[256,4608]{1,0:T(8,128)(2,1)S(1)}, u32[]{:S(2)}, u32[]{:S(2)}) %collective-permute-start.8) | collective-permute-done | bytes 2359328 | tf_op jit(solution)/shard_map/ppermute | solution.py:196
  168.9 8.9 %moved.6.refs_5_ = f32[1024,256]{1,0:T(8,128)S(1)} custom-call(bf16[512,16384]{1,0:T(8,128)(2,1)} %own_ref.3, bf16[512,16384]{1,0:T(8,128)(2,1)} %collective-permute-done.1.sibling_ref.refs_1_, f32[512,1]{1,0:T(8,128)S(1)} %copy.30.own_scaling_ref.refs_2_, f32[512,1]{1,0:T(8,128)S(1)} %collective-permute-done.2.sibling_scaling_ref.refs_3_, ...), custom_call_target="tpu_custom_call" | custom-call | tf_op jit(solution)/shard_map/moved/pallas_call | solution.py:95
  177.9 2.4 %collective-permute-done.7.refs_4_ = bf16[256,1024]{1,0:T(8,128)(2,1)} collective-permute-done((bf16[256,1024]{1,0:T(8,128)(2,1)}, bf16[256,1024]{1,0:T(8,128)(2,1)}, u32[]{:S(2)}, u32[]{:S(2)}) %collective-permute-start.7) | collective-permute-done | bytes 524320 | tf_op jit(solution)/shard_map/ppermute | solution.py:196
  180.3 2.5 %moved.7.start_ref = f32[1024,256]{1,0:T(8,128)S(1)} custom-call(bf16[512,16384]{1,0:T(8,128)(2,1)} %own_ref.3, bf16[512,16384]{1,0:T(8,128)(2,1)} %collective-permute-done.1.sibling_ref.refs_1_, f32[512,1]{1,0:T(8,128)S(1)} %copy.30.own_scaling_ref.refs_2_, f32[512,1]{1,0:T(8,128)S(1)} %collective-permute-done.2.sibling_scaling_ref.refs_3_, ...), custom_call_target="tpu_custom_call" | custom-call | tf_op jit(solution)/shard_map/moved/pallas_call | solution.py:95
  182.7 0.0 all-to-all-done.1
  182.7 1.0 reduce_sum.9
  183.7 2.0 collective-permute-done.gamma_ref
  185.7 2.5 %late.1 = (f32[512,128]{1,0:T(8,128)S(1)}, bf16[512,128]{1,0:T(8,128)(2,1)S(1)}) custom-call(s32[1]{0:T(128)} %bitcast.6.grp_ref, bf16[512,16384]{1,0:T(8,128)(2,1)} %own_ref.3, bf16[512,16384]{1,0:T(8,128)(2,1)} %collective-permute-done.1.sibling_ref.refs_1_, f32[512,1]{1,0:T(8,128)S(1)} %copy.30.own_scaling_ref.refs_2_, ...), custom_call_target="tpu_custom_call" | custom-call | tf_op jit(solution)/shard_map/late/pallas_call | solution.py:166
  188.2 0.1 collective-permute-start.9
  188.3 1.3 collective-permute-done.9
  189.7 1.8 collective-permute-start.10
  191.5 2.5 %collective-permute-done.10 = bf16[4,64,128]{2,1,0:T(8,128)(2,1)S(1)} collective-permute-done((bf16[4,64,128]{2,1,0:T(8,128)(2,1)S(1)}, bf16[4,64,128]{2,1,0:T(8,128)(2,1)S(1)}, u32[]{:S(2)}, u32[]{:S(2)}) %collective-permute-start.10) | collective-permute-done | bytes 65568 | tf_op jit(solution)/shard_map/ppermute | solution.py:255
  194.0 1.9 collective-permute-start.11
  195.9 2.1 %collective-permute-done.11 = bf16[2,64,128]{2,1,0:T(8,128)(2,1)S(1)} collective-permute-done((bf16[2,64,128]{2,1,0:T(8,128)(2,1)S(1)}, bf16[2,64,128]{2,1,0:T(8,128)(2,1)S(1)}, u32[]{:S(2)}, u32[]{:S(2)}) %collective-permute-start.11) | collective-permute-done | bytes 32800 | tf_op jit(solution)/shard_map/ppermute | solution.py:255
  198.0 2.9 %collective-permute-start.12 = (bf16[1,64,128]{2,1,0:T(8,128)(2,1)S(1)}, bf16[1,64,128]{2,1,0:T(8,128)(2,1)S(1)}, u32[]{:S(2)}, u32[]{:S(2)}) collective-permute-start(bf16[1,64,128]{2,1,0:T(8,128)(2,1)S(1)} %fusion.8), channel_id=1, source_target_pairs={{0,4},{1,5},{2,6},{3,7},{4,0},{5,1},{6,2},{7,3},{8,12},{9,13},{10,... | collective-permute-start | bytes 49160 | tf_op jit(solution)/shard_map/ppermute | solution.py:255
  200.9 1.8 collective-permute-done.12
  202.7 0.6 fusion.7
  (28 shorter events, 0.2 us)
Async XLA Ops:
  0.0 34.1 %collective-permute-start.1 = (bf16[512,16384]{1,0:T(8,128)(2,1)}, bf16[512,16384]{1,0:T(8,128)(2,1)}, u32[]{:S(2)}, u32[]{:S(2)}) collective-permute-start(bf16[512,16384]{1,0:T(8,128)(2,1)} %own_ref.3), channel_id=1, source_target_pairs={{0,8},{8,0},{16,24},{24,16},{1,9},{9,1},{17,25},{25,17},{2,10},{10... | collective-permute-start | bytes 50331656 | tf_op jit(solution)/shard_map/ppermute | solution.py:192
  1.9 6.9 %copy-start.9 = (f32[512]{0:T(512)S(1)}, f32[512]{0:T(512)}, u32[]{:S(2)}) copy-start(f32[512]{0:T(512)} %param.7) | copy-start | bytes 6148
  1.9 6.9 %copy-start.10 = (s32[512]{0:T(512)S(1)}, s32[512]{0:T(512)}, u32[]{:S(2)}) copy-start(s32[512]{0:T(512)} %param.8) | copy-start | bytes 6148
  1.9 7.3 %copy-start.7 = (s32[16384]{0:T(1024)S(1)}, s32[16384]{0:T(1024)}, u32[]{:S(2)}) copy-start(s32[16384]{0:T(1024)} %param.11) | copy-start | bytes 196612
  1.9 7.6 %copy-start.8 = (bf16[16384]{0:T(1024)(128)(2,1)S(1)}, bf16[16384]{0:T(1024)(128)(2,1)}, u32[]{:S(2)}) copy-start(bf16[16384]{0:T(1024)(128)(2,1)} %param.10) | copy-start | bytes 98308
  1.9 32.2 %collective-permute-start.3 = (bf16[256,2560]{1,0:T(8,128)(2,1)S(1)}, bf16[256,2560]{1,0:T(8,128)(2,1)S(1)}, u32[]{:S(2)}, u32[]{:S(2)}) collective-permute-start(bf16[256,2560]{1,0:T(8,128)(2,1)S(1)} %slice.52), channel_id=1, source_target_pairs={{0,16},{8,24},{16,0},{24,8},{1,17},{9,25},{17,1},{25,9},{2,18},{10... | collective-permute-start | bytes 3932168 | tf_op jit(solution)/shard_map/ppermute | solution.py:196
  8.7 109.7 %collective-permute-start.5 = (bf16[256,7680]{1,0:T(8,128)(2,1)}, bf16[256,7680]{1,0:T(8,128)(2,1)}, u32[]{:S(2)}, u32[]{:S(2)}) collective-permute-start(bf16[256,7680]{1,0:T(8,128)(2,1)} %slice.59), channel_id=1, source_target_pairs={{0,16},{8,24},{16,0},{24,8},{1,17},{9,25},{17,1},{25,9},{2,18},{10... | collective-permute-start | bytes 11796488 | tf_op jit(solution)/shard_map/ppermute | solution.py:196
  8.9 25.2 %collective-permute-start.2 = (f32[512,1]{1,0:T(8,128)S(1)}, f32[512,1]{1,0:T(8,128)S(1)}, u32[]{:S(2)}, u32[]{:S(2)}) collective-permute-start(f32[512,1]{1,0:T(8,128)S(1)} %copy.30.own_scaling_ref.refs_2_), channel_id=1, source_target_pairs={{0,8},{8,0},{16,24},{24,16},{1,9},{9,1},{17,25},{25,17},{2,10},{10... | collective-permute-start | bytes 6152 | tf_op jit(solution)/shard_map/ppermute | solution.py:192
  34.1 26.4 %copy-start.1 = (bf16[256,2560]{1,0:T(8,128)(2,1)}, bf16[256,2560]{1,0:T(8,128)(2,1)S(1)}, u32[]{:S(2)}) copy-start(bf16[256,2560]{1,0:T(8,128)(2,1)S(1)} %collective-permute-done.3.refs_4_) | copy-start | bytes 3932164
  34.1 3.9 %copy-start = (bf16[256,16384]{1,0:T(8,128)(2,1)S(1)}, bf16[256,16384]{1,0:T(8,128)(2,1)}, u32[]{:S(2)}) copy-start(bf16[256,16384]{1,0:T(8,128)(2,1)} %gamma_ref) | copy-start | bytes 25165828
  60.5 1.0 copy-start.3
  61.4 0.8 copy-start.5
  63.4 32.6 %all-to-all-start = ((bf16[8,528,128]{2,1,0:T(8,128)(2,1)}), bf16[8,528,128]{2,1,0:T(8,128)(2,1)}, u32[]{:S(2)}, u32[]{:S(2)}) async-start(bf16[8,528,128]{2,1,0:T(8,128)(2,1)} %broadcast_in_dim.26), calls=%async_computation | async-start | bytes 2162688 | tf_op jit(solution)/shard_map/all_to_all | solution.py:230
  72.9 25.4 %copy-start.6 = (f32[512,256]{1,0:T(8,128)S(1)}, f32[512,256]{1,0:T(8,128)}, u32[]{:S(2)}) copy-start(f32[512,256]{1,0:T(8,128)} %copy-done.5) | copy-start | bytes 1572868
  72.9 96.0 %collective-permute-start.8 = (bf16[256,4608]{1,0:T(8,128)(2,1)}, bf16[256,4608]{1,0:T(8,128)(2,1)S(1)}, u32[]{:S(2)}, u32[]{:S(2)}) collective-permute-start(bf16[256,4608]{1,0:T(8,128)(2,1)} %slice.61), channel_id=1, source_target_pairs={{0,16},{8,24},{16,0},{24,8},{1,17},{9,25},{17,1},{25,9},{2,18},{10... | collective-permute-start | bytes 7077896 | tf_op jit(solution)/shard_map/ppermute | solution.py:196
  98.4 37.4 %collective-permute-start.4 = (bf16[512,1024]{1,0:T(8,128)(2,1)}, bf16[512,1024]{1,0:T(8,128)(2,1)}, u32[]{:S(2)}, u32[]{:S(2)}) collective-permute-start(bf16[512,1024]{1,0:T(8,128)(2,1)} %copy_bitcast_fusion), channel_id=1, source_target_pairs={{0,8},{8,0},{16,24},{24,16},{1,9},{9,1},{17,25},{25,17},{2,10},{10... | collective-permute-start | bytes 3145736 | tf_op jit(solution)/shard_map/ppermute | solution.py:192
  98.4 1.3 copy-start.2
  135.8 1.6 copy-start.4
  138.5 3.9 %collective-permute-start.6 = (f32[512,128]{1,0:T(8,128)S(1)}, f32[512,128]{1,0:T(8,128)S(1)}, u32[]{:S(2)}, u32[]{:S(2)}) collective-permute-start(f32[512,128]{1,0:T(8,128)S(1)} %get-tuple-element.24), channel_id=1, source_target_pairs={{0,8},{8,0},{16,24},{24,16},{1,9},{9,1},{17,25},{25,17},{2,10},{10... | collective-permute-start | bytes 786440 | tf_op jit(solution)/shard_map/ppermute | solution.py:192
  140.5 39.8 %collective-permute-start.7 = (bf16[256,1024]{1,0:T(8,128)(2,1)}, bf16[256,1024]{1,0:T(8,128)(2,1)}, u32[]{:S(2)}, u32[]{:S(2)}) collective-permute-start(bf16[256,1024]{1,0:T(8,128)(2,1)} %slice.60), channel_id=1, source_target_pairs={{0,16},{8,24},{16,0},{24,8},{1,17},{9,25},{17,1},{25,9},{2,18},{10... | collective-permute-start | bytes 1572872 | tf_op jit(solution)/shard_map/ppermute | solution.py:196
  143.1 39.6 %all-to-all-start.1 = ((f32[8,64,128]{2,1,0:T(8,128)}), f32[8,64,128]{2,1,0:T(8,128)}, u32[]{:S(2)}, u32[]{:S(2)}) async-start(f32[8,64,128]{2,1,0:T(8,128)} %bitcast.53), calls=%async_computation.1 | async-start | bytes 524288 | tf_op jit(solution)/shard_map/all_to_all | solution.py:243
  150.6 35.0 %collective-permute-start = (bf16[256,512]{1,0:T(8,128)(2,1)}, bf16[256,512]{1,0:T(8,128)(2,1)}, u32[]{:S(2)}, u32[]{:S(2)}) collective-permute-start(bf16[256,512]{1,0:T(8,128)(2,1)} %slice.53), channel_id=1, source_target_pairs={{0,16},{8,24},{16,0},{24,8},{1,17},{9,25},{17,1},{25,9},{2,18},{10... | collective-permute-start | bytes 786440 | tf_op jit(solution)/shard_map/ppermute | solution.py:196
  188.2 1.4 collective-permute-start.9
  189.7 4.3 %collective-permute-start.10 = (bf16[4,64,128]{2,1,0:T(8,128)(2,1)S(1)}, bf16[4,64,128]{2,1,0:T(8,128)(2,1)S(1)}, u32[]{:S(2)}, u32[]{:S(2)}) collective-permute-start(bf16[4,64,128]{2,1,0:T(8,128)(2,1)S(1)} %fusion.1), channel_id=1, source_target_pairs={{0,1},{1,0},{2,3},{3,2},{4,5},{5,4},{6,7},{7,6},{8,9},{9,8},{10,11... | collective-permute-start | bytes 196616 | tf_op jit(solution)/shard_map/ppermute | solution.py:255
  194.0 4.0 %collective-permute-start.11 = (bf16[2,64,128]{2,1,0:T(8,128)(2,1)S(1)}, bf16[2,64,128]{2,1,0:T(8,128)(2,1)S(1)}, u32[]{:S(2)}, u32[]{:S(2)}) collective-permute-start(bf16[2,64,128]{2,1,0:T(8,128)(2,1)S(1)} %fusion.4), channel_id=1, source_target_pairs={{0,2},{1,3},{2,0},{3,1},{4,6},{5,7},{6,4},{7,5},{8,10},{9,11},{10,... | collective-permute-start | bytes 98312 | tf_op jit(solution)/shard_map/ppermute | solution.py:255
  198.0 4.7 %collective-permute-start.12 = (bf16[1,64,128]{2,1,0:T(8,128)(2,1)S(1)}, bf16[1,64,128]{2,1,0:T(8,128)(2,1)S(1)}, u32[]{:S(2)}, u32[]{:S(2)}) collective-permute-start(bf16[1,64,128]{2,1,0:T(8,128)(2,1)S(1)} %fusion.8), channel_id=1, source_target_pairs={{0,4},{1,5},{2,6},{3,7},{4,0},{5,1},{6,2},{7,3},{8,12},{9,13},{10,... | collective-permute-start | bytes 49160 | tf_op jit(solution)/shard_map/ppermute | solution.py:255

commit v3 on v2

--- a/solution.py
+++ b/solution.py
@@ -10,7 +10,7 @@
 DESKS = 128
 STRIDE = 128
 CORES = 2
-PARTS = (5, 15, 9, 2, 1)
+PARTS = (5, 15, 8, 3, 1)
 EARLY = 2
 VMEM_BYTES = 40 * 2**20
 
@@ -104,10 +104,10 @@
     )(own, sibling, own_scaling, sibling_scaling, gamma, *([] if start is None else [start]))
 
 
-def by_desk(moved, window, hot):
+def by_desk(moved, window, hot, pieces=3):
     quadratic = 0.5 * window.astype(F32) * moved
     total = None
-    for _ in range(3):
+    for _ in range(pieces):
         piece = quadratic.astype(BF16)
         quadratic = quadratic - piece.astype(F32)
         product = jnp.dot(piece, hot, preferred_element_type=F32)
@@ -132,50 +132,63 @@
     return call(early_kernel, out_shape=[shape, shape], name="early")(linear, *groups)
 
 
-def late_kernel(
-    blocks,
-    grp_ref,
-    own_ref,
-    sibling_ref,
-    own_scaling_ref,
-    sibling_scaling_ref,
-    gamma_ref,
-    start_ref,
-    window_ref,
-    hot_ref,
-    mine_ref,
-    theirs_ref,
-    terms_ref,
-):
-    gamma, hot, half = gamma_ref[...], hot_ref[...], own_ref.shape[0]
-    moved = start_ref[half:] + dot_t(scaled(sibling_ref, sibling_scaling_ref), gamma)
-    terms_ref[half:] = by_desk(moved, window_ref[half:], hot)
-    moved = start_ref[:half] + dot_t(scaled(own_ref, own_scaling_ref), gamma)
-    terms_ref[:half] = by_desk(moved, window_ref[:half], hot)
+def middle_kernel(own_ref, sibling_ref, own_scaling_ref, sibling_scaling_ref, gamma_ref, start_ref, window_ref, hot_ref, terms_ref, moved_ref):
+    step = pl.program_id(0)
+    half = own_ref.shape[0]
+
+    @pl.when(step == 0)
+    def _():
+        moved_ref[...] = start_ref[...]
+
+    gamma = gamma_ref[...]
+    moved_ref[:half] += dot_t(scaled(own_ref, own_scaling_ref), gamma)
+    moved_ref[half:] += dot_t(scaled(sibling_ref, sibling_scaling_ref), gamma)
+
+    @pl.when(step == pl.num_programs(0) - 1)
+    def _():
+        terms_ref[...] = by_desk(moved_ref[...], window_ref[...], hot_ref[...], 2)
+
+
+def middle_terms(own, sibling, own_scaling, sibling_scaling, gamma, first, start, window, hot):
+    rows, (count, cols) = own.shape[0], gamma.shape
+    width = next(size for size in (256, 128) if cols % size == 0 and first % size == 0)
+    normals = pl.BlockSpec((rows, width), lambda j: (0, j + first // width))
+    return call(
+        middle_kernel,
+        grid=(cols // width,),
+        in_specs=[normals, normals, whole((rows, 1)), whole((rows, 1))]
+        + [pl.BlockSpec((count, width), lambda j: (0, j))]
+        + [whole(shape) for shape in (start.shape, window.shape, hot.shape)],
+        out_specs=whole((2 * rows, DESKS)),
+        out_shape=jax.ShapeDtypeStruct((2 * rows, DESKS), F32),
+        scratch_shapes=[pltpu.VMEM((2 * rows, count), F32)],
+        name="middle",
+    )(own, sibling, own_scaling, sibling_scaling, gamma, start, window, hot)
+
+
+def late_kernel(blocks, first, grp_ref, normals_ref, scaling_ref, gamma_ref, start_ref, window_ref, hot_ref, out_ref, terms_ref):
+    half = normals_ref.shape[0]
+    place = slice(first, first + half)
+    moved = dot_t(scaled(normals_ref, scaling_ref), gamma_ref[...])
+    terms_ref[...] = start_ref[place] + by_desk(moved, window_ref[place], hot_ref[...], 1)
     height = half // blocks
     for index in range(blocks):
         source = pl.multiple_of((index ^ grp_ref[0]) * height, height)
-        place = slice(index * height, (index + 1) * height)
-        mine_ref[place, :] = terms_ref[pl.ds(source, height), :]
-        theirs_ref[place, :] = terms_ref[pl.ds(half + source, height), :].astype(BF16)
-
-
-def late_terms(grp, blocks, own, sibling, own_scaling, sibling_scaling, gamma, first, start, window, hot):
-    rows, (count, cols) = own.shape[0], gamma.shape
-    normals = pl.BlockSpec((rows, cols), lambda *_: (0, first // cols))
-    return call(
-        functools.partial(late_kernel, blocks),
-        grid_spec=pltpu.PrefetchScalarGridSpec(
-            num_scalar_prefetch=1,
-            grid=(1,),
-            in_specs=[normals, normals, whole((rows, 1)), whole((rows, 1))]
-            + [whole(shape) for shape in (gamma.shape, start.shape, window.shape, hot.shape)],
-            out_specs=[whole((rows, DESKS)), whole((rows, DESKS))],
-            scratch_shapes=[pltpu.VMEM((2 * rows, DESKS), F32)],
-        ),
-        out_shape=[jax.ShapeDtypeStruct((rows, DESKS), F32), jax.ShapeDtypeStruct((rows, DESKS), BF16)],
+        out_ref[index * height : (index + 1) * height, :] = terms_ref[pl.ds(source, height), :].astype(out_ref.dtype)
+
+
+def late_terms(grp, blocks, side, kind, normals, scaling, gamma, start, window, hot):
+    rows = normals.shape[0]
+    in_vmem = pl.BlockSpec(memory_space=pltpu.VMEM)
+    return pl.pallas_call(
+        functools.partial(late_kernel, blocks, side * rows),
+        in_specs=[pl.BlockSpec(memory_space=pltpu.SMEM)] + [in_vmem] * 6,
+        out_specs=in_vmem,
+        scratch_shapes=[pltpu.VMEM((rows, DESKS), F32)],
+        out_shape=jax.ShapeDtypeStruct((rows, DESKS), kind),
+        compiler_params=pltpu.CompilerParams(vmem_limit_bytes=12 * 2**20),
         name="late",
-    )(grp[None], own, sibling, own_scaling, sibling_scaling, gamma, start, window, hot)
+    )(grp[None], normals, scaling, gamma, start, window, hot)
 
 
 def local(n_blk, n_grp, normals, mean_square, freedom_degrees, gamma_slab, deltas, desk_map):
@@ -243,18 +256,24 @@
     early = lax.all_to_all(mine, "grp", 0, 0, tiled=True).sum(0)
 
     moved = None
-    for index in range(EARLY, last):
+    for index in range(EARLY, last - 1):
         moved = add_moved(*sides, arrived[index], starts[index], moved)
-    final, early = together((arrived[last], early))
-    mine, theirs = late_terms(grp, n_grp, *sides, final, starts[last], moved, other_window, other_hot)
+    ready = (arrived[last - 1], early, normals[:, starts[last] :], other[:, starts[last] :])
+    next_to_last, early, own_end, other_end = together(ready)
+    terms = middle_terms(*sides, next_to_last, starts[last - 1], moved, other_window, other_hot)
+    rest = (arrived[last], terms, other_window, other_hot)
+    theirs = late_terms(grp, n_grp, 1, BF16, other_end, sides[3], *rest)
+    mine = late_terms(grp, n_grp, 0, F32, own_end, sides[2], *rest)
     late = mine + to_sibling(theirs).astype(F32)
     late = late.reshape(n_grp, block, DESKS)
-    bit = 1
+    bit, width = 1, min(4, n_grp)
     while bit < n_grp:
-        halves = late.reshape(late.shape[0] // 2, 2, block, DESKS)
-        sent = lax.ppermute(halves[:, 1].astype(BF16), "grp", [(i, i ^ bit) for i in range(n_grp)])
-        late = halves[:, 0] + sent.astype(F32)
-        bit *= 2
+        parts = late.reshape(late.shape[0] // width, width, block, DESKS)
+        late = parts[:, 0]
+        for step in range(1, width):
+            pairs = [(i, i ^ (step * bit)) for i in range(n_grp)]
+            late = late + lax.ppermute(parts[:, step].astype(BF16), "grp", pairs).astype(F32)
+        bit, width = bit * width, 2
     return early + late[0]
 
 

time: 205 us -> 202 us (0.985)
  waiting for transfers between devices: 89.4 us -> 81.3 us
  local copies, waits for them, and re-layouts: 27 us -> 33.4 us
    ppermute x5, waiting for transfers between devices: 60.1 us -> 51.8 us  [from_chips(): lax.ppermute(array, 'blk', [(i, (i + CORES * step) % n_blk) for i in rang...]
    pallas_call x4 -> x3, Pallas kernels: 31.7 us -> 26 us  [add_moved(): call(functools.partial(moved_kernel, start is not None), grid=(cols // wi...]
    pallas_call x1 -> x3, Pallas kernels: 2.51 us -> 6.4 us  [the longest x1 5.32 us: middle_terms(): call(middle_kernel, grid=(cols // width,), in_specs=[normals, normals, wh...]
    slice x0 -> x2, local copies, waits for them, and re-layouts: none -> 3.75 us  [the longest x1 1.88 us: local(): other[:, starts[last]:]]
    unnamed x24 -> x28, local copies, waits for them, and re-layouts: 8.33 us -> 10.8 us
    ppermute x3 -> x4, waiting for transfers between devices: 6.39 us -> 5.9 us  [local(): lax.ppermute(parts[:, step].astype(BF16), 'grp', pairs).astype(F32)]
    ppermute x3 -> x4, starting transfers between devices: 6.63 us -> 6.27 us  [local(): lax.ppermute(parts[:, step].astype(BF16), 'grp', pairs).astype(F32)]
  transfers between devices with their start and end apart: 15 -> 16, of which waited for: 10 -> 11; matrix products, arithmetic and copies ran while one was open for 11% -> 13% of each run, Pallas kernels for 27% -> 28%
where the time goes in v3:
time: 202 us; the launch traced here: 200 us
  waiting for transfers between devices  81.3 us (40%)
  Pallas kernels  56.1 us (28%)
  local copies, waits for them, and re-layouts  33.4 us (17%)
  starting transfers between devices  26.8 us (13%)
  other arithmetic  2.64 us (1%)
    ppermute x5, waiting for transfers between devices, from_chips(): lax.ppermute(array, 'blk', [(i, (i + CORES * step) % n_blk) for i in rang...  51.8 us
    pallas_call x3, Pallas kernels, add_moved(): call(functools.partial(moved_kernel, start is not None), grid=(cols // wi...  26 us
    pallas_call x1, Pallas kernels, own_moved(): call(own_kernel, grid=(cols // width,), in_specs=[normals, normals, whole...  22.5 us
    all_to_all x1, waiting for transfers between devices, local(): lax.all_to_all(jnp.broadcast_to(packed, (n_grp,) + packed.shape), 'grp',...  21.7 us
    slice x5, local copies, waits for them, and re-layouts, chunk(): return gamma_slab[:, starts[index]:starts[index + 1]]  12.6 us
    unnamed x28, local copies, waits for them, and re-layouts  10.8 us
    ppermute x5, starting transfers between devices, from_chips(): lax.ppermute(array, 'blk', [(i, (i + CORES * step) % n_blk) for i in rang...  7.05 us
    all_to_all x1, starting transfers between devices, local(): lax.all_to_all(jnp.broadcast_to(packed, (n_grp,) + packed.shape), 'grp',...  6.28 us
  transfers between devices with their start and end apart: 16, of which 11 were waited for; matrix products, arithmetic and copies ran while one was open for 13% of the time, Pallas kernels for 28%

profile of v3, /device:TPU:0, one launch (start us, length us, event | category | flops | bytes accessed | tf_op | source)
XLA Modules:
  0.0 200.5 jit_solution(9149117536314124438)
XLA Ops:
  0.0 0.5 collective-permute-start.1
  0.5 1.4 slice.59
  1.9 0.0 copy-start.11
  1.9 0.0 copy-start.12
  1.9 0.0 copy-start.9
  1.9 0.0 copy-start.10
  1.9 2.6 %collective-permute-start.3 = (bf16[256,2560]{1,0:T(8,128)(2,1)S(1)}, bf16[256,2560]{1,0:T(8,128)(2,1)S(1)}, u32[]{:S(2)}, u32[]{:S(2)}) collective-permute-start(bf16[256,2560]{1,0:T(8,128)(2,1)S(1)} %slice.59), channel_id=1, source_target_pairs={{0,16},{8,24},{16,0},{24,8},{1,17},{9,25},{17,1},{25,9},{2,18},{10... | collective-permute-start | bytes 3932168 | tf_op jit(solution)/shard_map/ppermute | solution.py:209
  4.5 4.3 %slice.66 = bf16[256,7680]{1,0:T(8,128)(2,1)} slice(bf16[256,16384]{1,0:T(8,128)(2,1)} %gamma_ref), slice={[0:256], [2560:10240]} | slice | bytes 7864320 | tf_op jit(solution)/shard_map/slice | solution.py:227
  8.8 0.0 collective-permute-start.5
  8.8 0.2 copy.29.own_scaling_ref.refs_2_.scaling_ref
  9.0 0.3 collective-permute-start.2
  9.3 0.2 slice.63
  9.5 24.6 %collective-permute-done.3.refs_4_ = bf16[256,2560]{1,0:T(8,128)(2,1)S(1)} collective-permute-done((bf16[256,2560]{1,0:T(8,128)(2,1)S(1)}, bf16[256,2560]{1,0:T(8,128)(2,1)S(1)}, u32[]{:S(2)}, u32[]{:S(2)}) %collective-permute-start.3) | collective-permute-done | bytes 1310752 | tf_op jit(solution)/shard_map/ppermute | solution.py:209
  34.1 0.0 copy-start
  34.1 3.8 %copy-done = bf16[256,16384]{1,0:T(8,128)(2,1)S(1)} copy-done((bf16[256,16384]{1,0:T(8,128)(2,1)S(1)}, bf16[256,16384]{1,0:T(8,128)(2,1)}, u32[]{:S(2)}) %copy-start) | copy-done | bytes 8388632
  38.0 22.5 %own_rows.1 = (f32[1024,256]{1,0:T(8,128)S(1)}, f32[512,256]{1,0:T(8,128)S(1)}) custom-call(bf16[512,16384]{1,0:T(8,128)(2,1)} %own_ref.3, bf16[512,16384]{1,0:T(8,128)(2,1)} %collective-permute-done.1.sibling_ref.refs_1_, f32[512,1]{1,0:T(8,128)S(1)} %copy.29.own_scaling_ref.refs_2_.scaling_ref, ...), custom_call_target="tpu_custom_call" | custom-call | tf_op jit(solution)/shard_map/own_rows/pallas_call | solution.py:64
  60.5 1.0 copy-done.7
  61.5 1.1 broadcast_in_dim.27
  62.6 6.3 %all-to-all-start = ((bf16[8,528,128]{2,1,0:T(8,128)(2,1)}), bf16[8,528,128]{2,1,0:T(8,128)(2,1)}, u32[]{:S(2)}, u32[]{:S(2)}) async-start(bf16[8,528,128]{2,1,0:T(8,128)(2,1)} %broadcast_in_dim.27), calls=%async_computation | async-start | bytes 2162688 | tf_op jit(solution)/shard_map/all_to_all | solution.py:243
  68.9 3.1 %slice.70 = bf16[256,4096]{1,0:T(8,128)(2,1)} slice(bf16[256,16384]{1,0:T(8,128)(2,1)} %gamma_ref), slice={[0:256], [10240:14336]} | slice | bytes 4194304 | tf_op jit(solution)/shard_map/slice | solution.py:227
  72.0 1.5 collective-permute-start.8
  73.5 21.7 %all-to-all-done = bf16[8,528,128]{2,1,0:T(8,128)(2,1)} async-done(((bf16[8,528,128]{2,1,0:T(8,128)(2,1)}), bf16[8,528,128]{2,1,0:T(8,128)(2,1)}, u32[]{:S(2)}, u32[]{:S(2)}) %all-to-all-start) | async-done | bytes 1081376 | tf_op jit(solution)/shard_map/all_to_all | solution.py:243
  95.2 2.4 %copy_bitcast_fusion = bf16[512,1024]{1,0:T(8,128)(2,1)} fusion(bf16[8,528,128]{2,1,0:T(8,128)(2,1)} %all-to-all-done), kind=kLoop, calls=%fused_computation | loop fusion | bytes 2097152 | tf_op jit(solution)/shard_map/reshape | solution.py:247
  97.6 2.1 %slice.60 = bf16[256,1536]{1,0:T(8,128)(2,1)} slice(bf16[256,16384]{1,0:T(8,128)(2,1)} %gamma_ref), slice={[0:256], [14336:15872]} | slice | bytes 1572864 | tf_op jit(solution)/shard_map/slice | solution.py:227
  99.7 1.5 collective-permute-start
  101.2 1.3 copy-done.6
  102.5 5.3 %moved.3.refs_5_ = f32[1024,256]{1,0:T(8,128)S(1)} custom-call(bf16[512,16384]{1,0:T(8,128)(2,1)} %own_ref.3, bf16[512,16384]{1,0:T(8,128)(2,1)} %collective-permute-done.1.sibling_ref.refs_1_, f32[512,1]{1,0:T(8,128)S(1)} %copy.29.own_scaling_ref.refs_2_.scaling_ref, f32[512,1]{1,0:T(8,128)S(1)} %collective-permute-done.2.sibling_scaling_ref.refs_3_.scaling_ref, ...), custom_call_target="tpu_custom_call" | custom-call | tf_op jit(solution)/shard_map/moved/pallas_call | solution.py:95
  107.9 10.6 %collective-permute-done.5.refs_4_ = bf16[256,7680]{1,0:T(8,128)(2,1)} collective-permute-done((bf16[256,7680]{1,0:T(8,128)(2,1)}, bf16[256,7680]{1,0:T(8,128)(2,1)}, u32[]{:S(2)}, u32[]{:S(2)}) %collective-permute-start.5) | collective-permute-done | bytes 3932192 | tf_op jit(solution)/shard_map/ppermute | solution.py:209
  118.5 15.0 %moved.4.refs_3_ = f32[1024,256]{1,0:T(8,128)S(1)} custom-call(bf16[512,16384]{1,0:T(8,128)(2,1)} %own_ref.3, bf16[512,16384]{1,0:T(8,128)(2,1)} %collective-permute-done.1.sibling_ref.refs_1_, f32[512,1]{1,0:T(8,128)S(1)} %copy.29.own_scaling_ref.refs_2_.scaling_ref, f32[512,1]{1,0:T(8,128)S(1)} %collective-permute-done.2.sibling_scaling_ref.refs_3_.scaling_ref, ...), custom_call_target="tpu_custom_call" | custom-call | tf_op jit(solution)/shard_map/moved/pallas_call | solution.py:95
  133.4 0.7 slice.79
  134.2 0.2 compare_convert_fusion
  134.4 1.4 constant_dynamic-update-slice_fusion.1
  135.8 1.4 constant_dynamic-update-slice_fusion
  137.2 0.1 constant_dynamic-slice_fusion.1
  137.4 1.1 early.1
  138.5 0.1 collective-permute-start.6
  138.6 1.5 collective-permute-done.6
  140.1 0.7 add.37
  140.9 6.3 %all-to-all-start.1 = ((f32[8,64,128]{2,1,0:T(8,128)}), f32[8,64,128]{2,1,0:T(8,128)}, u32[]{:S(2)}, u32[]{:S(2)}) async-start(f32[8,64,128]{2,1,0:T(8,128)} %bitcast.5), calls=%async_computation.1 | async-start | bytes 524288 | tf_op jit(solution)/shard_map/all_to_all | solution.py:256
  147.1 1.7 slice.69
  148.8 1.5 collective-permute-start.7
  150.3 1.9 slice.67.normals_ref
  152.2 1.9 slice.80.normals_ref
  154.0 9.2 %collective-permute-done.8.refs_4_ = bf16[256,4096]{1,0:T(8,128)(2,1)S(1)} collective-permute-done((bf16[256,4096]{1,0:T(8,128)(2,1)}, bf16[256,4096]{1,0:T(8,128)(2,1)S(1)}, u32[]{:S(2)}, u32[]{:S(2)}) %collective-permute-start.8) | collective-permute-done | bytes 2097184 | tf_op jit(solution)/shard_map/ppermute | solution.py:209
  163.3 1.3 copy-done.1
  164.6 1.6 copy-done.2
  166.2 5.7 %moved.5.start_ref = f32[1024,256]{1,0:T(8,128)S(1)} custom-call(bf16[512,16384]{1,0:T(8,128)(2,1)} %own_ref.3, bf16[512,16384]{1,0:T(8,128)(2,1)} %collective-permute-done.1.sibling_ref.refs_1_, f32[512,1]{1,0:T(8,128)S(1)} %copy.29.own_scaling_ref.refs_2_.scaling_ref, f32[512,1]{1,0:T(8,128)S(1)} %collective-permute-done.2.sibling_scaling_ref.refs_3_.scaling_ref, ...), custom_call_target="tpu_custom_call" | custom-call | tf_op jit(solution)/shard_map/moved/pallas_call | solution.py:95
  171.9 1.0 reduce_sum.9
  172.9 7.3 %collective-permute-done.gamma_ref = bf16[256,1536]{1,0:T(8,128)(2,1)} collective-permute-done((bf16[256,1536]{1,0:T(8,128)(2,1)}, bf16[256,1536]{1,0:T(8,128)(2,1)}, u32[]{:S(2)}, u32[]{:S(2)}) %collective-permute-start) | collective-permute-done | bytes 786464 | tf_op jit(solution)/shard_map/ppermute | solution.py:209
  180.3 5.3 %middle.1.start_ref = f32[1024,128]{1,0:T(8,128)S(1)} custom-call(bf16[512,16384]{1,0:T(8,128)(2,1)} %own_ref.3, bf16[512,16384]{1,0:T(8,128)(2,1)} %collective-permute-done.1.sibling_ref.refs_1_, f32[512,1]{1,0:T(8,128)S(1)} %copy.29.own_scaling_ref.refs_2_.scaling_ref, f32[512,1]{1,0:T(8,128)S(1)} %collective-permute-done.2.sibling_scaling_ref.refs_3_.scaling_ref, ...), custom_call_target="tpu_custom_call" | custom-call | tf_op jit(solution)/shard_map/middle/pallas_call | solution.py:156
  185.6 0.5 late.3
  186.2 0.1 collective-permute-start.9
  186.2 0.4 copy-done.4
  186.6 0.5 late.2
  187.2 0.4 collective-permute-done.9
  187.6 2.0 %collective-permute-start.10 = (bf16[2,64,128]{2,1,0:T(8,128)(2,1)S(1)}, bf16[2,64,128]{2,1,0:T(8,128)(2,1)S(1)}, u32[]{:S(2)}, u32[]{:S(2)}) collective-permute-start(bf16[2,64,128]{2,1,0:T(8,128)(2,1)S(1)} %get-tuple-element.33), channel_id=1, source_target_pairs={{0,1},{1,0},{2,3},{3,2},{4,5},{5,4},{6,7},{7,6},{8,9},{9,8},{10,11... | collective-permute-start | bytes 98312 | tf_op jit(solution)/shard_map/ppermute | solution.py:275
  189.7 1.5 collective-permute-start.12
  191.2 0.1 collective-permute-start.11
  191.3 0.4 collective-permute-done.10
  191.6 3.0 %collective-permute-done.12 = bf16[2,64,128]{2,1,0:T(8,128)(2,1)S(1)} collective-permute-done((bf16[2,64,128]{2,1,0:T(8,128)(2,1)S(1)}, bf16[2,64,128]{2,1,0:T(8,128)(2,1)S(1)}, u32[]{:S(2)}, u32[]{:S(2)}) %collective-permute-start.12) | collective-permute-done | bytes 32800 | tf_op jit(solution)/shard_map/ppermute | solution.py:275
  194.6 0.5 collective-permute-done.11
  195.1 2.7 %collective-permute-start.13 = (bf16[1,64,128]{2,1,0:T(8,128)(2,1)S(1)}, bf16[1,64,128]{2,1,0:T(8,128)(2,1)S(1)}, u32[]{:S(2)}, u32[]{:S(2)}) collective-permute-start(bf16[1,64,128]{2,1,0:T(8,128)(2,1)S(1)} %fusion.7), channel_id=1, source_target_pairs={{0,4},{1,5},{2,6},{3,7},{4,0},{5,1},{6,2},{7,3},{8,12},{9,13},{10,... | collective-permute-start | bytes 49160 | tf_op jit(solution)/shard_map/ppermute | solution.py:275
  197.8 2.1 %collective-permute-done.13 = bf16[1,64,128]{2,1,0:T(8,128)(2,1)S(1)} collective-permute-done((bf16[1,64,128]{2,1,0:T(8,128)(2,1)S(1)}, bf16[1,64,128]{2,1,0:T(8,128)(2,1)S(1)}, u32[]{:S(2)}, u32[]{:S(2)}) %collective-permute-start.13) | collective-permute-done | bytes 16416 | tf_op jit(solution)/shard_map/ppermute | solution.py:275
  199.8 0.6 fusion.6
  (35 shorter events, 0.2 us)
Async XLA Ops:
  0.0 34.1 %collective-permute-start.1 = (bf16[512,16384]{1,0:T(8,128)(2,1)}, bf16[512,16384]{1,0:T(8,128)(2,1)}, u32[]{:S(2)}, u32[]{:S(2)}) collective-permute-start(bf16[512,16384]{1,0:T(8,128)(2,1)} %own_ref.3), channel_id=1, source_target_pairs={{0,8},{8,0},{16,24},{24,16},{1,9},{9,1},{17,25},{25,17},{2,10},{10... | collective-permute-start | bytes 50331656 | tf_op jit(solution)/shard_map/ppermute | solution.py:205
  1.9 6.9 %copy-start.11 = (f32[512]{0:T(512)S(1)}, f32[512]{0:T(512)}, u32[]{:S(2)}) copy-start(f32[512]{0:T(512)} %param.7) | copy-start | bytes 6148
  1.9 6.9 %copy-start.12 = (s32[512]{0:T(512)S(1)}, s32[512]{0:T(512)}, u32[]{:S(2)}) copy-start(s32[512]{0:T(512)} %param.8) | copy-start | bytes 6148
  1.9 7.4 %copy-start.9 = (s32[16384]{0:T(1024)S(1)}, s32[16384]{0:T(1024)}, u32[]{:S(2)}) copy-start(s32[16384]{0:T(1024)} %param.11) | copy-start | bytes 196612
  1.9 7.6 %copy-start.10 = (bf16[16384]{0:T(1024)(128)(2,1)S(1)}, bf16[16384]{0:T(1024)(128)(2,1)}, u32[]{:S(2)}) copy-start(bf16[16384]{0:T(1024)(128)(2,1)} %param.10) | copy-start | bytes 98308
  1.9 32.2 %collective-permute-start.3 = (bf16[256,2560]{1,0:T(8,128)(2,1)S(1)}, bf16[256,2560]{1,0:T(8,128)(2,1)S(1)}, u32[]{:S(2)}, u32[]{:S(2)}) collective-permute-start(bf16[256,2560]{1,0:T(8,128)(2,1)S(1)} %slice.59), channel_id=1, source_target_pairs={{0,16},{8,24},{16,0},{24,8},{1,17},{9,25},{17,1},{25,9},{2,18},{10... | collective-permute-start | bytes 3932168 | tf_op jit(solution)/shard_map/ppermute | solution.py:209
  8.8 109.7 %collective-permute-start.5 = (bf16[256,7680]{1,0:T(8,128)(2,1)}, bf16[256,7680]{1,0:T(8,128)(2,1)}, u32[]{:S(2)}, u32[]{:S(2)}) collective-permute-start(bf16[256,7680]{1,0:T(8,128)(2,1)} %slice.66), channel_id=1, source_target_pairs={{0,16},{8,24},{16,0},{24,8},{1,17},{9,25},{17,1},{25,9},{2,18},{10... | collective-permute-start | bytes 11796488 | tf_op jit(solution)/shard_map/ppermute | solution.py:209
  9.0 25.1 %collective-permute-start.2 = (f32[512,1]{1,0:T(8,128)S(1)}, f32[512,1]{1,0:T(8,128)S(1)}, u32[]{:S(2)}, u32[]{:S(2)}) collective-permute-start(f32[512,1]{1,0:T(8,128)S(1)} %copy.29.own_scaling_ref.refs_2_.scaling_ref), channel_id=1, source_target_pairs={{0,8},{8,0},{16,24},{24,16},{1,9},{9,1},{17,25},{25,17},{2,10},{10... | collective-permute-start | bytes 6152 | tf_op jit(solution)/shard_map/ppermute | solution.py:205
  34.1 26.4 %copy-start.5 = (bf16[256,2560]{1,0:T(8,128)(2,1)}, bf16[256,2560]{1,0:T(8,128)(2,1)S(1)}, u32[]{:S(2)}) copy-start(bf16[256,2560]{1,0:T(8,128)(2,1)S(1)} %collective-permute-done.3.refs_4_) | copy-start | bytes 3932164
  34.1 3.9 %copy-start = (bf16[256,16384]{1,0:T(8,128)(2,1)S(1)}, bf16[256,16384]{1,0:T(8,128)(2,1)}, u32[]{:S(2)}) copy-start(bf16[256,16384]{1,0:T(8,128)(2,1)} %gamma_ref) | copy-start | bytes 25165828
  60.5 1.0 copy-start.7
  62.6 32.6 %all-to-all-start = ((bf16[8,528,128]{2,1,0:T(8,128)(2,1)}), bf16[8,528,128]{2,1,0:T(8,128)(2,1)}, u32[]{:S(2)}, u32[]{:S(2)}) async-start(bf16[8,528,128]{2,1,0:T(8,128)(2,1)} %broadcast_in_dim.27), calls=%async_computation | async-start | bytes 2162688 | tf_op jit(solution)/shard_map/all_to_all | solution.py:243
  72.0 91.3 %collective-permute-start.8 = (bf16[256,4096]{1,0:T(8,128)(2,1)}, bf16[256,4096]{1,0:T(8,128)(2,1)S(1)}, u32[]{:S(2)}, u32[]{:S(2)}) collective-permute-start(bf16[256,4096]{1,0:T(8,128)(2,1)} %slice.70), channel_id=1, source_target_pairs={{0,16},{8,24},{16,0},{24,8},{1,17},{9,25},{17,1},{25,9},{2,18},{10... | collective-permute-start | bytes 6291464 | tf_op jit(solution)/shard_map/ppermute | solution.py:209
  97.6 38.2 %collective-permute-start.4 = (bf16[512,1024]{1,0:T(8,128)(2,1)}, bf16[512,1024]{1,0:T(8,128)(2,1)}, u32[]{:S(2)}, u32[]{:S(2)}) collective-permute-start(bf16[512,1024]{1,0:T(8,128)(2,1)} %copy_bitcast_fusion), channel_id=1, source_target_pairs={{0,8},{8,0},{16,24},{24,16},{1,9},{9,1},{17,25},{25,17},{2,10},{10... | collective-permute-start | bytes 3145736 | tf_op jit(solution)/shard_map/ppermute | solution.py:205
  99.7 80.6 %collective-permute-start = (bf16[256,1536]{1,0:T(8,128)(2,1)}, bf16[256,1536]{1,0:T(8,128)(2,1)}, u32[]{:S(2)}, u32[]{:S(2)}) collective-permute-start(bf16[256,1536]{1,0:T(8,128)(2,1)} %slice.60), channel_id=1, source_target_pairs={{0,16},{8,24},{16,0},{24,8},{1,17},{9,25},{17,1},{25,9},{2,18},{10... | collective-permute-start | bytes 2359304 | tf_op jit(solution)/shard_map/ppermute | solution.py:209
  101.2 1.3 copy-start.6
  135.8 1.6 copy-start.8
  138.5 1.6 collective-permute-start.6
  140.9 31.1 %all-to-all-start.1 = ((f32[8,64,128]{2,1,0:T(8,128)}), f32[8,64,128]{2,1,0:T(8,128)}, u32[]{:S(2)}, u32[]{:S(2)}) async-start(f32[8,64,128]{2,1,0:T(8,128)} %bitcast.5), calls=%async_computation.1 | async-start | bytes 524288 | tf_op jit(solution)/shard_map/all_to_all | solution.py:256
  148.8 36.8 %collective-permute-start.7 = (bf16[256,512]{1,0:T(8,128)(2,1)}, bf16[256,512]{1,0:T(8,128)(2,1)S(1)}, u32[]{:S(2)}, u32[]{:S(2)}) collective-permute-start(bf16[256,512]{1,0:T(8,128)(2,1)} %slice.69), channel_id=1, source_target_pairs={{0,16},{8,24},{16,0},{24,8},{1,17},{9,25},{17,1},{25,9},{2,18},{10... | collective-permute-start | bytes 786440 | tf_op jit(solution)/shard_map/ppermute | solution.py:209
  163.3 1.3 copy-start.1
  164.6 1.6 copy-start.2
  172.9 12.7 %copy-start.3 = (bf16[512,512]{1,0:T(8,128)(2,1)S(1)}, bf16[512,512]{1,0:T(8,128)(2,1)}, u32[]{:S(2)}) copy-start(bf16[512,512]{1,0:T(8,128)(2,1)} %slice.80.normals_ref) | copy-start | bytes 1572868
  185.6 1.0 copy-start.4
  186.2 1.4 collective-permute-start.9
  187.6 4.0 %collective-permute-start.10 = (bf16[2,64,128]{2,1,0:T(8,128)(2,1)S(1)}, bf16[2,64,128]{2,1,0:T(8,128)(2,1)S(1)}, u32[]{:S(2)}, u32[]{:S(2)}) collective-permute-start(bf16[2,64,128]{2,1,0:T(8,128)(2,1)S(1)} %get-tuple-element.33), channel_id=1, source_target_pairs={{0,1},{1,0},{2,3},{3,2},{4,5},{5,4},{6,7},{7,6},{8,9},{9,8},{10,11... | collective-permute-start | bytes 98312 | tf_op jit(solution)/shard_map/ppermute | solution.py:275
  189.7 5.0 %collective-permute-start.12 = (bf16[2,64,128]{2,1,0:T(8,128)(2,1)S(1)}, bf16[2,64,128]{2,1,0:T(8,128)(2,1)S(1)}, u32[]{:S(2)}, u32[]{:S(2)}) collective-permute-start(bf16[2,64,128]{2,1,0:T(8,128)(2,1)S(1)} %get-tuple-element.34), channel_id=1, source_target_pairs={{0,3},{1,2},{2,1},{3,0},{4,7},{5,6},{6,5},{7,4},{8,11},{9,10},{10,... | collective-permute-start | bytes 98312 | tf_op jit(solution)/shard_map/ppermute | solution.py:275
  191.2 3.9 %collective-permute-start.11 = (bf16[2,64,128]{2,1,0:T(8,128)(2,1)S(1)}, bf16[2,64,128]{2,1,0:T(8,128)(2,1)S(1)}, u32[]{:S(2)}, u32[]{:S(2)}) collective-permute-start(bf16[2,64,128]{2,1,0:T(8,128)(2,1)S(1)} %get-tuple-element.35), channel_id=1, source_target_pairs={{0,2},{1,3},{2,0},{3,1},{4,6},{5,7},{6,4},{7,5},{8,10},{9,11},{10,... | collective-permute-start | bytes 98312 | tf_op jit(solution)/shard_map/ppermute | solution.py:275
  195.1 4.7 %collective-permute-start.13 = (bf16[1,64,128]{2,1,0:T(8,128)(2,1)S(1)}, bf16[1,64,128]{2,1,0:T(8,128)(2,1)S(1)}, u32[]{:S(2)}, u32[]{:S(2)}) collective-permute-start(bf16[1,64,128]{2,1,0:T(8,128)(2,1)S(1)} %fusion.7), channel_id=1, source_target_pairs={{0,4},{1,5},{2,6},{3,7},{4,0},{5,1},{6,2},{7,3},{8,12},{9,13},{10,... | collective-permute-start | bytes 49160 | tf_op jit(solution)/shard_map/ppermute | solution.py:275

commit v4 on v3

--- a/solution.py
+++ b/solution.py
@@ -151,7 +151,7 @@
 
 def middle_terms(own, sibling, own_scaling, sibling_scaling, gamma, first, start, window, hot):
     rows, (count, cols) = own.shape[0], gamma.shape
-    width = next(size for size in (256, 128) if cols % size == 0 and first % size == 0)
+    width = next(size for size in (512, 256, 128) if cols % size == 0 and first % size == 0)
     normals = pl.BlockSpec((rows, width), lambda j: (0, j + first // width))
     return call(
         middle_kernel,
@@ -226,9 +226,9 @@
     def chunk(index):
         return gamma_slab[:, starts[index] : starts[index + 1]]
 
+    first = chunk(0)
+    first, gamma_slab, normals = together((first, gamma_slab, normals))
     other = to_sibling(normals)
-    first = chunk(0)
-    first, gamma_slab = together((first, gamma_slab))
     arrived = [from_chips(first)] + [from_chips(chunk(index)) for index in range(1, len(PARTS))]
     gamma_slab, arrived[0] = together((gamma_slab, arrived[0]))
 

time: 202 us -> 202 us (level)
  transfers between devices with their start and end apart: 16 -> 16, of which waited for: 11 -> 12; matrix products, arithmetic and copies ran while one was open for 13% -> 12% of each run, Pallas kernels for 28% -> 27%
where the time goes in v4:
time: 202 us; the launch traced here: 200 us
  waiting for transfers between devices  82.7 us (41%)
  Pallas kernels  54.9 us (27%)
  local copies, waits for them, and re-layouts  33 us (16%)
  starting transfers between devices  26.7 us (13%)
  other arithmetic  2.64 us (1%)
    ppermute x5, waiting for transfers between devices, from_chips(): lax.ppermute(array, 'blk', [(i, (i + CORES * step) % n_blk) for i in rang...  53.1 us
    pallas_call x3, Pallas kernels, add_moved(): call(functools.partial(moved_kernel, start is not None), grid=(cols // wi...  26 us
    pallas_call x1, Pallas kernels, own_moved(): call(own_kernel, grid=(cols // width,), in_specs=[normals, normals, whole...  22.5 us
    all_to_all x1, waiting for transfers between devices, local(): lax.all_to_all(jnp.broadcast_to(packed, (n_grp,) + packed.shape), 'grp',...  21.6 us
    slice x5, local copies, waits for them, and re-layouts, chunk(): return gamma_slab[:, starts[index]:starts[index + 1]]  12.6 us
    unnamed x28, local copies, waits for them, and re-layouts  10.4 us
    ppermute x5, starting transfers between devices, from_chips(): lax.ppermute(array, 'blk', [(i, (i + CORES * step) % n_blk) for i in rang...  7.05 us
    all_to_all x1, starting transfers between devices, local(): early = lax.all_to_all(mine, 'grp', 0, 0, tiled=True).sum(0)  6.3 us
  transfers between devices with their start and end apart: 16, of which 12 were waited for; matrix products, arithmetic and copies ran while one was open for 12% of the time, Pallas kernels for 27%

profile of v4, /device:TPU:0, one launch (start us, length us, event | category | flops | bytes accessed | tf_op | source)
XLA Modules:
  0.0 200.2 jit_solution(15221694560083219759)
XLA Ops:
  0.0 1.4 slice.59
  1.4 0.0 copy-start.11
  1.4 0.0 copy-start.12
  1.4 0.0 copy-start.9
  1.4 0.0 copy-start.10
  1.5 0.5 collective-permute-start.1
  2.0 2.6 %collective-permute-start.3 = (bf16[256,2560]{1,0:T(8,128)(2,1)S(1)}, bf16[256,2560]{1,0:T(8,128)(2,1)S(1)}, u32[]{:S(2)}, u32[]{:S(2)}) collective-permute-start(bf16[256,2560]{1,0:T(8,128)(2,1)S(1)} %slice.59), channel_id=1, source_target_pairs={{0,16},{8,24},{16,0},{24,8},{1,17},{9,25},{17,1},{25,9},{2,18},{10... | collective-permute-start | bytes 3932168 | tf_op jit(solution)/shard_map/ppermute | solution.py:209
  4.5 4.3 %slice.66 = bf16[256,7680]{1,0:T(8,128)(2,1)} slice(bf16[256,16384]{1,0:T(8,128)(2,1)} %gamma_ref), slice={[0:256], [2560:10240]} | slice | bytes 7864320 | tf_op jit(solution)/shard_map/slice | solution.py:227
  8.8 0.0 collective-permute-start.5
  8.9 0.2 copy.29.own_scaling_ref.refs_2_.scaling_ref
  9.0 0.2 collective-permute-start.2
  9.3 0.2 slice.63
  9.5 24.7 %collective-permute-done.3.refs_4_ = bf16[256,2560]{1,0:T(8,128)(2,1)S(1)} collective-permute-done((bf16[256,2560]{1,0:T(8,128)(2,1)S(1)}, bf16[256,2560]{1,0:T(8,128)(2,1)S(1)}, u32[]{:S(2)}, u32[]{:S(2)}) %collective-permute-start.3) | collective-permute-done | bytes 1310752 | tf_op jit(solution)/shard_map/ppermute | solution.py:209
  34.2 0.0 copy-start
  34.2 3.8 %copy-done = bf16[256,16384]{1,0:T(8,128)(2,1)S(1)} copy-done((bf16[256,16384]{1,0:T(8,128)(2,1)S(1)}, bf16[256,16384]{1,0:T(8,128)(2,1)}, u32[]{:S(2)}) %copy-start) | copy-done | bytes 8388632
  38.0 22.5 %own_rows.1 = (f32[1024,256]{1,0:T(8,128)S(1)}, f32[512,256]{1,0:T(8,128)S(1)}) custom-call(bf16[512,16384]{1,0:T(8,128)(2,1)} %own_ref.1, bf16[512,16384]{1,0:T(8,128)(2,1)} %collective-permute-done.1.sibling_ref.refs_1_, f32[512,1]{1,0:T(8,128)S(1)} %copy.29.own_scaling_ref.refs_2_.scaling_ref, ...), custom_call_target="tpu_custom_call" | custom-call | tf_op jit(solution)/shard_map/own_rows/pallas_call | solution.py:64
  60.6 1.0 copy-done.7
  61.6 1.1 broadcast_in_dim.27
  62.7 6.3 %all-to-all-start = ((bf16[8,528,128]{2,1,0:T(8,128)(2,1)}), bf16[8,528,128]{2,1,0:T(8,128)(2,1)}, u32[]{:S(2)}, u32[]{:S(2)}) async-start(bf16[8,528,128]{2,1,0:T(8,128)(2,1)} %broadcast_in_dim.27), calls=%async_computation | async-start | bytes 2162688 | tf_op jit(solution)/shard_map/all_to_all | solution.py:243
  69.0 3.1 %slice.70 = bf16[256,4096]{1,0:T(8,128)(2,1)} slice(bf16[256,16384]{1,0:T(8,128)(2,1)} %gamma_ref), slice={[0:256], [10240:14336]} | slice | bytes 4194304 | tf_op jit(solution)/shard_map/slice | solution.py:227
  72.1 1.5 collective-permute-start.8
  73.6 21.6 %all-to-all-done = bf16[8,528,128]{2,1,0:T(8,128)(2,1)} async-done(((bf16[8,528,128]{2,1,0:T(8,128)(2,1)}), bf16[8,528,128]{2,1,0:T(8,128)(2,1)}, u32[]{:S(2)}, u32[]{:S(2)}) %all-to-all-start) | async-done | bytes 1081376 | tf_op jit(solution)/shard_map/all_to_all | solution.py:243
  95.1 2.4 %copy_bitcast_fusion = bf16[512,1024]{1,0:T(8,128)(2,1)} fusion(bf16[8,528,128]{2,1,0:T(8,128)(2,1)} %all-to-all-done), kind=kLoop, calls=%fused_computation | loop fusion | bytes 2097152 | tf_op jit(solution)/shard_map/reshape | solution.py:247
  97.5 2.1 %slice.60 = bf16[256,1536]{1,0:T(8,128)(2,1)} slice(bf16[256,16384]{1,0:T(8,128)(2,1)} %gamma_ref), slice={[0:256], [14336:15872]} | slice | bytes 1572864 | tf_op jit(solution)/shard_map/slice | solution.py:227
  99.6 1.5 collective-permute-start
  101.2 1.3 copy-done.6
  102.5 5.3 %moved.3.refs_5_ = f32[1024,256]{1,0:T(8,128)S(1)} custom-call(bf16[512,16384]{1,0:T(8,128)(2,1)} %own_ref.1, bf16[512,16384]{1,0:T(8,128)(2,1)} %collective-permute-done.1.sibling_ref.refs_1_, f32[512,1]{1,0:T(8,128)S(1)} %copy.29.own_scaling_ref.refs_2_.scaling_ref, f32[512,1]{1,0:T(8,128)S(1)} %collective-permute-done.2.sibling_scaling_ref.refs_3_.scaling_ref, ...), custom_call_target="tpu_custom_call" | custom-call | tf_op jit(solution)/shard_map/moved/pallas_call | solution.py:95
  107.8 10.7 %collective-permute-done.5.refs_4_ = bf16[256,7680]{1,0:T(8,128)(2,1)} collective-permute-done((bf16[256,7680]{1,0:T(8,128)(2,1)}, bf16[256,7680]{1,0:T(8,128)(2,1)}, u32[]{:S(2)}, u32[]{:S(2)}) %collective-permute-start.5) | collective-permute-done | bytes 3932192 | tf_op jit(solution)/shard_map/ppermute | solution.py:209
  118.5 15.0 %moved.4.refs_3_ = f32[1024,256]{1,0:T(8,128)S(1)} custom-call(bf16[512,16384]{1,0:T(8,128)(2,1)} %own_ref.1, bf16[512,16384]{1,0:T(8,128)(2,1)} %collective-permute-done.1.sibling_ref.refs_1_, f32[512,1]{1,0:T(8,128)S(1)} %copy.29.own_scaling_ref.refs_2_.scaling_ref, f32[512,1]{1,0:T(8,128)S(1)} %collective-permute-done.2.sibling_scaling_ref.refs_3_.scaling_ref, ...), custom_call_target="tpu_custom_call" | custom-call | tf_op jit(solution)/shard_map/moved/pallas_call | solution.py:95
  133.5 0.7 slice.79
  134.2 0.2 compare_convert_fusion
  134.5 1.4 constant_dynamic-update-slice_fusion.1
  135.9 1.4 constant_dynamic-update-slice_fusion
  137.3 0.1 constant_dynamic-slice_fusion.1
  137.4 1.1 early.1
  138.6 0.1 collective-permute-start.6
  138.7 1.5 collective-permute-done.6
  140.2 0.7 add.37
  140.9 6.3 %all-to-all-start.1 = ((f32[8,64,128]{2,1,0:T(8,128)}), f32[8,64,128]{2,1,0:T(8,128)}, u32[]{:S(2)}, u32[]{:S(2)}) async-start(f32[8,64,128]{2,1,0:T(8,128)} %bitcast.5), calls=%async_computation.1 | async-start | bytes 524288 | tf_op jit(solution)/shard_map/all_to_all | solution.py:256
  147.2 1.7 slice.69
  148.9 1.5 collective-permute-start.7
  150.4 1.9 slice.67.normals_ref
  152.3 1.9 slice.80.normals_ref
  154.1 9.2 %collective-permute-done.8.refs_4_ = bf16[256,4096]{1,0:T(8,128)(2,1)S(1)} collective-permute-done((bf16[256,4096]{1,0:T(8,128)(2,1)}, bf16[256,4096]{1,0:T(8,128)(2,1)S(1)}, u32[]{:S(2)}, u32[]{:S(2)}) %collective-permute-start.8) | collective-permute-done | bytes 2097184 | tf_op jit(solution)/shard_map/ppermute | solution.py:209
  163.4 1.3 copy-done.1
  164.7 1.6 copy-done.2
  166.3 5.7 %moved.5.start_ref = f32[1024,256]{1,0:T(8,128)S(1)} custom-call(bf16[512,16384]{1,0:T(8,128)(2,1)} %own_ref.1, bf16[512,16384]{1,0:T(8,128)(2,1)} %collective-permute-done.1.sibling_ref.refs_1_, f32[512,1]{1,0:T(8,128)S(1)} %copy.29.own_scaling_ref.refs_2_.scaling_ref, f32[512,1]{1,0:T(8,128)S(1)} %collective-permute-done.2.sibling_scaling_ref.refs_3_.scaling_ref, ...), custom_call_target="tpu_custom_call" | custom-call | tf_op jit(solution)/shard_map/moved/pallas_call | solution.py:95
  172.0 1.0 reduce_sum.9
  173.0 7.4 %collective-permute-done.gamma_ref = bf16[256,1536]{1,0:T(8,128)(2,1)} collective-permute-done((bf16[256,1536]{1,0:T(8,128)(2,1)}, bf16[256,1536]{1,0:T(8,128)(2,1)}, u32[]{:S(2)}, u32[]{:S(2)}) %collective-permute-start) | collective-permute-done | bytes 786464 | tf_op jit(solution)/shard_map/ppermute | solution.py:209
  180.3 4.1 %middle.1.start_ref = f32[1024,128]{1,0:T(8,128)S(1)} custom-call(bf16[512,16384]{1,0:T(8,128)(2,1)} %own_ref.1, bf16[512,16384]{1,0:T(8,128)(2,1)} %collective-permute-done.1.sibling_ref.refs_1_, f32[512,1]{1,0:T(8,128)S(1)} %copy.29.own_scaling_ref.refs_2_.scaling_ref, f32[512,1]{1,0:T(8,128)S(1)} %collective-permute-done.2.sibling_scaling_ref.refs_3_.scaling_ref, ...), custom_call_target="tpu_custom_call" | custom-call | tf_op jit(solution)/shard_map/middle/pallas_call | solution.py:156
  184.5 1.1 collective-permute-done.7.gamma_ref
  185.6 0.5 late.3
  186.1 0.1 collective-permute-start.9
  186.2 0.5 late.2
  186.8 0.8 collective-permute-done.9
  187.6 1.9 collective-permute-start.10
  189.5 1.5 collective-permute-start.12
  191.0 0.2 collective-permute-start.11
  191.2 0.4 collective-permute-done.10
  191.6 2.8 %collective-permute-done.12 = bf16[2,64,128]{2,1,0:T(8,128)(2,1)S(1)} collective-permute-done((bf16[2,64,128]{2,1,0:T(8,128)(2,1)S(1)}, bf16[2,64,128]{2,1,0:T(8,128)(2,1)S(1)}, u32[]{:S(2)}, u32[]{:S(2)}) %collective-permute-start.12) | collective-permute-done | bytes 32800 | tf_op jit(solution)/shard_map/ppermute | solution.py:275
  194.4 0.5 collective-permute-done.11
  194.9 2.7 %collective-permute-start.13 = (bf16[1,64,128]{2,1,0:T(8,128)(2,1)S(1)}, bf16[1,64,128]{2,1,0:T(8,128)(2,1)S(1)}, u32[]{:S(2)}, u32[]{:S(2)}) collective-permute-start(bf16[1,64,128]{2,1,0:T(8,128)(2,1)S(1)} %fusion.7), channel_id=1, source_target_pairs={{0,4},{1,5},{2,6},{3,7},{4,0},{5,1},{6,2},{7,3},{8,12},{9,13},{10,... | collective-permute-start | bytes 49160 | tf_op jit(solution)/shard_map/ppermute | solution.py:275
  197.6 2.0 %collective-permute-done.13 = bf16[1,64,128]{2,1,0:T(8,128)(2,1)S(1)} collective-permute-done((bf16[1,64,128]{2,1,0:T(8,128)(2,1)S(1)}, bf16[1,64,128]{2,1,0:T(8,128)(2,1)S(1)}, u32[]{:S(2)}, u32[]{:S(2)}) %collective-permute-start.13) | collective-permute-done | bytes 16416 | tf_op jit(solution)/shard_map/ppermute | solution.py:275
  199.6 0.6 fusion.6
  (35 shorter events, 0.2 us)
Async XLA Ops:
  1.4 7.5 %copy-start.11 = (f32[512]{0:T(512)S(1)}, f32[512]{0:T(512)}, u32[]{:S(2)}) copy-start(f32[512]{0:T(512)} %param.7) | copy-start | bytes 6148
  1.4 7.5 %copy-start.12 = (s32[512]{0:T(512)S(1)}, s32[512]{0:T(512)}, u32[]{:S(2)}) copy-start(s32[512]{0:T(512)} %param.8) | copy-start | bytes 6148
  1.4 7.8 %copy-start.9 = (s32[16384]{0:T(1024)S(1)}, s32[16384]{0:T(1024)}, u32[]{:S(2)}) copy-start(s32[16384]{0:T(1024)} %param.11) | copy-start | bytes 196612
  1.4 8.0 %copy-start.10 = (bf16[16384]{0:T(1024)(128)(2,1)S(1)}, bf16[16384]{0:T(1024)(128)(2,1)}, u32[]{:S(2)}) copy-start(bf16[16384]{0:T(1024)(128)(2,1)} %param.10) | copy-start | bytes 98308
  1.5 32.7 %collective-permute-start.1 = (bf16[512,16384]{1,0:T(8,128)(2,1)}, bf16[512,16384]{1,0:T(8,128)(2,1)}, u32[]{:S(2)}, u32[]{:S(2)}) collective-permute-start(bf16[512,16384]{1,0:T(8,128)(2,1)} %own_ref.1), channel_id=1, source_target_pairs={{0,8},{8,0},{16,24},{24,16},{1,9},{9,1},{17,25},{25,17},{2,10},{10... | collective-permute-start | bytes 50331656 | tf_op jit(solution)/shard_map/ppermute | solution.py:205
  2.0 32.2 %collective-permute-start.3 = (bf16[256,2560]{1,0:T(8,128)(2,1)S(1)}, bf16[256,2560]{1,0:T(8,128)(2,1)S(1)}, u32[]{:S(2)}, u32[]{:S(2)}) collective-permute-start(bf16[256,2560]{1,0:T(8,128)(2,1)S(1)} %slice.59), channel_id=1, source_target_pairs={{0,16},{8,24},{16,0},{24,8},{1,17},{9,25},{17,1},{25,9},{2,18},{10... | collective-permute-start | bytes 3932168 | tf_op jit(solution)/shard_map/ppermute | solution.py:209
  8.8 109.7 %collective-permute-start.5 = (bf16[256,7680]{1,0:T(8,128)(2,1)}, bf16[256,7680]{1,0:T(8,128)(2,1)}, u32[]{:S(2)}, u32[]{:S(2)}) collective-permute-start(bf16[256,7680]{1,0:T(8,128)(2,1)} %slice.66), channel_id=1, source_target_pairs={{0,16},{8,24},{16,0},{24,8},{1,17},{9,25},{17,1},{25,9},{2,18},{10... | collective-permute-start | bytes 11796488 | tf_op jit(solution)/shard_map/ppermute | solution.py:209
  9.0 25.1 %collective-permute-start.2 = (f32[512,1]{1,0:T(8,128)S(1)}, f32[512,1]{1,0:T(8,128)S(1)}, u32[]{:S(2)}, u32[]{:S(2)}) collective-permute-start(f32[512,1]{1,0:T(8,128)S(1)} %copy.29.own_scaling_ref.refs_2_.scaling_ref), channel_id=1, source_target_pairs={{0,8},{8,0},{16,24},{24,16},{1,9},{9,1},{17,25},{25,17},{2,10},{10... | collective-permute-start | bytes 6152 | tf_op jit(solution)/shard_map/ppermute | solution.py:205
  34.2 26.4 %copy-start.5 = (bf16[256,2560]{1,0:T(8,128)(2,1)}, bf16[256,2560]{1,0:T(8,128)(2,1)S(1)}, u32[]{:S(2)}) copy-start(bf16[256,2560]{1,0:T(8,128)(2,1)S(1)} %collective-permute-done.3.refs_4_) | copy-start | bytes 3932164
  34.2 3.9 %copy-start = (bf16[256,16384]{1,0:T(8,128)(2,1)S(1)}, bf16[256,16384]{1,0:T(8,128)(2,1)}, u32[]{:S(2)}) copy-start(bf16[256,16384]{1,0:T(8,128)(2,1)} %gamma_ref) | copy-start | bytes 25165828
  60.5 1.0 copy-start.7
  62.7 32.4 %all-to-all-start = ((bf16[8,528,128]{2,1,0:T(8,128)(2,1)}), bf16[8,528,128]{2,1,0:T(8,128)(2,1)}, u32[]{:S(2)}, u32[]{:S(2)}) async-start(bf16[8,528,128]{2,1,0:T(8,128)(2,1)} %broadcast_in_dim.27), calls=%async_computation | async-start | bytes 2162688 | tf_op jit(solution)/shard_map/all_to_all | solution.py:243
  72.1 91.3 %collective-permute-start.8 = (bf16[256,4096]{1,0:T(8,128)(2,1)}, bf16[256,4096]{1,0:T(8,128)(2,1)S(1)}, u32[]{:S(2)}, u32[]{:S(2)}) collective-permute-start(bf16[256,4096]{1,0:T(8,128)(2,1)} %slice.70), channel_id=1, source_target_pairs={{0,16},{8,24},{16,0},{24,8},{1,17},{9,25},{17,1},{25,9},{2,18},{10... | collective-permute-start | bytes 6291464 | tf_op jit(solution)/shard_map/ppermute | solution.py:209
  97.5 38.4 %collective-permute-start.4 = (bf16[512,1024]{1,0:T(8,128)(2,1)}, bf16[512,1024]{1,0:T(8,128)(2,1)}, u32[]{:S(2)}, u32[]{:S(2)}) collective-permute-start(bf16[512,1024]{1,0:T(8,128)(2,1)} %copy_bitcast_fusion), channel_id=1, source_target_pairs={{0,8},{8,0},{16,24},{24,16},{1,9},{9,1},{17,25},{25,17},{2,10},{10... | collective-permute-start | bytes 3145736 | tf_op jit(solution)/shard_map/ppermute | solution.py:205
  99.6 80.7 %collective-permute-start = (bf16[256,1536]{1,0:T(8,128)(2,1)}, bf16[256,1536]{1,0:T(8,128)(2,1)}, u32[]{:S(2)}, u32[]{:S(2)}) collective-permute-start(bf16[256,1536]{1,0:T(8,128)(2,1)} %slice.60), channel_id=1, source_target_pairs={{0,16},{8,24},{16,0},{24,8},{1,17},{9,25},{17,1},{25,9},{2,18},{10... | collective-permute-start | bytes 2359304 | tf_op jit(solution)/shard_map/ppermute | solution.py:209
  101.1 1.3 copy-start.6
  135.9 1.6 copy-start.8
  138.6 1.6 collective-permute-start.6
  140.9 31.1 %all-to-all-start.1 = ((f32[8,64,128]{2,1,0:T(8,128)}), f32[8,64,128]{2,1,0:T(8,128)}, u32[]{:S(2)}, u32[]{:S(2)}) async-start(f32[8,64,128]{2,1,0:T(8,128)} %bitcast.5), calls=%async_computation.1 | async-start | bytes 524288 | tf_op jit(solution)/shard_map/all_to_all | solution.py:256
  148.9 36.7 %collective-permute-start.7 = (bf16[256,512]{1,0:T(8,128)(2,1)}, bf16[256,512]{1,0:T(8,128)(2,1)S(1)}, u32[]{:S(2)}, u32[]{:S(2)}) collective-permute-start(bf16[256,512]{1,0:T(8,128)(2,1)} %slice.69), channel_id=1, source_target_pairs={{0,16},{8,24},{16,0},{24,8},{1,17},{9,25},{17,1},{25,9},{2,18},{10... | collective-permute-start | bytes 786440 | tf_op jit(solution)/shard_map/ppermute | solution.py:209
  163.4 1.3 copy-start.1
  164.7 1.6 copy-start.2
  173.0 12.6 %copy-start.3 = (bf16[512,512]{1,0:T(8,128)(2,1)S(1)}, bf16[512,512]{1,0:T(8,128)(2,1)}, u32[]{:S(2)}) copy-start(bf16[512,512]{1,0:T(8,128)(2,1)} %slice.80.normals_ref) | copy-start | bytes 1572868
  184.5 1.7 copy-start.4
  186.1 1.4 collective-permute-start.9
  187.6 4.0 %collective-permute-start.10 = (bf16[2,64,128]{2,1,0:T(8,128)(2,1)S(1)}, bf16[2,64,128]{2,1,0:T(8,128)(2,1)S(1)}, u32[]{:S(2)}, u32[]{:S(2)}) collective-permute-start(bf16[2,64,128]{2,1,0:T(8,128)(2,1)S(1)} %get-tuple-element.35), channel_id=1, source_target_pairs={{0,1},{1,0},{2,3},{3,2},{4,5},{5,4},{6,7},{7,6},{8,9},{9,8},{10,11... | collective-permute-start | bytes 98312 | tf_op jit(solution)/shard_map/ppermute | solution.py:275
  189.5 5.0 %collective-permute-start.12 = (bf16[2,64,128]{2,1,0:T(8,128)(2,1)S(1)}, bf16[2,64,128]{2,1,0:T(8,128)(2,1)S(1)}, u32[]{:S(2)}, u32[]{:S(2)}) collective-permute-start(bf16[2,64,128]{2,1,0:T(8,128)(2,1)S(1)} %get-tuple-element.36), channel_id=1, source_target_pairs={{0,3},{1,2},{2,1},{3,0},{4,7},{5,6},{6,5},{7,4},{8,11},{9,10},{10,... | collective-permute-start | bytes 98312 | tf_op jit(solution)/shard_map/ppermute | solution.py:275
  191.0 3.9 %collective-permute-start.11 = (bf16[2,64,128]{2,1,0:T(8,128)(2,1)S(1)}, bf16[2,64,128]{2,1,0:T(8,128)(2,1)S(1)}, u32[]{:S(2)}, u32[]{:S(2)}) collective-permute-start(bf16[2,64,128]{2,1,0:T(8,128)(2,1)S(1)} %get-tuple-element.37), channel_id=1, source_target_pairs={{0,2},{1,3},{2,0},{3,1},{4,6},{5,7},{6,4},{7,5},{8,10},{9,11},{10,... | collective-permute-start | bytes 98312 | tf_op jit(solution)/shard_map/ppermute | solution.py:275
  194.9 4.7 %collective-permute-start.13 = (bf16[1,64,128]{2,1,0:T(8,128)(2,1)S(1)}, bf16[1,64,128]{2,1,0:T(8,128)(2,1)S(1)}, u32[]{:S(2)}, u32[]{:S(2)}) collective-permute-start(bf16[1,64,128]{2,1,0:T(8,128)(2,1)S(1)} %fusion.7), channel_id=1, source_target_pairs={{0,4},{1,5},{2,6},{3,7},{4,0},{5,1},{6,2},{7,3},{8,12},{9,13},{10,... | collective-permute-start | bytes 49160 | tf_op jit(solution)/shard_map/ppermute | solution.py:275

commit v5 on v4

--- a/solution.py
+++ b/solution.py
@@ -166,29 +166,58 @@
     )(own, sibling, own_scaling, sibling_scaling, gamma, start, window, hot)
 
 
-def late_kernel(blocks, first, grp_ref, normals_ref, scaling_ref, gamma_ref, start_ref, window_ref, hot_ref, out_ref, terms_ref):
-    half = normals_ref.shape[0]
-    place = slice(first, first + half)
-    moved = dot_t(scaled(normals_ref, scaling_ref), gamma_ref[...])
-    terms_ref[...] = start_ref[place] + by_desk(moved, window_ref[place], hot_ref[...], 1)
+def turns(block, width):
+    return (int(block % width != 0) + (block // width).bit_count()) % 2 == 1
+
+
+def late_kernel(
+    blocks,
+    width,
+    for_sibling,
+    grp_ref,
+    own_ref,
+    sibling_ref,
+    own_scaling_ref,
+    sibling_scaling_ref,
+    gamma_ref,
+    start_ref,
+    window_ref,
+    hot_ref,
+    out_ref,
+    shocks_ref,
+    weights_ref,
+):
+    half = own_ref.shape[0]
     height = half // blocks
+    places = []
     for index in range(blocks):
         source = pl.multiple_of((index ^ grp_ref[0]) * height, height)
-        out_ref[index * height : (index + 1) * height, :] = terms_ref[pl.ds(source, height), :].astype(out_ref.dtype)
-
-
-def late_terms(grp, blocks, side, kind, normals, scaling, gamma, start, window, hot):
-    rows = normals.shape[0]
+        here, there = pl.ds(index * height, height), pl.ds(source, height)
+        if for_sibling != turns(index, width):
+            normals, scaling, both = sibling_ref[there, :], sibling_scaling_ref[there, :], pl.ds(half + source, height)
+        else:
+            normals, scaling, both = own_ref[there, :], own_scaling_ref[there, :], there
+        shocks_ref[here, :] = (normals.astype(F32) * scaling).astype(BF16)
+        weights_ref[here, :] = window_ref[both, :]
+        places.append((here, both))
+    sums = by_desk(dot_t(shocks_ref[...], gamma_ref[...]), weights_ref[...], hot_ref[...], 1)
+    for index, (here, both) in enumerate(places):
+        block = sums[index * height : (index + 1) * height] + start_ref[both, :]
+        out_ref[here, :] = block.astype(out_ref.dtype)
+
+
+def late_terms(grp, blocks, width, for_sibling, own, sibling, own_scaling, sibling_scaling, gamma, start, window, hot):
+    rows, cols = own.shape
     in_vmem = pl.BlockSpec(memory_space=pltpu.VMEM)
     return pl.pallas_call(
-        functools.partial(late_kernel, blocks, side * rows),
-        in_specs=[pl.BlockSpec(memory_space=pltpu.SMEM)] + [in_vmem] * 6,
+        functools.partial(late_kernel, blocks, width, for_sibling),
+        in_specs=[pl.BlockSpec(memory_space=pltpu.SMEM)] + [in_vmem] * 8,
         out_specs=in_vmem,
-        scratch_shapes=[pltpu.VMEM((rows, DESKS), F32)],
-        out_shape=jax.ShapeDtypeStruct((rows, DESKS), kind),
+        scratch_shapes=[pltpu.VMEM((rows, cols), BF16), pltpu.VMEM((rows, window.shape[1]), BF16)],
+        out_shape=jax.ShapeDtypeStruct((rows, DESKS), BF16 if for_sibling else F32),
         compiler_params=pltpu.CompilerParams(vmem_limit_bytes=12 * 2**20),
         name="late",
-    )(grp[None], normals, scaling, gamma, start, window, hot)
+    )(grp[None], own, sibling, own_scaling, sibling_scaling, gamma, start, window, hot)
 
 
 def local(n_blk, n_grp, normals, mean_square, freedom_degrees, gamma_slab, deltas, desk_map):
@@ -261,18 +290,21 @@
     ready = (arrived[last - 1], early, normals[:, starts[last] :], other[:, starts[last] :])
     next_to_last, early, own_end, other_end = together(ready)
     terms = middle_terms(*sides, next_to_last, starts[last - 1], moved, other_window, other_hot)
-    rest = (arrived[last], terms, other_window, other_hot)
-    theirs = late_terms(grp, n_grp, 1, BF16, other_end, sides[3], *rest)
-    mine = late_terms(grp, n_grp, 0, F32, own_end, sides[2], *rest)
+    width = min(4, n_grp)
+    rest = (own_end, other_end, *sides[2:], arrived[last], terms, other_window, other_hot)
+    theirs = late_terms(grp, n_grp, width, True, *rest)
+    mine = late_terms(grp, n_grp, width, False, *rest)
     late = mine + to_sibling(theirs).astype(F32)
     late = late.reshape(n_grp, block, DESKS)
-    bit, width = 1, min(4, n_grp)
+    bit = 1
     while bit < n_grp:
         parts = late.reshape(late.shape[0] // width, width, block, DESKS)
         late = parts[:, 0]
         for step in range(1, width):
-            pairs = [(i, i ^ (step * bit)) for i in range(n_grp)]
-            late = late + lax.ppermute(parts[:, step].astype(BF16), "grp", pairs).astype(F32)
+            pairs = [
+                (i * n_grp + j, (i ^ 1) * n_grp + (j ^ (step * bit))) for i in range(n_blk) for j in range(n_grp)
+            ]
+            late = late + lax.ppermute(parts[:, step].astype(BF16), ("blk", "grp"), pairs).astype(F32)
         bit, width = bit * width, 2
     return early + late[0]
 

time: 202 us -> 200 us (0.990)
  local copies, waits for them, and re-layouts: 33 us -> 23.6 us
  waiting for transfers between devices: 82.7 us -> 91 us
    ppermute x5, waiting for transfers between devices: 53.1 us -> 62.3 us  [from_chips(): lax.ppermute(array, 'blk', [(i, (i + CORES * step) % n_blk) for i in rang...]
    unnamed x28 -> x16, local copies, waits for them, and re-layouts: 10.4 us -> 4.52 us
  transfers between devices with their start and end apart: 16 -> 16, of which waited for: 12 -> 12; matrix products, arithmetic and copies ran while one was open for 12% -> 10% of each run, Pallas kernels for 27% -> 27%
where the time goes in v5:
time: 200 us; the launch traced here: 199 us
  waiting for transfers between devices  91 us (46%)
  Pallas kernels  55.1 us (28%)
  starting transfers between devices  26.1 us (13%)
  local copies, waits for them, and re-layouts  23.6 us (12%)
  other arithmetic  2.62 us (1%)
    ppermute x5, waiting for transfers between devices, from_chips(): lax.ppermute(array, 'blk', [(i, (i + CORES * step) % n_blk) for i in rang...  62.3 us
    pallas_call x3, Pallas kernels, add_moved(): call(functools.partial(moved_kernel, start is not None), grid=(cols // wi...  26.3 us
    pallas_call x1, Pallas kernels, own_moved(): call(own_kernel, grid=(cols // width,), in_specs=[normals, normals, whole...  22.5 us
    all_to_all x1, waiting for transfers between devices, local(): lax.all_to_all(jnp.broadcast_to(packed, (n_grp,) + packed.shape), 'grp',...  21.4 us
    slice x5, local copies, waits for them, and re-layouts, chunk(): return gamma_slab[:, starts[index]:starts[index + 1]]  12.7 us
    ppermute x5, starting transfers between devices, from_chips(): lax.ppermute(array, 'blk', [(i, (i + CORES * step) % n_blk) for i in rang...  7.06 us
    all_to_all x1, starting transfers between devices, local(): early = lax.all_to_all(mine, 'grp', 0, 0, tiled=True).sum(0)  6.3 us
    all_to_all x1, starting transfers between devices, local(): lax.all_to_all(jnp.broadcast_to(packed, (n_grp,) + packed.shape), 'grp',...  6.3 us
  transfers between devices with their start and end apart: 16, of which 12 were waited for; matrix products, arithmetic and copies ran while one was open for 10% of the time, Pallas kernels for 27%

profile of v5, /device:TPU:0, one launch (start us, length us, event | category | flops | bytes accessed | tf_op | source)
XLA Modules:
  0.0 198.8 jit_solution(3476578799762599801)
XLA Ops:
  0.0 1.4 slice.59
  1.4 0.0 copy-start.5
  1.4 0.0 copy-start.6
  1.4 0.0 copy-start.3
  1.4 0.0 copy-start.4
  1.5 0.5 collective-permute-start.1
  2.0 2.6 %collective-permute-start.3 = (bf16[256,2560]{1,0:T(8,128)(2,1)S(1)}, bf16[256,2560]{1,0:T(8,128)(2,1)S(1)}, u32[]{:S(2)}, u32[]{:S(2)}) collective-permute-start(bf16[256,2560]{1,0:T(8,128)(2,1)S(1)} %slice.59), channel_id=1, source_target_pairs={{0,16},{8,24},{16,0},{24,8},{1,17},{9,25},{17,1},{25,9},{2,18},{10... | collective-permute-start | bytes 3932168 | tf_op jit(solution)/shard_map/ppermute | solution.py:238
  4.5 4.4 %slice.66 = bf16[256,7680]{1,0:T(8,128)(2,1)} slice(bf16[256,16384]{1,0:T(8,128)(2,1)} %gamma_ref), slice={[0:256], [2560:10240]} | slice | bytes 7864320 | tf_op jit(solution)/shard_map/slice | solution.py:256
  8.9 0.0 collective-permute-start.5
  8.9 0.2 copy.31.own_scaling_ref.refs_2_
  9.1 0.2 collective-permute-start.2
  9.3 0.2 slice.63
  9.6 24.6 %collective-permute-done.3.refs_4_ = bf16[256,2560]{1,0:T(8,128)(2,1)S(1)} collective-permute-done((bf16[256,2560]{1,0:T(8,128)(2,1)S(1)}, bf16[256,2560]{1,0:T(8,128)(2,1)S(1)}, u32[]{:S(2)}, u32[]{:S(2)}) %collective-permute-start.3) | collective-permute-done | bytes 1310752 | tf_op jit(solution)/shard_map/ppermute | solution.py:238
  34.2 0.0 collective-permute-done.2.sibling_scaling_ref.refs_3_
  34.2 0.0 collective-permute-done.1.sibling_ref.refs_1_
  34.2 3.4 %copy-done = bf16[256,16384]{1,0:T(8,128)(2,1)S(1)} copy-done((bf16[256,16384]{1,0:T(8,128)(2,1)S(1)}, bf16[256,16384]{1,0:T(8,128)(2,1)}, u32[]{:S(2)}) %copy-start) | copy-done | bytes 8388632
  37.6 22.5 %own_rows.1 = (f32[1024,256]{1,0:T(8,128)S(1)}, f32[512,256]{1,0:T(8,128)S(1)}) custom-call(bf16[512,16384]{1,0:T(8,128)(2,1)} %own_ref.1, bf16[512,16384]{1,0:T(8,128)(2,1)} %collective-permute-done.1.sibling_ref.refs_1_, f32[512,1]{1,0:T(8,128)S(1)} %copy.31.own_scaling_ref.refs_2_, f32[512,1]{1,0:T(8,128)S(1)} %collective-permute-done.2.sibling_scaling_ref.refs_3_, ...), custom_call_target="tpu_custom_call" | custom-call | tf_op jit(solution)/shard_map/own_rows/pallas_call | solution.py:64
  60.1 1.0 copy-done.1
  61.1 1.2 broadcast_in_dim.27
  62.3 6.3 %all-to-all-start = ((bf16[8,528,128]{2,1,0:T(8,128)(2,1)}), bf16[8,528,128]{2,1,0:T(8,128)(2,1)S(1)}, u32[]{:S(2)}, u32[]{:S(2)}) async-start(bf16[8,528,128]{2,1,0:T(8,128)(2,1)} %broadcast_in_dim.27), calls=%async_computation | async-start | bytes 2162688 | tf_op jit(solution)/shard_map/all_to_all | solution.py:272
  68.6 3.1 %slice.70 = bf16[256,4096]{1,0:T(8,128)(2,1)} slice(bf16[256,16384]{1,0:T(8,128)(2,1)} %gamma_ref), slice={[0:256], [10240:14336]} | slice | bytes 4194304 | tf_op jit(solution)/shard_map/slice | solution.py:256
  71.7 1.5 collective-permute-start.8
  73.2 21.4 %all-to-all-done = bf16[8,528,128]{2,1,0:T(8,128)(2,1)S(1)} async-done(((bf16[8,528,128]{2,1,0:T(8,128)(2,1)}), bf16[8,528,128]{2,1,0:T(8,128)(2,1)S(1)}, u32[]{:S(2)}, u32[]{:S(2)}) %all-to-all-start) | async-done | bytes 1081376 | tf_op jit(solution)/shard_map/all_to_all | solution.py:272
  94.6 1.2 copy_bitcast_fusion
  95.7 0.0 collective-permute-start.4
  95.8 2.1 %slice.60 = bf16[256,1536]{1,0:T(8,128)(2,1)} slice(bf16[256,16384]{1,0:T(8,128)(2,1)} %gamma_ref), slice={[0:256], [14336:15872]} | slice | bytes 1572864 | tf_op jit(solution)/shard_map/slice | solution.py:256
  97.9 1.5 collective-permute-start
  99.4 5.3 %moved.3.refs_5_ = f32[1024,256]{1,0:T(8,128)S(1)} custom-call(bf16[512,16384]{1,0:T(8,128)(2,1)} %own_ref.1, bf16[512,16384]{1,0:T(8,128)(2,1)} %collective-permute-done.1.sibling_ref.refs_1_, f32[512,1]{1,0:T(8,128)S(1)} %copy.31.own_scaling_ref.refs_2_, f32[512,1]{1,0:T(8,128)S(1)} %collective-permute-done.2.sibling_scaling_ref.refs_3_, ...), custom_call_target="tpu_custom_call" | custom-call | tf_op jit(solution)/shard_map/moved/pallas_call | solution.py:95
  104.7 13.8 %collective-permute-done.5.refs_4_ = bf16[256,7680]{1,0:T(8,128)(2,1)} collective-permute-done((bf16[256,7680]{1,0:T(8,128)(2,1)}, bf16[256,7680]{1,0:T(8,128)(2,1)}, u32[]{:S(2)}, u32[]{:S(2)}) %collective-permute-start.5) | collective-permute-done | bytes 3932192 | tf_op jit(solution)/shard_map/ppermute | solution.py:238
  118.5 15.0 %moved.4.refs_3_ = f32[1024,256]{1,0:T(8,128)S(1)} custom-call(bf16[512,16384]{1,0:T(8,128)(2,1)} %own_ref.1, bf16[512,16384]{1,0:T(8,128)(2,1)} %collective-permute-done.1.sibling_ref.refs_1_, f32[512,1]{1,0:T(8,128)S(1)} %copy.31.own_scaling_ref.refs_2_, f32[512,1]{1,0:T(8,128)S(1)} %collective-permute-done.2.sibling_scaling_ref.refs_3_, ...), custom_call_target="tpu_custom_call" | custom-call | tf_op jit(solution)/shard_map/moved/pallas_call | solution.py:95
  133.5 0.2 compare_convert_fusion
  133.8 0.1 constant_dynamic-update-slice_fusion.1
  133.9 0.0 collective-permute-done.4
  133.9 1.4 constant_dynamic-update-slice_fusion
  135.3 0.1 constant_dynamic-slice_fusion.1
  135.5 1.1 early.1
  136.6 0.1 collective-permute-start.6
  136.7 1.5 collective-permute-done.6
  138.2 0.7 add.37
  139.0 6.3 %all-to-all-start.1 = ((f32[8,64,128]{2,1,0:T(8,128)}), f32[8,64,128]{2,1,0:T(8,128)}, u32[]{:S(2)}, u32[]{:S(2)}) async-start(f32[8,64,128]{2,1,0:T(8,128)} %bitcast.5), calls=%async_computation.1 | async-start | bytes 524288 | tf_op jit(solution)/shard_map/all_to_all | solution.py:285
  145.3 1.7 slice.69
  146.9 1.5 collective-permute-start.7
  148.4 1.1 slice.67.own_ref
  149.5 1.1 slice.80.sibling_ref
  150.6 12.9 %collective-permute-done.8.refs_4_ = bf16[256,4096]{1,0:T(8,128)(2,1)} collective-permute-done((bf16[256,4096]{1,0:T(8,128)(2,1)}, bf16[256,4096]{1,0:T(8,128)(2,1)}, u32[]{:S(2)}, u32[]{:S(2)}) %collective-permute-start.8) | collective-permute-done | bytes 2097184 | tf_op jit(solution)/shard_map/ppermute | solution.py:238
  163.5 6.0 %moved.5.start_ref = f32[1024,256]{1,0:T(8,128)S(1)} custom-call(bf16[512,16384]{1,0:T(8,128)(2,1)} %own_ref.1, bf16[512,16384]{1,0:T(8,128)(2,1)} %collective-permute-done.1.sibling_ref.refs_1_, f32[512,1]{1,0:T(8,128)S(1)} %copy.31.own_scaling_ref.refs_2_, f32[512,1]{1,0:T(8,128)S(1)} %collective-permute-done.2.sibling_scaling_ref.refs_3_, ...), custom_call_target="tpu_custom_call" | custom-call | tf_op jit(solution)/shard_map/moved/pallas_call | solution.py:95
  169.5 0.0 all-to-all-done.1
  169.5 1.0 reduce_sum.9
  170.5 9.9 %collective-permute-done.gamma_ref = bf16[256,1536]{1,0:T(8,128)(2,1)} collective-permute-done((bf16[256,1536]{1,0:T(8,128)(2,1)}, bf16[256,1536]{1,0:T(8,128)(2,1)}, u32[]{:S(2)}, u32[]{:S(2)}) %collective-permute-start) | collective-permute-done | bytes 786464 | tf_op jit(solution)/shard_map/ppermute | solution.py:238
  180.3 4.1 %middle.1.start_ref = f32[1024,128]{1,0:T(8,128)S(1)} custom-call(bf16[512,16384]{1,0:T(8,128)(2,1)} %own_ref.1, bf16[512,16384]{1,0:T(8,128)(2,1)} %collective-permute-done.1.sibling_ref.refs_1_, f32[512,1]{1,0:T(8,128)S(1)} %copy.31.own_scaling_ref.refs_2_, f32[512,1]{1,0:T(8,128)S(1)} %collective-permute-done.2.sibling_scaling_ref.refs_3_, ...), custom_call_target="tpu_custom_call" | custom-call | tf_op jit(solution)/shard_map/middle/pallas_call | solution.py:156
  184.5 1.1 collective-permute-done.7.gamma_ref
  185.6 0.5 late.3
  186.1 0.1 collective-permute-start.9
  186.2 0.5 late.2
  186.7 0.8 collective-permute-done.9
  187.6 1.6 collective-permute-start.10
  189.2 1.5 collective-permute-start.12
  190.7 0.1 collective-permute-start.11
  190.7 0.3 collective-permute-done.10
  191.0 2.4 %collective-permute-done.12 = bf16[2,64,128]{2,1,0:T(8,128)(2,1)S(1)} collective-permute-done((bf16[2,64,128]{2,1,0:T(8,128)(2,1)S(1)}, bf16[2,64,128]{2,1,0:T(8,128)(2,1)S(1)}, u32[]{:S(2)}, u32[]{:S(2)}) %collective-permute-start.12) | collective-permute-done | bytes 32800 | tf_op jit(solution)/shard_map/ppermute | solution.py:307
  193.4 0.6 collective-permute-done.11
  194.1 2.4 %collective-permute-start.13 = (bf16[1,64,128]{2,1,0:T(8,128)(2,1)S(1)}, bf16[1,64,128]{2,1,0:T(8,128)(2,1)S(1)}, u32[]{:S(2)}, u32[]{:S(2)}) collective-permute-start(bf16[1,64,128]{2,1,0:T(8,128)(2,1)S(1)} %fusion.7), channel_id=1, source_target_pairs={{0,12},{1,13},{2,14},{3,15},{4,8},{5,9},{6,10},{7,11},{8,4},{9,5},... | collective-permute-start | bytes 49160 | tf_op jit(solution)/shard_map/ppermute | solution.py:307
  196.5 1.7 collective-permute-done.13
  198.2 0.6 fusion.6
  (23 shorter events, 0.2 us)
Async XLA Ops:
  1.4 7.5 %copy-start.5 = (f32[512]{0:T(512)S(1)}, f32[512]{0:T(512)}, u32[]{:S(2)}) copy-start(f32[512]{0:T(512)} %param.7) | copy-start | bytes 6148
  1.4 7.5 %copy-start.6 = (s32[512]{0:T(512)S(1)}, s32[512]{0:T(512)}, u32[]{:S(2)}) copy-start(s32[512]{0:T(512)} %param.8) | copy-start | bytes 6148
  1.4 7.9 %copy-start.3 = (s32[16384]{0:T(1024)S(1)}, s32[16384]{0:T(1024)}, u32[]{:S(2)}) copy-start(s32[16384]{0:T(1024)} %param.11) | copy-start | bytes 196612
  1.4 8.1 %copy-start.4 = (bf16[16384]{0:T(1024)(128)(2,1)S(1)}, bf16[16384]{0:T(1024)(128)(2,1)}, u32[]{:S(2)}) copy-start(bf16[16384]{0:T(1024)(128)(2,1)} %param.10) | copy-start | bytes 98308
  1.5 32.7 %collective-permute-start.1 = (bf16[512,16384]{1,0:T(8,128)(2,1)}, bf16[512,16384]{1,0:T(8,128)(2,1)}, u32[]{:S(2)}, u32[]{:S(2)}) collective-permute-start(bf16[512,16384]{1,0:T(8,128)(2,1)} %own_ref.1), channel_id=1, source_target_pairs={{0,8},{8,0},{16,24},{24,16},{1,9},{9,1},{17,25},{25,17},{2,10},{10... | collective-permute-start | bytes 50331656 | tf_op jit(solution)/shard_map/ppermute | solution.py:234
  2.0 32.2 %collective-permute-start.3 = (bf16[256,2560]{1,0:T(8,128)(2,1)S(1)}, bf16[256,2560]{1,0:T(8,128)(2,1)S(1)}, u32[]{:S(2)}, u32[]{:S(2)}) collective-permute-start(bf16[256,2560]{1,0:T(8,128)(2,1)S(1)} %slice.59), channel_id=1, source_target_pairs={{0,16},{8,24},{16,0},{24,8},{1,17},{9,25},{17,1},{25,9},{2,18},{10... | collective-permute-start | bytes 3932168 | tf_op jit(solution)/shard_map/ppermute | solution.py:238
  8.9 109.6 %collective-permute-start.5 = (bf16[256,7680]{1,0:T(8,128)(2,1)}, bf16[256,7680]{1,0:T(8,128)(2,1)}, u32[]{:S(2)}, u32[]{:S(2)}) collective-permute-start(bf16[256,7680]{1,0:T(8,128)(2,1)} %slice.66), channel_id=1, source_target_pairs={{0,16},{8,24},{16,0},{24,8},{1,17},{9,25},{17,1},{25,9},{2,18},{10... | collective-permute-start | bytes 11796488 | tf_op jit(solution)/shard_map/ppermute | solution.py:238
  9.1 25.1 %collective-permute-start.2 = (f32[512,1]{1,0:T(8,128)S(1)}, f32[512,1]{1,0:T(8,128)S(1)}, u32[]{:S(2)}, u32[]{:S(2)}) collective-permute-start(f32[512,1]{1,0:T(8,128)S(1)} %copy.31.own_scaling_ref.refs_2_), channel_id=1, source_target_pairs={{0,8},{8,0},{16,24},{24,16},{1,9},{9,1},{17,25},{25,17},{2,10},{10... | collective-permute-start | bytes 6152 | tf_op jit(solution)/shard_map/ppermute | solution.py:234
  34.2 3.4 %copy-start = (bf16[256,16384]{1,0:T(8,128)(2,1)S(1)}, bf16[256,16384]{1,0:T(8,128)(2,1)}, u32[]{:S(2)}) copy-start(bf16[256,16384]{1,0:T(8,128)(2,1)} %gamma_ref) | copy-start | bytes 25165828
  60.1 1.0 copy-start.1
  62.3 32.3 %all-to-all-start = ((bf16[8,528,128]{2,1,0:T(8,128)(2,1)}), bf16[8,528,128]{2,1,0:T(8,128)(2,1)S(1)}, u32[]{:S(2)}, u32[]{:S(2)}) async-start(bf16[8,528,128]{2,1,0:T(8,128)(2,1)} %broadcast_in_dim.27), calls=%async_computation | async-start | bytes 2162688 | tf_op jit(solution)/shard_map/all_to_all | solution.py:272
  71.7 91.8 %collective-permute-start.8 = (bf16[256,4096]{1,0:T(8,128)(2,1)}, bf16[256,4096]{1,0:T(8,128)(2,1)}, u32[]{:S(2)}, u32[]{:S(2)}) collective-permute-start(bf16[256,4096]{1,0:T(8,128)(2,1)} %slice.70), channel_id=1, source_target_pairs={{0,16},{8,24},{16,0},{24,8},{1,17},{9,25},{17,1},{25,9},{2,18},{10... | collective-permute-start | bytes 6291464 | tf_op jit(solution)/shard_map/ppermute | solution.py:238
  95.7 38.2 %collective-permute-start.4 = (bf16[512,1024]{1,0:T(8,128)(2,1)}, bf16[512,1024]{1,0:T(8,128)(2,1)}, u32[]{:S(2)}, u32[]{:S(2)}) collective-permute-start(bf16[512,1024]{1,0:T(8,128)(2,1)} %copy_bitcast_fusion), channel_id=1, source_target_pairs={{0,8},{8,0},{16,24},{24,16},{1,9},{9,1},{17,25},{25,17},{2,10},{10... | collective-permute-start | bytes 3145736 | tf_op jit(solution)/shard_map/ppermute | solution.py:234
  97.9 82.5 %collective-permute-start = (bf16[256,1536]{1,0:T(8,128)(2,1)}, bf16[256,1536]{1,0:T(8,128)(2,1)}, u32[]{:S(2)}, u32[]{:S(2)}) collective-permute-start(bf16[256,1536]{1,0:T(8,128)(2,1)} %slice.60), channel_id=1, source_target_pairs={{0,16},{8,24},{16,0},{24,8},{1,17},{9,25},{17,1},{25,9},{2,18},{10... | collective-permute-start | bytes 2359304 | tf_op jit(solution)/shard_map/ppermute | solution.py:238
  133.9 1.6 copy-start.2
  136.6 1.6 collective-permute-start.6
  139.0 30.5 %all-to-all-start.1 = ((f32[8,64,128]{2,1,0:T(8,128)}), f32[8,64,128]{2,1,0:T(8,128)}, u32[]{:S(2)}, u32[]{:S(2)}) async-start(f32[8,64,128]{2,1,0:T(8,128)} %bitcast.5), calls=%async_computation.1 | async-start | bytes 524288 | tf_op jit(solution)/shard_map/all_to_all | solution.py:285
  146.9 38.7 %collective-permute-start.7 = (bf16[256,512]{1,0:T(8,128)(2,1)}, bf16[256,512]{1,0:T(8,128)(2,1)S(1)}, u32[]{:S(2)}, u32[]{:S(2)}) collective-permute-start(bf16[256,512]{1,0:T(8,128)(2,1)} %slice.69), channel_id=1, source_target_pairs={{0,16},{8,24},{16,0},{24,8},{1,17},{9,25},{17,1},{25,9},{2,18},{10... | collective-permute-start | bytes 786440 | tf_op jit(solution)/shard_map/ppermute | solution.py:238
  186.1 1.4 collective-permute-start.9
  187.6 3.4 %collective-permute-start.10 = (bf16[2,64,128]{2,1,0:T(8,128)(2,1)S(1)}, bf16[2,64,128]{2,1,0:T(8,128)(2,1)S(1)}, u32[]{:S(2)}, u32[]{:S(2)}) collective-permute-start(bf16[2,64,128]{2,1,0:T(8,128)(2,1)S(1)} %get-tuple-element.35), channel_id=1, source_target_pairs={{0,9},{1,8},{2,11},{3,10},{4,13},{5,12},{6,15},{7,14},{8,1},{9,0},... | collective-permute-start | bytes 98312 | tf_op jit(solution)/shard_map/ppermute | solution.py:307
  189.2 4.3 %collective-permute-start.12 = (bf16[2,64,128]{2,1,0:T(8,128)(2,1)S(1)}, bf16[2,64,128]{2,1,0:T(8,128)(2,1)S(1)}, u32[]{:S(2)}, u32[]{:S(2)}) collective-permute-start(bf16[2,64,128]{2,1,0:T(8,128)(2,1)S(1)} %get-tuple-element.36), channel_id=1, source_target_pairs={{0,11},{1,10},{2,9},{3,8},{4,15},{5,14},{6,13},{7,12},{8,3},{9,2},... | collective-permute-start | bytes 98312 | tf_op jit(solution)/shard_map/ppermute | solution.py:307
  190.7 3.3 %collective-permute-start.11 = (bf16[2,64,128]{2,1,0:T(8,128)(2,1)S(1)}, bf16[2,64,128]{2,1,0:T(8,128)(2,1)S(1)}, u32[]{:S(2)}, u32[]{:S(2)}) collective-permute-start(bf16[2,64,128]{2,1,0:T(8,128)(2,1)S(1)} %get-tuple-element.37), channel_id=1, source_target_pairs={{0,10},{1,11},{2,8},{3,9},{4,14},{5,15},{6,12},{7,13},{8,2},{9,3},... | collective-permute-start | bytes 98312 | tf_op jit(solution)/shard_map/ppermute | solution.py:307
  194.1 4.1 %collective-permute-start.13 = (bf16[1,64,128]{2,1,0:T(8,128)(2,1)S(1)}, bf16[1,64,128]{2,1,0:T(8,128)(2,1)S(1)}, u32[]{:S(2)}, u32[]{:S(2)}) collective-permute-start(bf16[1,64,128]{2,1,0:T(8,128)(2,1)S(1)} %fusion.7), channel_id=1, source_target_pairs={{0,12},{1,13},{2,14},{3,15},{4,8},{5,9},{6,10},{7,11},{8,4},{9,5},... | collective-permute-start | bytes 49160 | tf_op jit(solution)/shard_map/ppermute | solution.py:307

commit v6 on v5

--- a/solution.py
+++ b/solution.py
@@ -300,7 +300,7 @@
     while bit < n_grp:
         parts = late.reshape(late.shape[0] // width, width, block, DESKS)
         late = parts[:, 0]
-        for step in range(1, width):
+        for step in range(width - 1, 0, -1):
             pairs = [
                 (i * n_grp + j, (i ^ 1) * n_grp + (j ^ (step * bit))) for i in range(n_blk) for j in range(n_grp)
             ]

time: 200 us -> 200 us (level)
  no operation moved by 1% of the time
where the time goes in v6:
time: 200 us; the launch traced here: 199 us
  waiting for transfers between devices  91 us (46%)
  Pallas kernels  55.1 us (28%)
  starting transfers between devices  26.2 us (13%)
  local copies, waits for them, and re-layouts  23.6 us (12%)
  other arithmetic  2.62 us (1%)
    ppermute x5, waiting for transfers between devices, from_chips(): lax.ppermute(array, 'blk', [(i, (i + CORES * step) % n_blk) for i in rang...  62.3 us
    pallas_call x3, Pallas kernels, add_moved(): call(functools.partial(moved_kernel, start is not None), grid=(cols // wi...  26.3 us
    pallas_call x1, Pallas kernels, own_moved(): call(own_kernel, grid=(cols // width,), in_specs=[normals, normals, whole...  22.5 us
    all_to_all x1, waiting for transfers between devices, local(): lax.all_to_all(jnp.broadcast_to(packed, (n_grp,) + packed.shape), 'grp',...  21.4 us
    slice x5, local copies, waits for them, and re-layouts, chunk(): return gamma_slab[:, starts[index]:starts[index + 1]]  12.7 us
    ppermute x5, starting transfers between devices, from_chips(): lax.ppermute(array, 'blk', [(i, (i + CORES * step) % n_blk) for i in rang...  7.06 us
    all_to_all x1, starting transfers between devices, local(): early = lax.all_to_all(mine, 'grp', 0, 0, tiled=True).sum(0)  6.3 us
    all_to_all x1, starting transfers between devices, local(): lax.all_to_all(jnp.broadcast_to(packed, (n_grp,) + packed.shape), 'grp',...  6.3 us
  transfers between devices with their start and end apart: 16, of which 12 were waited for; matrix products, arithmetic and copies ran while one was open for 10% of the time, Pallas kernels for 27%

profile of v6, /device:TPU:0, one launch (start us, length us, event | category | flops | bytes accessed | tf_op | source)
XLA Modules:
  0.0 198.8 jit_solution(8422604018632146009)
XLA Ops:
  0.0 1.4 slice.59
  1.4 0.0 copy-start.5
  1.4 0.0 copy-start.6
  1.4 0.0 copy-start.3
  1.4 0.0 copy-start.4
  1.5 0.5 collective-permute-start.1
  2.0 2.6 %collective-permute-start.3 = (bf16[256,2560]{1,0:T(8,128)(2,1)S(1)}, bf16[256,2560]{1,0:T(8,128)(2,1)S(1)}, u32[]{:S(2)}, u32[]{:S(2)}) collective-permute-start(bf16[256,2560]{1,0:T(8,128)(2,1)S(1)} %slice.59), channel_id=1, source_target_pairs={{0,16},{8,24},{16,0},{24,8},{1,17},{9,25},{17,1},{25,9},{2,18},{10... | collective-permute-start | bytes 3932168 | tf_op jit(solution)/shard_map/ppermute | solution.py:238
  4.5 4.4 %slice.66 = bf16[256,7680]{1,0:T(8,128)(2,1)} slice(bf16[256,16384]{1,0:T(8,128)(2,1)} %gamma_ref), slice={[0:256], [2560:10240]} | slice | bytes 7864320 | tf_op jit(solution)/shard_map/slice | solution.py:256
  8.9 0.0 collective-permute-start.5
  8.9 0.2 copy.31.own_scaling_ref.refs_2_
  9.1 0.2 collective-permute-start.2
  9.3 0.2 slice.63
  9.6 24.6 %collective-permute-done.3.refs_4_ = bf16[256,2560]{1,0:T(8,128)(2,1)S(1)} collective-permute-done((bf16[256,2560]{1,0:T(8,128)(2,1)S(1)}, bf16[256,2560]{1,0:T(8,128)(2,1)S(1)}, u32[]{:S(2)}, u32[]{:S(2)}) %collective-permute-start.3) | collective-permute-done | bytes 1310752 | tf_op jit(solution)/shard_map/ppermute | solution.py:238
  34.2 0.0 collective-permute-done.2.sibling_scaling_ref.refs_3_
  34.2 0.0 collective-permute-done.1.sibling_ref.refs_1_
  34.2 3.4 %copy-done = bf16[256,16384]{1,0:T(8,128)(2,1)S(1)} copy-done((bf16[256,16384]{1,0:T(8,128)(2,1)S(1)}, bf16[256,16384]{1,0:T(8,128)(2,1)}, u32[]{:S(2)}) %copy-start) | copy-done | bytes 8388632
  37.6 22.5 %own_rows.1 = (f32[1024,256]{1,0:T(8,128)S(1)}, f32[512,256]{1,0:T(8,128)S(1)}) custom-call(bf16[512,16384]{1,0:T(8,128)(2,1)} %own_ref.1, bf16[512,16384]{1,0:T(8,128)(2,1)} %collective-permute-done.1.sibling_ref.refs_1_, f32[512,1]{1,0:T(8,128)S(1)} %copy.31.own_scaling_ref.refs_2_, f32[512,1]{1,0:T(8,128)S(1)} %collective-permute-done.2.sibling_scaling_ref.refs_3_, ...), custom_call_target="tpu_custom_call" | custom-call | tf_op jit(solution)/shard_map/own_rows/pallas_call | solution.py:64
  60.1 1.0 copy-done.1
  61.1 1.2 broadcast_in_dim.27
  62.3 6.3 %all-to-all-start = ((bf16[8,528,128]{2,1,0:T(8,128)(2,1)}), bf16[8,528,128]{2,1,0:T(8,128)(2,1)S(1)}, u32[]{:S(2)}, u32[]{:S(2)}) async-start(bf16[8,528,128]{2,1,0:T(8,128)(2,1)} %broadcast_in_dim.27), calls=%async_computation | async-start | bytes 2162688 | tf_op jit(solution)/shard_map/all_to_all | solution.py:272
  68.6 3.1 %slice.70 = bf16[256,4096]{1,0:T(8,128)(2,1)} slice(bf16[256,16384]{1,0:T(8,128)(2,1)} %gamma_ref), slice={[0:256], [10240:14336]} | slice | bytes 4194304 | tf_op jit(solution)/shard_map/slice | solution.py:256
  71.7 1.5 collective-permute-start.8
  73.2 21.4 %all-to-all-done = bf16[8,528,128]{2,1,0:T(8,128)(2,1)S(1)} async-done(((bf16[8,528,128]{2,1,0:T(8,128)(2,1)}), bf16[8,528,128]{2,1,0:T(8,128)(2,1)S(1)}, u32[]{:S(2)}, u32[]{:S(2)}) %all-to-all-start) | async-done | bytes 1081376 | tf_op jit(solution)/shard_map/all_to_all | solution.py:272
  94.6 1.2 copy_bitcast_fusion
  95.7 0.0 collective-permute-start.4
  95.8 2.1 %slice.60 = bf16[256,1536]{1,0:T(8,128)(2,1)} slice(bf16[256,16384]{1,0:T(8,128)(2,1)} %gamma_ref), slice={[0:256], [14336:15872]} | slice | bytes 1572864 | tf_op jit(solution)/shard_map/slice | solution.py:256
  97.9 1.5 collective-permute-start
  99.4 5.3 %moved.3.refs_5_ = f32[1024,256]{1,0:T(8,128)S(1)} custom-call(bf16[512,16384]{1,0:T(8,128)(2,1)} %own_ref.1, bf16[512,16384]{1,0:T(8,128)(2,1)} %collective-permute-done.1.sibling_ref.refs_1_, f32[512,1]{1,0:T(8,128)S(1)} %copy.31.own_scaling_ref.refs_2_, f32[512,1]{1,0:T(8,128)S(1)} %collective-permute-done.2.sibling_scaling_ref.refs_3_, ...), custom_call_target="tpu_custom_call" | custom-call | tf_op jit(solution)/shard_map/moved/pallas_call | solution.py:95
  104.7 13.8 %collective-permute-done.5.refs_4_ = bf16[256,7680]{1,0:T(8,128)(2,1)} collective-permute-done((bf16[256,7680]{1,0:T(8,128)(2,1)}, bf16[256,7680]{1,0:T(8,128)(2,1)}, u32[]{:S(2)}, u32[]{:S(2)}) %collective-permute-start.5) | collective-permute-done | bytes 3932192 | tf_op jit(solution)/shard_map/ppermute | solution.py:238
  118.5 15.0 %moved.4.refs_3_ = f32[1024,256]{1,0:T(8,128)S(1)} custom-call(bf16[512,16384]{1,0:T(8,128)(2,1)} %own_ref.1, bf16[512,16384]{1,0:T(8,128)(2,1)} %collective-permute-done.1.sibling_ref.refs_1_, f32[512,1]{1,0:T(8,128)S(1)} %copy.31.own_scaling_ref.refs_2_, f32[512,1]{1,0:T(8,128)S(1)} %collective-permute-done.2.sibling_scaling_ref.refs_3_, ...), custom_call_target="tpu_custom_call" | custom-call | tf_op jit(solution)/shard_map/moved/pallas_call | solution.py:95
  133.5 0.2 compare_convert_fusion
  133.8 0.1 constant_dynamic-update-slice_fusion.1
  133.9 0.0 collective-permute-done.4
  133.9 1.4 constant_dynamic-update-slice_fusion
  135.3 0.1 constant_dynamic-slice_fusion.1
  135.5 1.1 early.1
  136.6 0.1 collective-permute-start.6
  136.7 1.5 collective-permute-done.6
  138.2 0.7 add.37
  139.0 6.3 %all-to-all-start.1 = ((f32[8,64,128]{2,1,0:T(8,128)}), f32[8,64,128]{2,1,0:T(8,128)}, u32[]{:S(2)}, u32[]{:S(2)}) async-start(f32[8,64,128]{2,1,0:T(8,128)} %bitcast.5), calls=%async_computation.1 | async-start | bytes 524288 | tf_op jit(solution)/shard_map/all_to_all | solution.py:285
  145.3 1.7 slice.69
  146.9 1.5 collective-permute-start.7
  148.4 1.1 slice.67.own_ref
  149.5 1.1 slice.80.sibling_ref
  150.6 12.9 %collective-permute-done.8.refs_4_ = bf16[256,4096]{1,0:T(8,128)(2,1)} collective-permute-done((bf16[256,4096]{1,0:T(8,128)(2,1)}, bf16[256,4096]{1,0:T(8,128)(2,1)}, u32[]{:S(2)}, u32[]{:S(2)}) %collective-permute-start.8) | collective-permute-done | bytes 2097184 | tf_op jit(solution)/shard_map/ppermute | solution.py:238
  163.5 6.0 %moved.5.start_ref = f32[1024,256]{1,0:T(8,128)S(1)} custom-call(bf16[512,16384]{1,0:T(8,128)(2,1)} %own_ref.1, bf16[512,16384]{1,0:T(8,128)(2,1)} %collective-permute-done.1.sibling_ref.refs_1_, f32[512,1]{1,0:T(8,128)S(1)} %copy.31.own_scaling_ref.refs_2_, f32[512,1]{1,0:T(8,128)S(1)} %collective-permute-done.2.sibling_scaling_ref.refs_3_, ...), custom_call_target="tpu_custom_call" | custom-call | tf_op jit(solution)/shard_map/moved/pallas_call | solution.py:95
  169.5 0.0 all-to-all-done.1
  169.5 1.0 reduce_sum.9
  170.5 9.9 %collective-permute-done.gamma_ref = bf16[256,1536]{1,0:T(8,128)(2,1)} collective-permute-done((bf16[256,1536]{1,0:T(8,128)(2,1)}, bf16[256,1536]{1,0:T(8,128)(2,1)}, u32[]{:S(2)}, u32[]{:S(2)}) %collective-permute-start) | collective-permute-done | bytes 786464 | tf_op jit(solution)/shard_map/ppermute | solution.py:238
  180.3 4.1 %middle.1.start_ref = f32[1024,128]{1,0:T(8,128)S(1)} custom-call(bf16[512,16384]{1,0:T(8,128)(2,1)} %own_ref.1, bf16[512,16384]{1,0:T(8,128)(2,1)} %collective-permute-done.1.sibling_ref.refs_1_, f32[512,1]{1,0:T(8,128)S(1)} %copy.31.own_scaling_ref.refs_2_, f32[512,1]{1,0:T(8,128)S(1)} %collective-permute-done.2.sibling_scaling_ref.refs_3_, ...), custom_call_target="tpu_custom_call" | custom-call | tf_op jit(solution)/shard_map/middle/pallas_call | solution.py:156
  184.5 1.1 collective-permute-done.7.gamma_ref
  185.6 0.5 late.3
  186.1 0.1 collective-permute-start.9
  186.2 0.5 late.2
  186.7 0.8 collective-permute-done.9
  187.6 2.6 %collective-permute-start.10 = (bf16[2,64,128]{2,1,0:T(8,128)(2,1)S(1)}, bf16[2,64,128]{2,1,0:T(8,128)(2,1)S(1)}, u32[]{:S(2)}, u32[]{:S(2)}) collective-permute-start(bf16[2,64,128]{2,1,0:T(8,128)(2,1)S(1)} %get-tuple-element.35), channel_id=1, source_target_pairs={{0,11},{1,10},{2,9},{3,8},{4,15},{5,14},{6,13},{7,12},{8,3},{9,2},... | collective-permute-start | bytes 98312 | tf_op jit(solution)/shard_map/ppermute | solution.py:307
  190.2 0.5 collective-permute-start.12
  190.7 0.1 collective-permute-start.11
  190.8 1.1 collective-permute-done.10
  191.9 1.6 collective-permute-done.12
  193.6 0.5 collective-permute-done.11
  194.1 2.4 %collective-permute-start.13 = (bf16[1,64,128]{2,1,0:T(8,128)(2,1)S(1)}, bf16[1,64,128]{2,1,0:T(8,128)(2,1)S(1)}, u32[]{:S(2)}, u32[]{:S(2)}) collective-permute-start(bf16[1,64,128]{2,1,0:T(8,128)(2,1)S(1)} %fusion.7), channel_id=1, source_target_pairs={{0,12},{1,13},{2,14},{3,15},{4,8},{5,9},{6,10},{7,11},{8,4},{9,5},... | collective-permute-start | bytes 49160 | tf_op jit(solution)/shard_map/ppermute | solution.py:307
  196.5 1.7 collective-permute-done.13
  198.2 0.6 fusion.6
  (23 shorter events, 0.2 us)
Async XLA Ops:
  1.4 7.5 %copy-start.5 = (f32[512]{0:T(512)S(1)}, f32[512]{0:T(512)}, u32[]{:S(2)}) copy-start(f32[512]{0:T(512)} %param.7) | copy-start | bytes 6148
  1.4 7.5 %copy-start.6 = (s32[512]{0:T(512)S(1)}, s32[512]{0:T(512)}, u32[]{:S(2)}) copy-start(s32[512]{0:T(512)} %param.8) | copy-start | bytes 6148
  1.4 7.9 %copy-start.3 = (s32[16384]{0:T(1024)S(1)}, s32[16384]{0:T(1024)}, u32[]{:S(2)}) copy-start(s32[16384]{0:T(1024)} %param.11) | copy-start | bytes 196612
  1.4 8.1 %copy-start.4 = (bf16[16384]{0:T(1024)(128)(2,1)S(1)}, bf16[16384]{0:T(1024)(128)(2,1)}, u32[]{:S(2)}) copy-start(bf16[16384]{0:T(1024)(128)(2,1)} %param.10) | copy-start | bytes 98308
  1.5 32.7 %collective-permute-start.1 = (bf16[512,16384]{1,0:T(8,128)(2,1)}, bf16[512,16384]{1,0:T(8,128)(2,1)}, u32[]{:S(2)}, u32[]{:S(2)}) collective-permute-start(bf16[512,16384]{1,0:T(8,128)(2,1)} %own_ref.1), channel_id=1, source_target_pairs={{0,8},{8,0},{16,24},{24,16},{1,9},{9,1},{17,25},{25,17},{2,10},{10... | collective-permute-start | bytes 50331656 | tf_op jit(solution)/shard_map/ppermute | solution.py:234
  2.0 32.2 %collective-permute-start.3 = (bf16[256,2560]{1,0:T(8,128)(2,1)S(1)}, bf16[256,2560]{1,0:T(8,128)(2,1)S(1)}, u32[]{:S(2)}, u32[]{:S(2)}) collective-permute-start(bf16[256,2560]{1,0:T(8,128)(2,1)S(1)} %slice.59), channel_id=1, source_target_pairs={{0,16},{8,24},{16,0},{24,8},{1,17},{9,25},{17,1},{25,9},{2,18},{10... | collective-permute-start | bytes 3932168 | tf_op jit(solution)/shard_map/ppermute | solution.py:238
  8.9 109.6 %collective-permute-start.5 = (bf16[256,7680]{1,0:T(8,128)(2,1)}, bf16[256,7680]{1,0:T(8,128)(2,1)}, u32[]{:S(2)}, u32[]{:S(2)}) collective-permute-start(bf16[256,7680]{1,0:T(8,128)(2,1)} %slice.66), channel_id=1, source_target_pairs={{0,16},{8,24},{16,0},{24,8},{1,17},{9,25},{17,1},{25,9},{2,18},{10... | collective-permute-start | bytes 11796488 | tf_op jit(solution)/shard_map/ppermute | solution.py:238
  9.1 25.1 %collective-permute-start.2 = (f32[512,1]{1,0:T(8,128)S(1)}, f32[512,1]{1,0:T(8,128)S(1)}, u32[]{:S(2)}, u32[]{:S(2)}) collective-permute-start(f32[512,1]{1,0:T(8,128)S(1)} %copy.31.own_scaling_ref.refs_2_), channel_id=1, source_target_pairs={{0,8},{8,0},{16,24},{24,16},{1,9},{9,1},{17,25},{25,17},{2,10},{10... | collective-permute-start | bytes 6152 | tf_op jit(solution)/shard_map/ppermute | solution.py:234
  34.2 3.4 %copy-start = (bf16[256,16384]{1,0:T(8,128)(2,1)S(1)}, bf16[256,16384]{1,0:T(8,128)(2,1)}, u32[]{:S(2)}) copy-start(bf16[256,16384]{1,0:T(8,128)(2,1)} %gamma_ref) | copy-start | bytes 25165828
  60.1 1.0 copy-start.1
  62.3 32.3 %all-to-all-start = ((bf16[8,528,128]{2,1,0:T(8,128)(2,1)}), bf16[8,528,128]{2,1,0:T(8,128)(2,1)S(1)}, u32[]{:S(2)}, u32[]{:S(2)}) async-start(bf16[8,528,128]{2,1,0:T(8,128)(2,1)} %broadcast_in_dim.27), calls=%async_computation | async-start | bytes 2162688 | tf_op jit(solution)/shard_map/all_to_all | solution.py:272
  71.7 91.8 %collective-permute-start.8 = (bf16[256,4096]{1,0:T(8,128)(2,1)}, bf16[256,4096]{1,0:T(8,128)(2,1)}, u32[]{:S(2)}, u32[]{:S(2)}) collective-permute-start(bf16[256,4096]{1,0:T(8,128)(2,1)} %slice.70), channel_id=1, source_target_pairs={{0,16},{8,24},{16,0},{24,8},{1,17},{9,25},{17,1},{25,9},{2,18},{10... | collective-permute-start | bytes 6291464 | tf_op jit(solution)/shard_map/ppermute | solution.py:238
  95.7 38.2 %collective-permute-start.4 = (bf16[512,1024]{1,0:T(8,128)(2,1)}, bf16[512,1024]{1,0:T(8,128)(2,1)}, u32[]{:S(2)}, u32[]{:S(2)}) collective-permute-start(bf16[512,1024]{1,0:T(8,128)(2,1)} %copy_bitcast_fusion), channel_id=1, source_target_pairs={{0,8},{8,0},{16,24},{24,16},{1,9},{9,1},{17,25},{25,17},{2,10},{10... | collective-permute-start | bytes 3145736 | tf_op jit(solution)/shard_map/ppermute | solution.py:234
  97.9 82.5 %collective-permute-start = (bf16[256,1536]{1,0:T(8,128)(2,1)}, bf16[256,1536]{1,0:T(8,128)(2,1)}, u32[]{:S(2)}, u32[]{:S(2)}) collective-permute-start(bf16[256,1536]{1,0:T(8,128)(2,1)} %slice.60), channel_id=1, source_target_pairs={{0,16},{8,24},{16,0},{24,8},{1,17},{9,25},{17,1},{25,9},{2,18},{10... | collective-permute-start | bytes 2359304 | tf_op jit(solution)/shard_map/ppermute | solution.py:238
  133.9 1.6 copy-start.2
  136.6 1.6 collective-permute-start.6
  139.0 30.5 %all-to-all-start.1 = ((f32[8,64,128]{2,1,0:T(8,128)}), f32[8,64,128]{2,1,0:T(8,128)}, u32[]{:S(2)}, u32[]{:S(2)}) async-start(f32[8,64,128]{2,1,0:T(8,128)} %bitcast.5), calls=%async_computation.1 | async-start | bytes 524288 | tf_op jit(solution)/shard_map/all_to_all | solution.py:285
  146.9 38.7 %collective-permute-start.7 = (bf16[256,512]{1,0:T(8,128)(2,1)}, bf16[256,512]{1,0:T(8,128)(2,1)S(1)}, u32[]{:S(2)}, u32[]{:S(2)}) collective-permute-start(bf16[256,512]{1,0:T(8,128)(2,1)} %slice.69), channel_id=1, source_target_pairs={{0,16},{8,24},{16,0},{24,8},{1,17},{9,25},{17,1},{25,9},{2,18},{10... | collective-permute-start | bytes 786440 | tf_op jit(solution)/shard_map/ppermute | solution.py:238
  186.1 1.4 collective-permute-start.9
  187.6 4.4 %collective-permute-start.10 = (bf16[2,64,128]{2,1,0:T(8,128)(2,1)S(1)}, bf16[2,64,128]{2,1,0:T(8,128)(2,1)S(1)}, u32[]{:S(2)}, u32[]{:S(2)}) collective-permute-start(bf16[2,64,128]{2,1,0:T(8,128)(2,1)S(1)} %get-tuple-element.35), channel_id=1, source_target_pairs={{0,11},{1,10},{2,9},{3,8},{4,15},{5,14},{6,13},{7,12},{8,3},{9,2},... | collective-permute-start | bytes 98312 | tf_op jit(solution)/shard_map/ppermute | solution.py:307
  190.2 3.4 %collective-permute-start.12 = (bf16[2,64,128]{2,1,0:T(8,128)(2,1)S(1)}, bf16[2,64,128]{2,1,0:T(8,128)(2,1)S(1)}, u32[]{:S(2)}, u32[]{:S(2)}) collective-permute-start(bf16[2,64,128]{2,1,0:T(8,128)(2,1)S(1)} %get-tuple-element.36), channel_id=1, source_target_pairs={{0,9},{1,8},{2,11},{3,10},{4,13},{5,12},{6,15},{7,14},{8,1},{9,0},... | collective-permute-start | bytes 98312 | tf_op jit(solution)/shard_map/ppermute | solution.py:307
  190.7 3.3 %collective-permute-start.11 = (bf16[2,64,128]{2,1,0:T(8,128)(2,1)S(1)}, bf16[2,64,128]{2,1,0:T(8,128)(2,1)S(1)}, u32[]{:S(2)}, u32[]{:S(2)}) collective-permute-start(bf16[2,64,128]{2,1,0:T(8,128)(2,1)S(1)} %get-tuple-element.37), channel_id=1, source_target_pairs={{0,10},{1,11},{2,8},{3,9},{4,14},{5,15},{6,12},{7,13},{8,2},{9,3},... | collective-permute-start | bytes 98312 | tf_op jit(solution)/shard_map/ppermute | solution.py:307
  194.1 4.1 %collective-permute-start.13 = (bf16[1,64,128]{2,1,0:T(8,128)(2,1)S(1)}, bf16[1,64,128]{2,1,0:T(8,128)(2,1)S(1)}, u32[]{:S(2)}, u32[]{:S(2)}) collective-permute-start(bf16[1,64,128]{2,1,0:T(8,128)(2,1)S(1)} %fusion.7), channel_id=1, source_target_pairs={{0,12},{1,13},{2,14},{3,15},{4,8},{5,9},{6,10},{7,11},{8,4},{9,5},... | collective-permute-start | bytes 49160 | tf_op jit(solution)/shard_map/ppermute | solution.py:307
